TPU v7x, 32 devices: a whole 2x2x4 slice. The times are simulated.
32 devices in a mesh: member: 2 (over y), lon: 4 (over z), lat: 2 (over x), lev: 2 (over core).
Axes of the slice: x: 2, y: 2, z: 4, core: 2. Of those that a mesh axis runs over, the one named last changes fastest.
Arguments:
- tracers: float32 [20, 8, 720, 1440], P('member', 'lev', 'lat', 'lon'), parts along dimension 0, may hold values from -6 to 6
- thickness: float32 [16, 720, 1440], P(('member', 'lev'), 'lat', 'lon'), parts along dimension 0, may hold values from 0.5 to 1.5
- zonal: float32 [16, 720, 1440], P(('member', 'lev'), 'lat', 'lon'), parts along dimension 0, may hold values from -6 to 6
- meridional: float32 [16, 720, 1440], P(('member', 'lev'), 'lat', 'lon'), parts along dimension 0, may hold values from -6 to 6
- cutoff: int32 [2, 60], replicated, may hold values from 1 to 191, as said below
Outputs:
- tracers_out: float32 [20, 8, 720, 1440], P('member', 'lev', 'lat', 'lon'), parts along dimension 0
- thickness_out: float32 [16, 720, 1440], P(('member', 'lev'), 'lat', 'lon'), parts along dimension 0
- zonal_out: float32 [16, 720, 1440], P(('member', 'lev'), 'lat', 'lon'), parts along dimension 0
- meridional_out: float32 [16, 720, 1440], P(('member', 'lev'), 'lat', 'lon'), parts along dimension 0
There are 2 independent parts, one for each index of `member`. A program takes and returns all parts, laid end to end along the dimension named above; an argument that names none is the same for every part. Nothing has to cross between parts.
Inputs may be any that keep to these rules, and one draw needn't show every extreme that they name: `cutoff`: one entry equals 191 in every draw.
All inputs are finite; a program needn't handle non-finite values.
Results may differ from a plain program's by a relative error of at most 0.00011.
Values sent between devices are 32-bit elements; how exact they have to be, the bound alone decides.
No kernel may reach another device: no remote copies, remote signals or barrier semaphores. Data moves between devices by JAX's collectives and lax.ppermute only.
A program may use at most 320 MiB of HBM per device.

v0:
```python
import math

import jax
import jax.numpy as jnp
from jax import lax
from jax.sharding import PartitionSpec as P

NSUB = 2
POLAR = 60
KMAX = 191


COURANT_CAP = 0.15
GRADIENT_COEF = 0.1


def extended_2(block, sides, width):
    for axis, dim in sides:
        count = lax.axis_size(axis)
        forward = [(i, i + 1) for i in range(count - 1)]
        forward.append((count - 1, 0))
        backward = [(target, source) for source, target in forward]
        low = lax.ppermute(
            lax.slice_in_dim(block, block.shape[dim] - width, None, axis=dim), axis, forward
        )
        high = lax.ppermute(lax.slice_in_dim(block, 0, width, axis=dim), axis, backward)
        block = jnp.concatenate([low, block, high], axis=dim)
    return block


def shifted(block, axis, distance):
    devices = range(lax.axis_size(axis))
    route = [((i - distance) % len(devices), i) for i in devices]
    return lax.ppermute(block, axis, route)


def entering(value, axis, join, neutral):
    count, mine = (lax.axis_size(axis), lax.axis_index(axis))
    pieces = lax.all_gather(value, axis)
    running = jnp.full_like(value, 0) + jnp.asarray(neutral, value.dtype)

    def step(position, running):
        longer = join(running, pieces[position])
        return jnp.where(position < mine, longer, running)

    return lax.fori_loop(0, count - 1, step, running)


def advance_level(extended, pressure):
    tracer_count = extended.shape[0] - 3
    thick = extended[tracer_count]
    east_wind = extended[tracer_count + 1]
    north_wind = extended[tracer_count + 2]
    masses = jnp.concatenate([thick[None], extended[:tracer_count] * thick[None]], 0)
    east_courant = COURANT_CAP * jnp.tanh(0.5 * (east_wind[1:-1, :-1] + east_wind[1:-1, 1:]))
    east_flux = (
        jnp.maximum(east_courant, 0.0) * masses[:, 1:-1, :-1]
        + jnp.minimum(east_courant, 0.0) * masses[:, 1:-1, 1:]
    )
    south_courant = COURANT_CAP * jnp.tanh(0.5 * (north_wind[:-1, 1:-1] + north_wind[1:, 1:-1]))
    south_flux = (
        jnp.maximum(south_courant, 0.0) * masses[:, :-1, 1:-1]
        + jnp.minimum(south_courant, 0.0) * masses[:, 1:, 1:-1]
    )
    updated = (
        masses[:, 1:-1, 1:-1]
        - (east_flux[:, :, 1:] - east_flux[:, :, :-1])
        - (south_flux[:, 1:] - south_flux[:, :-1])
    )
    new_thick = updated[0]
    new_mixing = updated[1:] / new_thick[None]
    new_east = east_wind[1:-1, 1:-1] - GRADIENT_COEF * (pressure[1:-1, 2:] - pressure[1:-1, :-2])
    new_north = north_wind[1:-1, 1:-1] - GRADIENT_COEF * (pressure[2:, 1:-1] - pressure[:-2, 1:-1])
    return (new_mixing, new_thick, new_east, new_north)


def wave_basis(anchor, length, lon_total):
    cells = anchor + jnp.arange(length, dtype=jnp.int32)
    waves = jnp.arange(KMAX + 1, dtype=jnp.int32)
    phase = (cells[:, None] * waves[None, :] % lon_total).astype(jnp.float32) * (
        2.0 * math.pi / lon_total
    )
    return jnp.concatenate([jnp.cos(phase), jnp.sin(phase)], 1)


def wave_weights(limits, lon_total):
    waves = jnp.arange(KMAX + 1, dtype=jnp.int32)
    scaled = jnp.where(waves == 0, 1.0, 2.0).astype(jnp.float32) / lon_total
    kept = jnp.where(waves[None, :] <= limits[:, None], scaled[None, :], 0.0)
    return jnp.concatenate([kept, kept], 1)


def smooth_winds(zonal, meridional, cutoff, is_north, is_south):
    level_count, row_count, col_count = zonal.shape
    lon_count = lax.axis_size("lon")
    lon_total = col_count * lon_count
    north_rows = jnp.stack([zonal[:, :POLAR], meridional[:, :POLAR]], 0)
    south_rows = jnp.stack([zonal[:, row_count - POLAR :], meridional[:, row_count - POLAR :]], 0)
    selected = jnp.where(is_north, north_rows, south_rows).reshape(-1, col_count)
    limits = jnp.tile(jnp.where(is_north, cutoff[0], cutoff[1]), 2 * level_count)
    fragment = lax.all_gather(selected, "lon", axis=1, tiled=True)
    basis = wave_basis(jnp.int32(0), fragment.shape[1], lon_total)
    spectrum = jnp.dot(
        fragment, basis, precision=lax.Precision.HIGHEST, preferred_element_type=jnp.float32
    )
    own_basis = wave_basis(lax.axis_index("lon") * col_count, col_count, lon_total)
    filtered = jnp.dot(
        spectrum * wave_weights(limits, lon_total),
        own_basis.T,
        precision=lax.Precision.HIGHEST,
        preferred_element_type=jnp.float32,
    )
    filtered = filtered.reshape(2, level_count, POLAR, col_count)
    row_start = jnp.where(is_north, 0, row_count - POLAR).astype(jnp.int32)
    polar_band = jnp.logical_or(is_north, is_south)
    new_zonal = lax.dynamic_update_slice_in_dim(zonal, filtered[0], row_start, 1)
    new_merid = lax.dynamic_update_slice_in_dim(meridional, filtered[1], row_start, 1)
    return (jnp.where(polar_band, new_zonal, zonal), jnp.where(polar_band, new_merid, meridional))


def shards(tracers, thickness, zonal, meridional, cutoff):
    tracer_count = tracers.shape[0]
    lat_index = lax.axis_index("lat")
    is_north = lat_index == 0
    is_south = lat_index == lax.axis_size("lat") - 1
    lon_count = lax.axis_size("lon")
    flip_sign = jnp.concatenate(
        [jnp.ones((tracer_count + 1,), jnp.float32), -jnp.ones((2,), jnp.float32)]
    )[:, None, None]
    advance_all = jax.vmap(advance_level, in_axes=(1, 0), out_axes=(1, 0, 0, 0))
    for substep in range(NSUB):
        zonal, meridional = smooth_winds(zonal, meridional, cutoff, is_north, is_south)
        state = jnp.concatenate([tracers, thickness[None], zonal[None], meridional[None]], 0)
        extended = extended_2(state, (("lat", 2), ("lon", 3)), 1)
        edges = jnp.stack([state[:, :, 0], state[:, :, -1]], 2)
        opposite = shifted(edges, "lon", lon_count // 2)
        north_rim = jnp.where(is_north, opposite[:, :, 0] * flip_sign, extended[:, :, 0, 1:-1])
        south_rim = jnp.where(is_south, opposite[:, :, 1] * flip_sign, extended[:, :, -1, 1:-1])
        extended = extended.at[:, :, 0, 1:-1].set(north_rim)
        extended = extended.at[:, :, -1, 1:-1].set(south_rim)
        thick_ext = extended[tracer_count]
        column_above = entering(
            jnp.sum(thick_ext, 0),
            "lev",
            lambda earlier, later: earlier + later,
            jnp.zeros(thick_ext.shape[1:], jnp.float32),
        )
        pressure = jnp.cumsum(thick_ext, axis=0) - 0.5 * thick_ext + column_above[None]
        tracers, thickness, zonal, meridional = advance_all(extended, pressure)
    return (tracers, thickness, zonal, meridional)


def solution(mesh):
    placed = (
        P("member", "lev", "lat", "lon"),
        P(("member", "lev"), "lat", "lon"),
        P(("member", "lev"), "lat", "lon"),
        P(("member", "lev"), "lat", "lon"),
        P(),
    )
    return jax.shard_map(
        shards,
        mesh=mesh,
        in_specs=placed,
        out_specs=(
            P("member", "lev", "lat", "lon"),
            P(("member", "lev"), "lat", "lon"),
            P(("member", "lev"), "lat", "lon"),
            P(("member", "lev"), "lat", "lon"),
        ),
        check_vma=False,
    )
```

profile of v0, /device:TPU:0, one launch (start us, length us, event | category | flops | bytes accessed | tf_op | source)
XLA Modules:
  0.0 677.9 jit_solution(5528478332591272286)
XLA Ops:
  7.2 3.3 copy.29
  10.7 1.3 slice_bitcast_fusion.15
  13.0 2.2 copy.9
  16.2 1.6 fusion.67
  17.9 8.4 %fusion.52 = (f32[1440,192]{1,0:T(8,128)}, f32[1440,192]{1,0:T(8,128)}) fusion(), kind=kLoop, calls=%fused_computation.112 | loop fusion | flops 2488320 | bytes 2211840 | tf_op jit(solution)/shard_map/sin | solution.py:83
  26.3 52.1 %all-gather.7.cloned.1.call-done = f32[480,1440]{0,1:T(8,128)} async-done(((f32[480,360]{0,1:T(8,128)}), f32[480,1440]{0,1:T(8,128)}) %all-gather.7.cloned.1.call-update) | async-done | bytes 2764816 | tf_op jit(solution)/shard_map/all_gather | solution.py:101
  78.4 8.5 %fusion.57 = f32[480,384]{1,0:T(8,128)S(1)} fusion(f32[480,1440]{0,1:T(8,128)} %all-gather.7.cloned.1.call-done, f32[1440,192]{1,0:T(8,128)} %get-tuple-element.136, f32[1440,192]{1,0:T(8,128)} %get-tuple-element.137, f32[480,192]{1,0:T(8,128)S(1)} %fusion.61), kind=kOutput, calls=%fused_computation.117 | convolution fusion | flops 3185971200 | bytes 6082560 | tf_op jit(solution)/shard_map/dot_general | solution.py:103
  86.9 1.6 fusion.70
  89.8 3.4 select_n.170
  93.2 4.4 select_n.173
  97.6 1.6 pad_maximum_fusion.36
  99.2 2.0 collective-permute-start.1
  102.6 1.6 collective-permute-done
  105.1 16.3 %pad_maximum_fusion.15 = (f32[13,4,362,1]{3,2,1,0:T(8,128)}, f32[13,4,362,1]{3,2,1,0:T(8,128)}) fusion(f32[13,4,1,360]{3,2,1,0:T(1,128)S(1)} %collective-permute-done.1, f32[13,4,1,360]{3,2,1,0:T(1,128)S(1)} %collective-permute-done, f32[1,4,360,360]{3,2,1,0:T(8,128)S(1)} %select_n.173, f32[1,4,360,360]{3,2,1,0:T(8,128)S(1)} %copy-done.1, ...), kind=kLoop, calls=%fused_computation.61 | loop fusion | flops 188240 | bytes 27257152 | tf_op jit(solution)/shard_map/slice | solution.py:24
  121.3 6.5 copy.10
  127.8 6.7 copy.11
  136.8 5.0 collective-permute-done.2
  141.7 5.2 copy.12
  147.0 5.3 copy.13
  152.3 39.2 %pad_maximum_fusion = f32[13,4,362,362]{3,2,1,0:T(8,128)} fusion(f32[13,4,362,1]{3,2,1,0:T(8,128)} %copy.13, f32[13,4,1,360]{3,2,1,0:T(1,128)S(1)} %collective-permute-done.1, f32[1,4,360,360]{3,2,1,0:T(8,128)S(1)} %select_n.173, f32[1,4,360,360]{3,2,1,0:T(8,128)} %select_n.170, f32[1,4,360,360]{3,2,1,0:T(8,128)} %bitcast.86, f32[10,4,360,360]{3,2,1,0:T(8,128)} %param.13, ...), kind=kLoop, calls=%fused_computation.8 | loop fusion | flops 47700016 | bytes 54514304 | tf_op jit(solution)/shard_map/concatenate | solution.py:27
  191.5 12.4 %scatter.14 = f32[13,4,362,362]{3,2,1,0:T(8,128)} dynamic-update-slice(f32[13,4,362,362]{3,2,1,0:T(8,128)} %pad_maximum_fusion, f32[13,4,1,360]{3,2,1,0:T(1,128)S(1)} %get-tuple-element.129, s32[]{:T(128)} %constant.178.clone.1, s32[]{:T(128)} %constant.178.clone.1, s32[]{:T(128)} %bitcast.10, s32[]{:T(128)} %bitcast.11) | dynamic-update-slice | bytes 149764 | tf_op jit(solution)/shard_map/scatter | solution.py:139
  203.9 11.2 %scatter.15 = f32[13,4,362,362]{3,2,1,0:T(8,128)} dynamic-update-slice(f32[13,4,362,362]{3,2,1,0:T(8,128)} %scatter.14, f32[13,4,1,360]{3,2,1,0:T(1,128)S(1)} %get-tuple-element.128, s32[]{:T(128)} %constant.178.clone.1, s32[]{:T(128)} %constant.178.clone.1, s32[]{:T(128)} %constant.191.clone.1, s32[]{:T(128)} %constant.179.clone.1) | dynamic-update-slice | bytes 149764 | tf_op jit(solution)/shard_map/scatter | solution.py:140
  215.1 5.1 slice_bitcast_fusion.9
  220.2 2.6 all-gather.2
  222.8 2.6 subtract_add_fusion.1
  225.4 16.5 %fusion.25 = f32[4,10,362,362]{3,2,0,1:T(8,128)} fusion(f32[13,4,362,362]{3,2,1,0:T(8,128)} %scatter.15, f32[4,362,362]{2,1,0:T(8,128)S(1)} %get-tuple-element.87), kind=kLoop, calls=%fused_computation.45 | loop fusion | flops 5241760 | bytes 44030784 | tf_op jit(solution)/shard_map/vmap()/mul | solution.py:54
  241.9 3.0 broadcast_maximum_fusion.3
  244.9 3.5 broadcast_maximum_fusion.1
  248.4 3.3 fusion.44
  251.7 1.3 copy-done.2
  254.3 2.3 copy.14
  256.7 29.4 %fusion.21 = f32[4,11,360,361]{3,2,0,1:T(8,128)} fusion(f32[4,1,362,362]{3,2,0,1:T(8,128)} %get-tuple-element.91, f32[4,10,362,362]{3,2,0,1:T(8,128)} %fusion.25, f32[4,360,361]{2,1,0:T(8,128)} %get-tuple-element.109, f32[4,360,361]{2,1,0:T(8,128)} %get-tuple-element.108), kind=kLoop, calls=%fused_computation.33 | loop fusion | flops 28591200 | bytes 50095424 | tf_op jit(solution)/shard_map/vmap()/add | solution.py:57
  286.0 28.5 %fusion.5 = f32[4,11,361,360]{3,2,0,1:T(8,128)} fusion(f32[4,1,362,362]{3,2,0,1:T(8,128)S(1)} %copy-done.4, f32[4,10,362,362]{3,2,0,1:T(8,128)} %fusion.25, f32[4,361,360]{2,1,0:T(8,128)S(1)} %copy-done.8, f32[4,361,360]{2,1,0:T(8,128)S(1)} %copy-done.7), kind=kLoop, calls=%fused_computation.15 | loop fusion | flops 28591200 | bytes 50095424 | tf_op jit(solution)/shard_map/vmap()/add | solution.py:62
  314.5 48.1 %fusion.18 = f32[4,11,360,360]{3,2,0,1:T(8,128)} fusion(f32[4,1,362,362]{3,2,0,1:T(8,128)S(1)} %copy-done.4, f32[4,11,361,360]{3,2,0,1:T(8,128)} %fusion.5, f32[4,11,360,361]{3,2,0,1:T(8,128)} %fusion.21, f32[4,10,362,362]{3,2,0,1:T(8,128)} %fusion.25), kind=kLoop, calls=%fused_computation.30 | loop fusion | flops 28512000 | bytes 137111744 | tf_op jit(solution)/shard_map/vmap()/sub | solution.py:66
  362.6 3.3 slice_bitcast_fusion.6
  365.9 16.6 %fusion.27 = f32[10,4,360,360]{3,2,1,0:T(8,128)} fusion(f32[4,11,360,360]{3,2,0,1:T(8,128)} %fusion.18, f32[4,360,360]{2,1,0:T(8,128)S(1)} %get-tuple-element.100), kind=kLoop, calls=%fused_computation.49 | loop fusion | flops 5184000 | bytes 43545600 | tf_op jit(solution)/shard_map/vmap()/transpose | solution.py:149
  382.4 8.6 %fusion.58 = f32[480,384]{1,0:T(8,128)S(1)} fusion(f32[480,1440]{0,1:T(8,128)} %all-gather.9.cloned.1.call-done, f32[1440,192]{1,0:T(8,128)} %get-tuple-element.136, f32[1440,192]{1,0:T(8,128)} %get-tuple-element.137, f32[480,192]{1,0:T(8,128)S(1)} %copy-done.11), kind=kOutput, calls=%fused_computation.118 | convolution fusion | flops 3185971200 | bytes 6082560 | tf_op jit(solution)/shard_map/dot_general | solution.py:103
  391.0 1.6 fusion.69
  395.6 3.4 select_n.184
  399.0 4.4 select_n.187
  403.4 1.6 pad_maximum_fusion.32
  405.0 2.0 collective-permute-start.6
  407.3 3.0 collective-permute-done.5
  412.3 11.6 %pad_maximum_fusion.9 = (f32[13,4,362,1]{3,2,1,0:T(8,128)}, f32[13,4,362,1]{3,2,1,0:T(8,128)}) fusion(f32[13,4,1,360]{3,2,1,0:T(1,128)S(1)} %collective-permute-done.6, f32[13,4,1,360]{3,2,1,0:T(1,128)S(1)} %collective-permute-done.5, f32[1,4,360,360]{3,2,1,0:T(8,128)S(1)} %select_n.187, f32[1,4,360,360]{3,2,1,0:T(8,128)S(1)} %copy-done.3, ...), kind=kLoop, calls=%fused_computation.55 | loop fusion | flops 188240 | bytes 27257152 | tf_op jit(solution)/shard_map/slice | solution.py:24
  423.9 6.5 copy.15
  430.4 6.5 copy.16
  437.3 1.7 collective-permute-start.7
  439.2 4.3 collective-permute-done.7
  443.5 5.2 copy.17
  448.7 5.3 copy.18
  454.0 39.2 %pad_maximum_fusion.1 = f32[13,4,362,362]{3,2,1,0:T(8,128)} fusion(f32[13,4,362,1]{3,2,1,0:T(8,128)} %copy.18, f32[13,4,1,360]{3,2,1,0:T(1,128)S(1)} %collective-permute-done.6, f32[1,4,360,360]{3,2,1,0:T(8,128)S(1)} %select_n.187, f32[1,4,360,360]{3,2,1,0:T(8,128)} %select_n.184, f32[1,4,360,360]{3,2,1,0:T(8,128)} %get-tuple-element.101, ...), kind=kLoop, calls=%fused_computation.9 | loop fusion | flops 47700016 | bytes 54514304 | tf_op jit(solution)/shard_map/concatenate | solution.py:27
  493.2 12.4 %scatter.16 = f32[13,4,362,362]{3,2,1,0:T(8,128)} dynamic-update-slice(f32[13,4,362,362]{3,2,1,0:T(8,128)} %pad_maximum_fusion.1, f32[13,4,1,360]{3,2,1,0:T(1,128)S(1)} %get-tuple-element.127, s32[]{:T(128)} %constant.178.clone.1, s32[]{:T(128)} %constant.178.clone.1, s32[]{:T(128)} %bitcast.10, s32[]{:T(128)} %bitcast.11) | dynamic-update-slice | bytes 149764 | tf_op jit(solution)/shard_map/scatter | solution.py:139
  505.6 11.2 %scatter.19 = f32[13,4,362,362]{3,2,1,0:T(8,128)} dynamic-update-slice(f32[13,4,362,362]{3,2,1,0:T(8,128)} %scatter.16, f32[13,4,1,360]{3,2,1,0:T(1,128)S(1)} %get-tuple-element.126, s32[]{:T(128)} %constant.178.clone.1, s32[]{:T(128)} %constant.178.clone.1, s32[]{:T(128)} %constant.191.clone.1, s32[]{:T(128)} %constant.179.clone.1) | dynamic-update-slice | bytes 149764 | tf_op jit(solution)/shard_map/scatter | solution.py:140
  516.8 3.7 slice_reduce_fusion
  520.5 2.8 all-gather.3
  523.3 2.6 subtract_add_fusion
  526.0 16.2 %fusion.24 = f32[4,10,362,362]{3,2,0,1:T(8,128)} fusion(f32[13,4,362,362]{3,2,1,0:T(8,128)} %scatter.19, f32[4,362,362]{2,1,0:T(8,128)S(1)} %get-tuple-element.83), kind=kLoop, calls=%fused_computation.43 | loop fusion | flops 5241760 | bytes 44030784 | tf_op jit(solution)/shard_map/vmap()/mul | solution.py:54
  543.2 1.3 broadcast_maximum_fusion
  544.5 5.3 fusion.35
  549.8 25.6 %fusion.13 = f32[4,11,360,361]{3,2,0,1:T(8,128)} fusion(f32[4,1,362,362]{3,2,0,1:T(8,128)S(1)} %get-tuple-element.86, f32[4,10,362,362]{3,2,0,1:T(8,128)} %fusion.24, f32[4,360,361]{2,1,0:T(8,128)S(1)} %get-tuple-element.105, f32[4,360,361]{2,1,0:T(8,128)S(1)} %get-tuple-element.104), kind=kLoop, calls=%fused_computation.25 | loop fusion | flops 28591200 | bytes 50095424 | tf_op jit(solution)/shard_map/vmap()/add | solution.py:57
  575.4 28.4 %fusion.2 = f32[4,11,361,360]{3,2,0,1:T(8,128)} fusion(f32[4,1,362,362]{3,2,0,1:T(8,128)S(1)} %get-tuple-element.86, f32[4,10,362,362]{3,2,0,1:T(8,128)} %fusion.24, f32[4,361,360]{2,1,0:T(8,128)S(1)} %get-tuple-element.107, f32[4,361,360]{2,1,0:T(8,128)S(1)} %get-tuple-element.106), kind=kLoop, calls=%fused_computation.12 | loop fusion | flops 28591200 | bytes 50095424 | tf_op jit(solution)/shard_map/vmap()/add | solution.py:62
  603.8 47.9 %fusion.10 = f32[4,11,360,360]{3,2,0,1:T(8,128)} fusion(f32[4,1,362,362]{3,2,0,1:T(8,128)S(1)} %get-tuple-element.86, f32[4,11,361,360]{3,2,0,1:T(8,128)} %fusion.2, f32[4,11,360,361]{3,2,0,1:T(8,128)} %fusion.13, f32[4,10,362,362]{3,2,0,1:T(8,128)} %fusion.24), kind=kLoop, calls=%fused_computation.22 | loop fusion | flops 28512000 | bytes 137111744 | tf_op jit(solution)/shard_map/vmap()/sub | solution.py:66
  651.7 1.8 slice_bitcast_fusion.4
  653.5 17.3 %fusion.26 = f32[10,4,360,360]{3,2,1,0:T(8,128)} fusion(f32[4,11,360,360]{3,2,0,1:T(8,128)} %fusion.10, f32[4,360,360]{2,1,0:T(8,128)S(1)} %slice_bitcast_fusion.4), kind=kLoop, calls=%fused_computation.47 | loop fusion | flops 5184000 | bytes 43545600 | tf_op jit(solution)/shard_map/vmap()/transpose | solution.py:149
  (89 shorter events, 16.2 us)
Async XLA Ops:
  7.2 71.2 %all-gather.7.cloned.1.call-start = ((), (), s32[]{:S(2)}) async-start(), calls=%async_computation | async-start | bytes 3686400 | tf_op jit(solution)/shard_map/all_gather | solution.py:101
  7.2 3.3 copy-start.16
  11.9 3.4 copy-start.19
  15.2 367.2 %all-gather.9.cloned.1.call-start = ((), (), s32[]{:S(2)}) async-start(), calls=%async_computation.1 | async-start | bytes 3686400 | tf_op jit(solution)/shard_map/all_gather | solution.py:101
  16.2 70.7 %copy-start.10 = (f32[480,192]{1,0:T(8,128)}, f32[480,192]{1,0:T(8,128)S(1)}, u32[]{:S(2)}) copy-start(f32[480,192]{1,0:T(8,128)S(1)} %fusion.61) | copy-start | bytes 1105924
  17.8 69.1 %copy-start.12 = (f32[360,192]{1,0:T(8,128)}, f32[360,192]{1,0:T(8,128)S(1)}, u32[]{:S(2)}) copy-start(f32[360,192]{1,0:T(8,128)S(1)} %get-tuple-element.130) | copy-start | bytes 829444
  17.9 69.1 %copy-start.14 = (f32[360,192]{1,0:T(8,128)}, f32[360,192]{1,0:T(8,128)S(1)}, u32[]{:S(2)}) copy-start(f32[360,192]{1,0:T(8,128)S(1)} %get-tuple-element.131) | copy-start | bytes 829444
  97.6 7.5 %copy-start.1 = (f32[1,4,360,360]{3,2,1,0:T(8,128)S(1)}, f32[1,4,360,360]{3,2,1,0:T(8,128)}, u32[]{:S(2)}) copy-start(f32[1,4,360,360]{3,2,1,0:T(8,128)} %select_n.170) | copy-start | bytes 6220804
  97.6 7.5 %copy-start.6 = (f32[4,360,360]{2,1,0:T(8,128)S(1)}, f32[4,360,360]{2,1,0:T(8,128)}, u32[]{:S(2)}) copy-start(f32[4,360,360]{2,1,0:T(8,128)} %param.14) | copy-start | bytes 6220804
  99.2 5.0 collective-permute-start
  99.2 5.8 collective-permute-start.1
  101.4 35.1 %collective-permute-start.4 = (f32[13,4,2,360]{3,2,1,0:T(2,128)S(1)}, f32[13,4,2,360]{3,2,1,0:T(2,128)S(1)}, u32[]{:S(2)}, u32[]{:S(2)}) collective-permute-start(f32[13,4,2,360]{3,2,1,0:T(2,128)S(1)} %pad_maximum_fusion.27), channel_id=1, source_target_pairs={{8,0},{12,4},{0,8},{4,12},{9,1},{13,5},{1,9},{5,13},{10,2},{14,6},... | collective-permute-start | bytes 449288 | tf_op jit(solution)/shard_map/ppermute | solution.py:34
  127.8 8.8 %copy-start.17 = (f32[13]{0:T(128)S(1)}, f32[13]{0:T(128)}, u32[]{:S(2)}) copy-start(f32[13]{0:T(128)} %constant.190.clone.1) | copy-start | bytes 160
  134.5 12.5 %collective-permute-start.3 = (f32[13,4,362,1]{2,1,3,0:T(4,128)S(1)}, f32[13,4,362,1]{2,1,3,0:T(4,128)S(1)}, u32[]{:S(2)}, u32[]{:S(2)}) collective-permute-start(f32[13,4,362,1]{2,1,3,0:T(4,128)S(1)} %copy.11), channel_id=1, source_target_pairs={{4,0},{8,4},{12,8},{0,12},{5,1},{9,5},{13,9},{1,13},{6,2},{10,6},{... | collective-permute-start | bytes 225896 | tf_op jit(solution)/shard_map/ppermute | solution.py:26
  135.5 6.2 collective-permute-start.2
  251.7 1.4 copy-start.2
  256.6 29.4 %copy-start.4 = (f32[4,1,362,362]{3,2,0,1:T(8,128)S(1)}, f32[4,1,362,362]{3,2,0,1:T(8,128)}, u32[]{:S(2)}) copy-start(f32[4,1,362,362]{3,2,0,1:T(8,128)} %get-tuple-element.91) | copy-start | bytes 6290116
  256.6 29.4 %copy-start.7 = (f32[4,361,360]{2,1,0:T(8,128)S(1)}, f32[4,361,360]{2,1,0:T(8,128)}, u32[]{:S(2)}) copy-start(f32[4,361,360]{2,1,0:T(8,128)} %get-tuple-element.110) | copy-start | bytes 6238084
  256.6 29.4 %copy-start.8 = (f32[4,361,360]{2,1,0:T(8,128)S(1)}, f32[4,361,360]{2,1,0:T(8,128)}, u32[]{:S(2)}) copy-start(f32[4,361,360]{2,1,0:T(8,128)} %get-tuple-element.111) | copy-start | bytes 6238084
  365.9 16.6 %copy-start.11 = (f32[480,192]{1,0:T(8,128)S(1)}, f32[480,192]{1,0:T(8,128)}, u32[]{:S(2)}) copy-start(f32[480,192]{1,0:T(8,128)} %copy-done.10) | copy-start | bytes 1105924
  382.4 8.6 %copy-start.13 = (f32[360,192]{1,0:T(8,128)S(1)}, f32[360,192]{1,0:T(8,128)}, u32[]{:S(2)}) copy-start(f32[360,192]{1,0:T(8,128)} %copy-done.12) | copy-start | bytes 829444
  382.4 8.6 %copy-start.15 = (f32[360,192]{1,0:T(8,128)S(1)}, f32[360,192]{1,0:T(8,128)}, u32[]{:S(2)}) copy-start(f32[360,192]{1,0:T(8,128)} %copy-done.14) | copy-start | bytes 829444
  403.4 7.8 %copy-start = (f32[10,4,360,360]{3,2,1,0:T(8,128)S(1)}, f32[10,4,360,360]{3,2,1,0:T(8,128)}, u32[]{:S(2)}) copy-start(f32[10,4,360,360]{3,2,1,0:T(8,128)} %fusion.27) | copy-start | bytes 62208004
  403.4 8.3 %copy-start.3 = (f32[1,4,360,360]{3,2,1,0:T(8,128)S(1)}, f32[1,4,360,360]{3,2,1,0:T(8,128)}, u32[]{:S(2)}) copy-start(f32[1,4,360,360]{3,2,1,0:T(8,128)} %select_n.184) | copy-start | bytes 6220804
  403.4 8.9 %copy-start.5 = (f32[1,4,360,360]{3,2,1,0:T(8,128)S(1)}, f32[1,4,360,360]{3,2,1,0:T(8,128)}, u32[]{:S(2)}) copy-start(f32[1,4,360,360]{3,2,1,0:T(8,128)} %get-tuple-element.101) | copy-start | bytes 6220804
  405.0 5.3 collective-permute-start.5
  405.0 6.2 collective-permute-start.6
  407.2 31.8 %collective-permute-start.9 = (f32[13,4,2,360]{3,2,1,0:T(2,128)S(1)}, f32[13,4,2,360]{3,2,1,0:T(2,128)S(1)}, u32[]{:S(2)}, u32[]{:S(2)}) collective-permute-start(f32[13,4,2,360]{3,2,1,0:T(2,128)S(1)} %pad_maximum_fusion.28), channel_id=1, source_target_pairs={{8,0},{12,4},{0,8},{4,12},{9,1},{13,5},{1,9},{5,13},{10,2},{14,6},... | collective-permute-start | bytes 449288 | tf_op jit(solution)/shard_map/ppermute | solution.py:34
  430.4 8.6 %copy-start.18 = (f32[13]{0:T(128)S(1)}, f32[13]{0:T(128)}, u32[]{:S(2)}) copy-start(f32[13]{0:T(128)} %constant.190.clone.1) | copy-start | bytes 160
  436.9 11.8 %collective-permute-start.8 = (f32[13,4,362,1]{2,1,3,0:T(4,128)S(1)}, f32[13,4,362,1]{2,1,3,0:T(4,128)S(1)}, u32[]{:S(2)}, u32[]{:S(2)}) collective-permute-start(f32[13,4,362,1]{2,1,3,0:T(4,128)S(1)} %copy.16), channel_id=1, source_target_pairs={{4,0},{8,4},{12,8},{0,12},{5,1},{9,5},{13,9},{1,13},{6,2},{10,6},{... | collective-permute-start | bytes 225896 | tf_op jit(solution)/shard_map/ppermute | solution.py:26
  437.3 6.2 collective-permute-start.7
  653.5 17.3 %copy-start.9 = (f32[4,360,360]{2,1,0:T(8,128)}, f32[4,360,360]{2,1,0:T(8,128)S(1)}, u32[]{:S(2)}) copy-start(f32[4,360,360]{2,1,0:T(8,128)S(1)} %slice_bitcast_fusion.4) | copy-start | bytes 6220804
Sparse Core Ops, SparseCore 0:
  15.4 62.9 all-gather.6
  256.7 57.6 all-gather.8
where the time goes:
time: 682 us; the launch traced here: 678 us
  other arithmetic  429 us (63%)
  local copies, waits for them, and re-layouts  131 us (19%)
  waiting for transfers between devices  67.8 us (10%)
  matrix products  20.2 us (3%)
  between operations  14.8 us (2%)
  starting transfers between devices  9.63 us (1%)
    sub x2, other arithmetic, advance_level(): masses[:, 1:-1, 1:-1] - (east_flux[:, :, 1:] - east_flux[:, :, :-1])  96 us
    concatenate x2, other arithmetic, extended_2(): block = jnp.concatenate([low, block, high], axis=dim)  78.4 us
    add x2, other arithmetic, advance_level(): jnp.maximum(south_courant, 0.0) * masses[:, :-1, 1:-1]  56.9 us
    add x2, other arithmetic, advance_level(): jnp.maximum(east_courant, 0.0) * masses[:, 1:-1, :-1]  54.9 us
    all_gather x2, waiting for transfers between devices, smooth_winds(): fragment = lax.all_gather(selected, 'lon', axis=1, tiled=True)  52.1 us
    mul x3, other arithmetic, advance_level(): extended[:tracer_count] * thick[None]  37.8 us
    transpose x2, other arithmetic, shards(): tracers, thickness, zonal, meridional = advance_all(extended, pressure)  33.9 us
    slice x4, other arithmetic, extended_2(): lax.slice_in_dim(block, block.shape[dim] - width, None, axis=dim)  31 us
  transfers between devices with their start and end apart: 12, of which 7 were waited for; matrix products, arithmetic and copies ran while one was open for 30% of the time, Pallas kernels for 0%

commit v1 on v0

--- a/solution.py
+++ b/solution.py
@@ -1,8 +1,12 @@
+import functools
 import math
 
 import jax
 import jax.numpy as jnp
+import numpy as np
 from jax import lax
+from jax.experimental import pallas as pl
+from jax.experimental.pallas import tpu as pltpu
 from jax.sharding import PartitionSpec as P
 
 NSUB = 2
@@ -150,6 +154,820 @@
     return (tracers, thickness, zonal, meridional)
 
 
+LANE = 128
+PAD = 16
+BAND = 64
+
+
+def cost(flops, moved):
+    return pl.CostEstimate(flops=int(flops), bytes_accessed=int(moved), transcendentals=0)
+
+
+def params(mib=56):
+    return pltpu.CompilerParams(vmem_limit_bytes=mib * 1024 * 1024)
+
+
+def lanes():
+    return lax.broadcasted_iota(jnp.int32, (8, LANE), 1)
+
+
+def eight(index):
+    return pl.ds(pl.multiple_of(8 * index, 8), 8)
+
+
+def from_east(tiles, lane):
+    turned = [pltpu.roll(t, LANE - 1, 1) for t in tiles]
+    n = len(tiles)
+    return [jnp.where(lane < LANE - 1, turned[c], turned[(c + 1) % n]) for c in range(n)]
+
+
+def from_west(tiles, lane):
+    turned = [pltpu.roll(t, 1, 1) for t in tiles]
+    n = len(tiles)
+    return [jnp.where(lane > 0, turned[c], turned[(c - 1) % n]) for c in range(n)]
+
+
+def courant(a, b):
+    return COURANT_CAP * jnp.tanh(0.5 * (a + b))
+
+
+def rim_lanes(east, west, plane, last, lane):
+    to_east = lax.rem(last + LANE - 2 * plane, LANE)
+    to_west = lax.rem(2 * LANE - 2 - 2 * plane, LANE)
+    return jnp.where(lane < last + 2, pltpu.roll(east, to_east, 1), pltpu.roll(west, to_west, 1))
+
+
+def inflows(h, u, v, h_n, h_s, v_n, v_s, lane):
+    count = range(len(h))
+    u_e, h_e = from_east(u, lane), from_east(h, lane)
+    c_e = [courant(u[c], u_e[c]) for c in count]
+    out_e = [jnp.maximum(c_e[c], 0.0) * h[c] for c in count]
+    in_e = [jnp.maximum(-c_e[c], 0.0) * h_e[c] for c in count]
+    in_w, out_w = from_west(out_e, lane), from_west(in_e, lane)
+    c_s = [courant(v[c], v_s[c]) for c in count]
+    c_n = [courant(v_n[c], v[c]) for c in count]
+    in_s = [jnp.maximum(-c_s[c], 0.0) * h_s[c] for c in count]
+    out_s = [jnp.maximum(c_s[c], 0.0) * h[c] for c in count]
+    in_n = [jnp.maximum(c_n[c], 0.0) * h_n[c] for c in count]
+    out_n = [jnp.maximum(-c_n[c], 0.0) * h[c] for c in count]
+    new = [
+        h[c] - (out_e[c] - in_e[c]) + (in_w[c] - out_w[c]) - (out_s[c] - in_s[c]) + (in_n[c] - out_n[c])
+        for c in count
+    ]
+    return in_e, in_w, in_n, in_s, new
+
+
+def tiles_at(ref, base, count, lead=()):
+    return [ref[lead + (c, base, slice(None))] for c in range(count)]
+
+
+def inflows_at(h, u, v, row, count, lead, lane):
+    mid = pl.ds(pl.multiple_of(row, 8), 8)
+    up, down = pl.ds(row - 1, 8), pl.ds(row + 1, 8)
+    hl, vl = lead
+    return inflows(
+        tiles_at(h, mid, count, hl),
+        tiles_at(u, mid, count, vl),
+        tiles_at(v, mid, count, vl),
+        tiles_at(h, up, count, hl),
+        tiles_at(h, down, count, hl),
+        tiles_at(v, up, count, vl),
+        tiles_at(v, down, count, vl),
+        lane,
+    )
+
+
+def band_kernel(n, s, *refs):
+    ins, outs = refs[: 3 * n], refs[3 * n :]
+    for north in (True, False):
+
+        @pl.when(s[0] == int(north))
+        def _():
+            lo = 0 if north else BAND - POLAR
+            for d in range(n):
+                u, v, h = ins[3 * d : 3 * d + 3]
+                outs[d][0:POLAR, :] = u[0, lo : lo + POLAR, :]
+                outs[d][POLAR : 2 * POLAR, :] = v[0, lo : lo + POLAR, :]
+                first = 0 if north else BAND - POLAR - 1
+                outs[d][2 * POLAR : 3 * POLAR + 1, :] = h[0, first : first + POLAR + 1, :]
+                outs[d][3 * POLAR + 1 :, :] = jnp.zeros((3, h.shape[2]), jnp.float32)
+
+
+def band_rows(scalars, u, v, h, n):
+    levels, _, cols = u.shape
+
+    def spec(d):
+        return pl.BlockSpec(
+            (pl.Element(1), pl.Element(BAND), pl.Element(cols)),
+            lambda i, s: (lax.rem(s[1] + d, n), s[2] * 8, 0),
+        )
+
+    rows = 3 * POLAR + 4
+    return pl.pallas_call(
+        functools.partial(band_kernel, n),
+        grid_spec=pltpu.PrefetchScalarGridSpec(
+            num_scalar_prefetch=1,
+            grid=(1,),
+            in_specs=[spec(d) for d in range(n) for _ in range(3)],
+            out_specs=[pl.BlockSpec((rows, cols), lambda i, s: (0, 0))] * n,
+        ),
+        out_shape=[jax.ShapeDtypeStruct((rows, cols), jnp.float32)] * n,
+        cost_estimate=cost(1e6, 8 * n * rows * cols),
+        compiler_params=params(),
+        name="band_rows",
+    )(scalars, *([u, v, h] * n))
+
+
+def spectrum_kernel(n, s, *refs):
+    total = None
+    for d in range(n):
+        part = jnp.dot(
+            refs[d][...],
+            refs[n + d][0],
+            precision=lax.Precision.HIGHEST,
+            preferred_element_type=jnp.float32,
+        )
+        total = part if total is None else total + part
+    refs[2 * n][...] = total
+
+
+def spectra(scalars, pieces, basis):
+    n = len(pieces)
+    rows, cols = pieces[0].shape
+    waves = basis.shape[2]
+
+    def spec(d):
+        return pl.BlockSpec((1, cols, waves), lambda i, s: (lax.rem(s[1] + n - d, n), 0, 0))
+
+    return pl.pallas_call(
+        functools.partial(spectrum_kernel, n),
+        grid_spec=pltpu.PrefetchScalarGridSpec(
+            num_scalar_prefetch=1,
+            grid=(1,),
+            in_specs=[pl.BlockSpec((rows, cols), lambda i, s: (0, 0))] * n + [spec(d) for d in range(n)],
+            out_specs=pl.BlockSpec((rows, waves), lambda i, s: (0, 0)),
+        ),
+        out_shape=jax.ShapeDtypeStruct((rows, waves), jnp.float32),
+        cost_estimate=cost(12 * n * rows * cols * waves, 4 * n * cols * (rows + waves)),
+        compiler_params=params(),
+        name="spectra",
+    )(scalars, *pieces, *([basis] * n))
+
+
+def pack_kernel(fields, last, t_lo, t_hi, h_lo, h_hi, u_lo, u_hi, v_lo, v_hi, west, east):
+    level = pl.program_id(0)
+    lane = lanes()
+    lows = [(t_lo, (f, 0)) for f in range(fields - 3)] + [(h_lo, (0,)), (u_lo, (0,)), (v_lo, (0,))]
+    highs = [(t_hi, (f, 0)) for f in range(fields - 3)] + [(h_hi, (0,)), (u_hi, (0,)), (v_hi, (0,))]
+    begin = 2 * fields * level
+    mine = jnp.logical_and(lane >= begin, lane < begin + 2 * fields)
+
+    def step(i, _):
+        rows = eight(i)
+        got_w = got_e = jnp.zeros((8, LANE), jnp.float32)
+        for f in range(fields):
+            here = lane // 2 == f
+            ref, lead = lows[f]
+            tile = ref[lead + (rows, slice(None))]
+            got_w = jnp.where(here, pltpu.roll(tile, 2 * f, 1) if f else tile, got_w)
+            ref, lead = highs[f]
+            tile = ref[lead + (rows, slice(None))]
+            got_e = jnp.where(here, pltpu.roll(tile, (2 * f - last + 2) % LANE, 1), got_e)
+        west[rows, :] = jnp.where(mine, pltpu.roll(got_w, begin, 1), west[rows, :])
+        east[rows, :] = jnp.where(mine, pltpu.roll(got_e, begin, 1), east[rows, :])
+        return 0
+
+    lax.fori_loop(0, west.shape[0] // 8, step, 0)
+
+
+def pack_columns(tracers, h, u, v):
+    count, levels, rows, cols = tracers.shape
+    high = (cols - 1) // LANE
+    t_spec = [pl.BlockSpec((count, 1, rows, LANE), lambda l, c=c: (0, l, 0, c)) for c in (0, high)]
+    f_spec = [pl.BlockSpec((1, rows, LANE), lambda l, c=c: (l, 0, c)) for c in (0, high)]
+    out = jax.ShapeDtypeStruct((rows, LANE), jnp.float32)
+    return pl.pallas_call(
+        functools.partial(pack_kernel, count + 3, cols - LANE * high),
+        grid=(levels,),
+        in_specs=t_spec + f_spec * 3,
+        out_specs=[pl.BlockSpec((rows, LANE), lambda l: (0, 0))] * 2,
+        out_shape=[out, out],
+        cost_estimate=cost(1e7, 8 * (count + 3) * levels * rows * LANE),
+        compiler_params=params(),
+        name="pack_columns",
+    )(tracers, tracers, h, h, u, u, v, v)
+
+
+def rows_kernel(fields, s, t_top, t_bot, h_top, h_bot, u_top, u_bot, v_top, v_bot,
+                e_top, e_bot, w_top, w_bot, pole, facing, top, bot):
+    level = pl.program_id(0)
+    lane = lanes()
+    cols = h_top.shape[2]
+    tail = top.shape[1] - LANE
+    last = cols - tail
+    refs = [(t_top, t_bot, (f, 0)) for f in range(fields - 3)]
+    refs += [(h_top, h_bot, (0,)), (u_top, u_bot, (0,)), (v_top, v_bot, (0,))]
+    for f in range(fields):
+        plane = fields * level + f
+        a, b, lead = refs[f]
+        top[:, 0:cols] = a[lead]
+        bot[:, 0:cols] = b[lead]
+        top[:, cols:] = rim_lanes(e_top[...], w_top[...], plane, last, lane)[:, last:]
+        bot[:, cols:] = rim_lanes(e_bot[...], w_bot[...], plane, last, lane)[:, last:]
+        flip = -1.0 if f == fields - 1 else 1.0
+
+        @pl.when(s[0] == 1)
+        def _():
+            pole[0, f, 0:1, :] = flip * top[1:2, :]
+            pole[0, f, 1:2, :] = flip * top[0:1, :]
+            facing[0, f] = bot[6:8, :]
+
+        @pl.when(s[0] == 0)
+        def _():
+            pole[0, f, 0:1, :] = flip * bot[7:8, :]
+            pole[0, f, 1:2, :] = flip * bot[6:7, :]
+            facing[0, f] = top[0:2, :]
+
+
+def edge_rows(scalars, tracers, h, u, v, east, west):
+    count, levels, rows, cols = tracers.shape
+    fields = count + 3
+    width = LANE * ((cols - 1) // LANE + 1)
+    ends = (0, rows // 8 - 1)
+    t_spec = [pl.BlockSpec((count, 1, 8, cols), lambda l, s, r=r: (0, l, r, 0)) for r in ends]
+    f_spec = [pl.BlockSpec((1, 8, cols), lambda l, s, r=r: (l, r, 0)) for r in ends]
+    c_spec = [pl.BlockSpec((8, LANE), lambda l, s, r=r: (r, 0)) for r in ends]
+    out = jax.ShapeDtypeStruct((levels, fields, 2, width), jnp.float32)
+    return pl.pallas_call(
+        functools.partial(rows_kernel, fields),
+        grid_spec=pltpu.PrefetchScalarGridSpec(
+            num_scalar_prefetch=1,
+            grid=(levels,),
+            in_specs=t_spec + f_spec * 3 + c_spec * 2,
+            out_specs=[pl.BlockSpec((1, fields, 2, width), lambda l, s: (l, 0, 0, 0))] * 2,
+            scratch_shapes=[pltpu.VMEM((8, width), jnp.float32)] * 2,
+        ),
+        out_shape=[out, out],
+        cost_estimate=cost(1e6, 100 * levels * fields * width),
+        compiler_params=params(),
+        name="edge_rows",
+    )(scalars, tracers, tracers, h, h, u, u, v, v, east, east, west, west)
+
+
+def extend_kernel(fields, s, h, u, v, east, west, pole, facing, h_out, u_out, v_out, total):
+    level = pl.program_id(0)
+    lane = lanes()
+    rows, cols = h.shape[1:]
+    count = h_out.shape[1]
+    last = cols - LANE * (count - 1)
+    for f, (ref, out) in enumerate(((h, h_out), (u, u_out), (v, v_out))):
+        plane = fields * level + fields - 3 + f
+
+        def step(i, _):
+            here, there = eight(i), pl.ds(pl.multiple_of(8 * i, 8) + PAD, 8)
+            for c in range(count - 1):
+                out[0, c, there, :] = ref[0, here, c * LANE : (c + 1) * LANE]
+            out[0, count - 1, there, 0:last] = ref[0, here, LANE * (count - 1) : cols]
+            rim = rim_lanes(east[here, :], west[here, :], plane, last, lane)
+            out[0, count - 1, there, last:] = rim[:, last:]
+            return 0
+
+        lax.fori_loop(0, rows // 8, step, 0)
+        for c in range(count):
+            part = slice(c * LANE, (c + 1) * LANE)
+            a = pole[0, fields - 3 + f, :, part]
+            b = facing[0, fields - 3 + f, :, part]
+            out[0, c, PAD - 2 : PAD, :] = jnp.where(s[0] == 1, a, b)
+            out[0, c, PAD + rows : PAD + rows + 2, :] = jnp.where(s[0] == 1, b, a)
+
+    def add(i, _):
+        here = eight(i)
+        for c in range(count):
+            now = h_out[0, c, here, :]
+            total[c, here, :] = jnp.where(level == 0, now, total[c, here, :] + now)
+        return 0
+
+    lax.fori_loop(0, h_out.shape[2] // 8, add, 0)
+
+
+def extend_fields(scalars, h, u, v, east, west, pole, facing):
+    levels, rows, cols = h.shape
+    fields = pole.shape[1]
+    count = (cols - 1) // LANE + 1
+    tall = rows + 2 * PAD
+    f_spec = pl.BlockSpec((1, rows, cols), lambda l, s: (l, 0, 0))
+    c_spec = pl.BlockSpec((rows, LANE), lambda l, s: (0, 0))
+    r_spec = pl.BlockSpec((1, fields, 2, count * LANE), lambda l, s: (l, 0, 0, 0))
+    out = jax.ShapeDtypeStruct((levels, count, tall, LANE), jnp.float32)
+    return pl.pallas_call(
+        functools.partial(extend_kernel, fields),
+        grid_spec=pltpu.PrefetchScalarGridSpec(
+            num_scalar_prefetch=1,
+            grid=(levels,),
+            in_specs=[f_spec] * 3 + [c_spec] * 2 + [r_spec] * 2,
+            out_specs=[pl.BlockSpec((1, count, tall, LANE), lambda l, s: (l, 0, 0, 0))] * 3
+            + [pl.BlockSpec((count, tall, LANE), lambda l, s: (0, 0, 0))],
+        ),
+        out_shape=[out] * 3 + [jax.ShapeDtypeStruct((count, tall, LANE), jnp.float32)],
+        cost_estimate=cost(1e6, 28 * levels * tall * count * LANE),
+        compiler_params=params(),
+        name="extend_fields",
+    )(scalars, h, u, v, east, west, pole, facing)
+
+
+def first_kernel(h, u, v, above, u_out, v_out, h_out, total, cum, press):
+    level = pl.program_id(0)
+    lane = lanes()
+    count, tall = h.shape[1:3]
+
+    def column(i, _):
+        here = eight(i)
+        for c in range(count):
+            before = jnp.where(level == 0, above[c, here, :], cum[c, here, :])
+            now = h[0, c, here, :]
+            press[c, here, :] = before + 0.5 * now
+            cum[c, here, :] = before + now
+        return 0
+
+    lax.fori_loop(0, tall // 8, column, 0)
+
+    def step(i, _):
+        row = 8 * i
+        here = eight(i)
+        p = tiles_at(press, here, count)
+        p_e, p_w = from_east(p, lane), from_west(p, lane)
+        p_n, p_s = tiles_at(press, pl.ds(row - 1, 8), count), tiles_at(press, pl.ds(row + 1, 8), count)
+        new = inflows_at(h, u, v, row, count, ((0,), (0,)), lane)[4]
+        for c in range(count):
+            u_out[0, c, here, :] = u[0, c, here, :] - GRADIENT_COEF * (p_e[c] - p_w[c])
+            v_out[0, c, here, :] = v[0, c, here, :] - GRADIENT_COEF * (p_s[c] - p_n[c])
+            h_out[0, c, here, :] = new[c]
+            total[c, here, :] = jnp.where(level == 0, new[c], total[c, here, :] + new[c])
+        return 0
+
+    lax.fori_loop(1, tall // 8 - 1, step, 0)
+
+
+def first_substep(h, u, v, above):
+    levels, count, tall, _ = h.shape
+    spec = pl.BlockSpec((1, count, tall, LANE), lambda l: (l, 0, 0, 0))
+    flat = pl.BlockSpec((count, tall, LANE), lambda l: (0, 0, 0))
+    out = jax.ShapeDtypeStruct(h.shape, jnp.float32)
+    return pl.pallas_call(
+        first_kernel,
+        grid=(levels,),
+        in_specs=[spec] * 3 + [flat],
+        out_specs=[spec] * 3 + [flat],
+        out_shape=[out] * 3 + [jax.ShapeDtypeStruct((count, tall, LANE), jnp.float32)],
+        scratch_shapes=[pltpu.VMEM((count, tall, LANE), jnp.float32)] * 2,
+        cost_estimate=cost(80 * h.size, 30 * h.size),
+        compiler_params=params(),
+        name="first_substep",
+    )(h, u, v, above)
+
+
+def filter_kernel(n, s, *refs):
+    pieces = refs[:n]
+    above, limits, basis, slope, h0, u0, v0, u1, v1 = refs[n : n + 9]
+    u0_out, v0_out, u1_out, v1_out, h1_out, total = refs[n + 9 : n + 15]
+    held, lhs, rhs = refs[n + 15 :]
+    levels, count, slab = u0.shape[:3]
+    waves = basis.shape[1]
+    for d in range(n):
+        held[lax.rem(s[1] + n - d, n)] = pieces[d][...]
+    for raw, out in ((u0, u0_out), (v0, v0_out), (u1, u1_out), (v1, v1_out)):
+        out[...] = raw[...]
+    half = waves // 2
+    wave = lax.broadcasted_iota(jnp.int32, (POLAR, waves), 1)
+    wave = jnp.where(wave < half, wave, wave - half)
+    scale = jnp.where(wave == 0, 1.0, 2.0) / (n * s[3]).astype(jnp.float32)
+    keep = jnp.where(wave <= limits[0:POLAR, 0:1], scale, 0.0)
+    turn = jnp.where(lax.rem(wave[0:2], 2) == 0, 1.0, -1.0)
+    one = turn[0:1]
+    for north in (True, False):
+
+        @pl.when(s[0] == int(north))
+        def _():
+            first = PAD if north else PAD + BAND - POLAR
+            rim = PAD - 2 if north else PAD + BAND
+
+            def level_step(l, cum):
+                u = held[l, 0:POLAR, :] * keep
+                v = held[l, POLAR : 2 * POLAR, :] * keep
+                thick = held[l, 2 * POLAR : 3 * POLAR + 1, :]
+                p = cum + 0.5 * thick
+                if north:
+                    before = jnp.concatenate([one * p[0:1], p[0 : POLAR - 1]], 0)
+                    diff = (p[1:] - before) * keep
+                    rhs[0:POLAR, :] = p[0:POLAR] * keep
+                else:
+                    after = jnp.concatenate([p[2:], one * p[POLAR:]], 0)
+                    diff = (after - p[0:POLAR]) * keep
+                    rhs[0:POLAR, :] = p[1:] * keep
+                w = v - GRADIENT_COEF * diff
+                lhs[0:POLAR, :] = u
+                lhs[POLAR : 2 * POLAR, :] = v
+                lhs[2 * POLAR : 3 * POLAR, :] = w
+                for k, (x, sign) in enumerate(((u, 1.0), (v, -1.0), (w, -1.0))):
+                    a, b = (x[1:2], x[0:1]) if north else (x[POLAR - 1 :], x[POLAR - 2 : POLAR - 1])
+                    at = 3 * POLAR + 2 * k
+                    lhs[at : at + 1, :] = sign * one * a
+                    lhs[at + 1 : at + 2, :] = sign * one * b
+                back = jnp.dot(
+                    lhs[...], basis[0], precision=lax.Precision.HIGHEST, preferred_element_type=jnp.float32
+                )
+                grad = jnp.dot(
+                    rhs[...], slope[0], precision=lax.Precision.HIGHEST, preferred_element_type=jnp.float32
+                )
+                zonal = back[0:POLAR]
+                later = zonal - GRADIENT_COEF * grad[0:POLAR]
+                for c in range(count):
+                    part = slice(c * LANE, (c + 1) * LANE)
+                    u0_out[l, c, first : first + POLAR, :] = zonal[:, part]
+                    v0_out[l, c, first : first + POLAR, :] = back[POLAR : 2 * POLAR, part]
+                    u1_out[l, c, first : first + POLAR, :] = later[:, part]
+                    v1_out[l, c, first : first + POLAR, :] = back[2 * POLAR : 3 * POLAR, part]
+                    u0_out[l, c, rim : rim + 2, :] = back[3 * POLAR : 3 * POLAR + 2, part]
+                    v0_out[l, c, rim : rim + 2, :] = back[3 * POLAR + 2 : 3 * POLAR + 4, part]
+                    v1_out[l, c, rim : rim + 2, :] = back[3 * POLAR + 4 : 3 * POLAR + 6, part]
+                return cum + thick
+
+            lax.fori_loop(0, levels, level_step, above[0 : POLAR + 1, :])
+
+    lane = lanes()
+
+    def step(k, _):
+        l, i = k // (slab // 8 - 2), lax.rem(k, slab // 8 - 2) + 1
+        here = eight(i)
+        new = inflows_at(h0, u0_out, v0_out, 8 * i, count, ((l,), (l,)), lane)[4]
+        for c in range(count):
+            h1_out[l, c, here, :] = new[c]
+            total[c, here, :] = jnp.where(l == 0, new[c], total[c, here, :] + new[c])
+        return 0
+
+    lax.fori_loop(0, levels * (slab // 8 - 2), step, 0)
+
+
+def filtered_band(scalars, pieces, above, limits, basis, slope, fields):
+    n = len(pieces)
+    rows, waves = pieces[0].shape
+    width = basis.shape[2]
+    levels, count = fields[0].shape[:2]
+    slab = BAND + 2 * PAD
+    window = pl.BlockSpec(
+        (pl.Element(levels), pl.Element(count), pl.Element(slab), pl.Element(LANE)),
+        lambda i, s: (0, 0, s[2] * 8, 0),
+    )
+    out = jax.ShapeDtypeStruct((levels, count, slab, LANE), jnp.float32)
+    whole = pl.BlockSpec((levels, count, slab, LANE), lambda i, s: (0, 0, 0, 0))
+    return pl.pallas_call(
+        functools.partial(filter_kernel, n),
+        grid_spec=pltpu.PrefetchScalarGridSpec(
+            num_scalar_prefetch=1,
+            grid=(1,),
+            in_specs=[pl.BlockSpec((rows, waves), lambda i, s: (0, 0))] * n
+            + [
+                pl.BlockSpec(above.shape, lambda i, s: (0, 0)),
+                pl.BlockSpec(limits.shape, lambda i, s: (0, 0)),
+                pl.BlockSpec((1, waves, width), lambda i, s: (s[1], 0, 0)),
+                pl.BlockSpec((1, waves, width), lambda i, s: (s[1], 0, 0)),
+            ]
+            + [window] * 5,
+            out_specs=[whole] * 5 + [pl.BlockSpec((count, slab, LANE), lambda i, s: (0, 0, 0))],
+            scratch_shapes=[
+                pltpu.VMEM((n, rows, waves), jnp.float32),
+                pltpu.VMEM((3 * POLAR + 12, waves), jnp.float32),
+                pltpu.VMEM((BAND, waves), jnp.float32),
+            ],
+        ),
+        out_shape=[out] * 5 + [jax.ShapeDtypeStruct((count, slab, LANE), jnp.float32)],
+        cost_estimate=cost(12 * levels * 256 * waves * width, 40 * levels * count * slab * LANE),
+        compiler_params=params(),
+        name="filtered_band",
+    )(scalars, *pieces, above, limits, basis, slope, *fields)
+
+
+def slab_kernel(fields, group, rows, has_base, s, *refs):
+    (tr, h0, u0, v0, u1, v1, east, west, rim) = refs[:9]
+    refs = refs[11:] if has_base else refs[9:]
+    tr_out, h_out, early, late, first_h, t0, t1 = refs
+    level, part = pl.program_id(0), pl.program_id(1)
+    lane = lanes()
+    count = h0.shape[1]
+    cols = h_out.shape[2]
+    last = cols - LANE * (count - 1)
+    tiles = rows // 8
+
+    @pl.when(part == 0)
+    def _():
+        def one(i, _):
+            here = eight(i)
+            in_e, in_w, in_n, in_s, new = inflows_at(
+                h0, u0, v0, 8 * i + PAD - 8, count, ((0,), (0,)), lane
+            )
+            for c in range(count):
+                inv = 1.0 / new[c]
+                w = [x[c] * inv for x in (in_e, in_w, in_n, in_s)]
+                for k in range(4):
+                    early[k + 1, c, here, :] = w[k]
+                early[0, c, here, :] = 1.0 - ((w[0] + w[1]) + (w[2] + w[3]))
+                first_h[c, pl.ds(pl.multiple_of(8 * i, 8) + PAD - 8, 8), :] = new[c]
+            return 0
+
+        lax.fori_loop(0, tiles + 2, one, 0)
+
+        def two(i, _):
+            here = eight(i)
+            in_e, in_w, in_n, in_s, new = inflows_at(
+                first_h, u1, v1, 8 * i + PAD, count, ((), (0,)), lane
+            )
+            for c in range(count):
+                inv = 1.0 / new[c]
+                w = [x[c] * inv for x in (in_e, in_w, in_n, in_s)]
+                for k in range(4):
+                    late[k + 1, c, here, :] = w[k]
+                late[0, c, here, :] = 1.0 - ((w[0] + w[1]) + (w[2] + w[3]))
+                wide = min(LANE, cols - c * LANE)
+                h_out[0, here, c * LANE : c * LANE + wide] = new[c][:, 0:wide]
+            return 0
+
+        lax.fori_loop(0, tiles, two, 0)
+
+    def bring(i, _):
+        here = eight(i)
+        there = pl.ds(pl.multiple_of(8 * (i + s[4]), 8), 8)
+        rim_rows = eight(i + s[3])
+        e, w = east[rim_rows, :], west[rim_rows, :]
+        for j in range(group):
+            plane = fields * level + part * group + j
+            for c in range(count - 1):
+                t0[j, c, there, :] = tr[j, 0, here, c * LANE : (c + 1) * LANE]
+            t0[j, count - 1, there, 0:last] = tr[j, 0, here, LANE * (count - 1) : cols]
+            t0[j, count - 1, there, last:] = rim_lanes(e, w, plane, last, lane)[:, last:]
+        return 0
+
+    lax.fori_loop(0, tiles + 1, bring, 0)
+    for ends in (True, False):
+
+        @pl.when(s[5] == int(ends))
+        def _():
+            at = PAD + rows if ends else PAD - 2
+            for j in range(group):
+                for c in range(count):
+                    t0[j, c, at : at + 2, :] = rim[0, part * group + j, :, c * LANE : (c + 1) * LANE]
+
+    def advance(source, j, row, weights):
+        mid = tiles_at(source, pl.ds(pl.multiple_of(row, 8), 8), count, (j,))
+        up = tiles_at(source, pl.ds(row - 1, 8), count, (j,))
+        down = tiles_at(source, pl.ds(row + 1, 8), count, (j,))
+        right, left = from_east(mid, lane), from_west(mid, lane)
+        return [
+            weights[0][c] * mid[c]
+            + weights[1][c] * right[c]
+            + weights[2][c] * left[c]
+            + weights[3][c] * up[c]
+            + weights[4][c] * down[c]
+            for c in range(count)
+        ]
+
+    def one(i, _):
+        weights = [tiles_at(early, eight(i), count, (k,)) for k in range(5)]
+        for j in range(group):
+            new = advance(t0, j, 8 * i + PAD - 8, weights)
+            for c in range(count):
+                t1[j, c, pl.ds(pl.multiple_of(8 * i, 8) + PAD - 8, 8), :] = new[c]
+        return 0
+
+    lax.fori_loop(0, tiles + 2, one, 0)
+
+    def two(i, _):
+        here = eight(i)
+        weights = [tiles_at(late, here, count, (k,)) for k in range(5)]
+        for j in range(group):
+            new = advance(t1, j, 8 * i + PAD, weights)
+            for c in range(count):
+                wide = min(LANE, cols - c * LANE)
+                tr_out[j, 0, here, c * LANE : c * LANE + wide] = new[c][:, 0:wide]
+        return 0
+
+    lax.fori_loop(0, tiles, two, 0)
+
+
+def tracer_slab(scalars, tracers, slabs, offsets, east, west, rim, rows, base, group, name):
+    count, levels, height, cols = tracers.shape
+    tiles = slabs[0].shape[1]
+    slab = rows + 2 * PAD
+    E = pl.Element
+
+    def spec(moves):
+        return pl.BlockSpec(
+            (E(1), E(tiles), E(slab), E(LANE)), lambda l, g, s: (l, 0, s[2] * 8 if moves else 0, 0)
+        )
+
+    in_specs = [
+        pl.BlockSpec((E(group), E(1), E(rows + 8), E(cols)), lambda l, g, s: (g * group, l, s[3] * 8, 0))
+    ]
+    in_specs += [spec(m) for m in offsets]
+    in_specs += [pl.BlockSpec((height, LANE), lambda l, g, s: (0, 0))] * 2
+    in_specs += [pl.BlockSpec((1,) + rim.shape[1:], lambda l, g, s: (l, 0, 0, 0))]
+    operands = [tracers, *slabs, east, west, rim]
+    aliases = {}
+    if base is not None:
+        in_specs += [pl.BlockSpec(memory_space=pl.ANY)] * 2
+        operands += list(base)
+        aliases = {len(operands) - 1: 0, len(operands): 1}
+    return pl.pallas_call(
+        functools.partial(slab_kernel, rim.shape[1], group, rows, base is not None),
+        grid_spec=pltpu.PrefetchScalarGridSpec(
+            num_scalar_prefetch=1,
+            grid=(levels, count // group),
+            in_specs=in_specs,
+            out_specs=[
+                pl.BlockSpec((E(group), E(1), E(rows), E(cols)), lambda l, g, s: (g * group, l, s[2] * 8, 0)),
+                pl.BlockSpec((E(1), E(rows), E(cols)), lambda l, g, s: (l, s[2] * 8, 0)),
+            ],
+            scratch_shapes=[
+                pltpu.VMEM((5, tiles, rows + 16, LANE), jnp.float32),
+                pltpu.VMEM((5, tiles, rows, LANE), jnp.float32),
+                pltpu.VMEM((tiles, slab, LANE), jnp.float32),
+                pltpu.VMEM((group, tiles, slab, LANE), jnp.float32),
+                pltpu.VMEM((group, tiles, slab, LANE), jnp.float32),
+            ],
+        ),
+        out_shape=[
+            jax.ShapeDtypeStruct(tracers.shape, jnp.float32),
+            jax.ShapeDtypeStruct((levels, height, cols), jnp.float32),
+        ],
+        input_output_aliases=aliases,
+        cost_estimate=cost(60 * count * levels * rows * cols, 8 * count * levels * rows * cols),
+        compiler_params=params(),
+        name=name,
+    )(scalars, *operands)
+
+
+def winds_kernel(rows, has_base, s, h, u, v, above, *refs):
+    u_out, v_out, cum, press = refs[2:] if has_base else refs
+    level = pl.program_id(0)
+    lane = lanes()
+    count, slab = h.shape[1:3]
+    cols = u_out.shape[2]
+
+    def column(i, _):
+        here = eight(i)
+        for c in range(count):
+            before = jnp.where(level == 0, above[c, here, :], cum[c, here, :])
+            now = h[0, c, here, :]
+            press[c, here, :] = before + 0.5 * now
+            cum[c, here, :] = before + now
+        return 0
+
+    lax.fori_loop(0, slab // 8, column, 0)
+
+    def step(i, _):
+        row = 8 * i + PAD
+        mid = pl.ds(pl.multiple_of(row, 8), 8)
+        p = tiles_at(press, mid, count)
+        p_e, p_w = from_east(p, lane), from_west(p, lane)
+        p_n, p_s = tiles_at(press, pl.ds(row - 1, 8), count), tiles_at(press, pl.ds(row + 1, 8), count)
+        for c in range(count):
+            wide = min(LANE, cols - c * LANE)
+            part = slice(c * LANE, c * LANE + wide)
+            east = u[0, c, mid, :] - GRADIENT_COEF * (p_e[c] - p_w[c])
+            north = v[0, c, mid, :] - GRADIENT_COEF * (p_s[c] - p_n[c])
+            u_out[0, eight(i), part] = east[:, 0:wide]
+            v_out[0, eight(i), part] = north[:, 0:wide]
+        return 0
+
+    lax.fori_loop(0, rows // 8, step, 0)
+
+
+def last_winds(scalars, h, u, v, above, moves, rows, height, cols, base, name):
+    levels, tiles = h.shape[:2]
+    slab = rows + 2 * PAD
+    E = pl.Element
+    spec = pl.BlockSpec(
+        (E(1), E(tiles), E(slab), E(LANE)), lambda l, s: (l, 0, s[2] * 8 if moves else 0, 0)
+    )
+    flat = pl.BlockSpec((E(tiles), E(slab), E(LANE)), lambda l, s: (0, s[2] * 8 if moves else 0, 0))
+    out_spec = pl.BlockSpec((E(1), E(rows), E(cols)), lambda l, s: (l, s[2] * 8, 0))
+    out = jax.ShapeDtypeStruct((levels, height, cols), jnp.float32)
+    in_specs, operands, aliases = [spec] * 3 + [flat], [h, u, v, above], {}
+    if base is not None:
+        in_specs += [pl.BlockSpec(memory_space=pl.ANY)] * 2
+        operands += list(base)
+        aliases = {5: 0, 6: 1}
+    return pl.pallas_call(
+        functools.partial(winds_kernel, rows, base is not None),
+        grid_spec=pltpu.PrefetchScalarGridSpec(
+            num_scalar_prefetch=1,
+            grid=(levels,),
+            in_specs=in_specs,
+            out_specs=[out_spec] * 2,
+            scratch_shapes=[pltpu.VMEM((tiles, slab, LANE), jnp.float32)] * 2,
+        ),
+        out_shape=[out, out],
+        input_output_aliases=aliases,
+        cost_estimate=cost(20 * levels * rows * cols, 24 * levels * rows * cols),
+        compiler_params=params(),
+        name=name,
+    )(scalars, *operands)
+
+
+def bases(n, cols):
+    total = n * cols
+    wave = np.arange(KMAX + 1)
+    cell = np.arange(total).reshape(n, cols)
+    angle = (cell[:, :, None] * wave % total) * (2.0 * math.pi / total)
+    forward = np.concatenate([np.cos(angle), np.sin(angle)], 2)
+    width = LANE * ((cols - 1) // LANE + 1)
+    lane = np.arange(width)
+    lane = np.where(lane < width - 2, lane, lane - width)
+    cell = np.arange(n)[:, None] * cols + lane[None, :]
+    angle = (cell[:, None, :] * wave[:, None] % total) * (2.0 * math.pi / total)
+    inverse = np.concatenate([np.cos(angle), np.sin(angle)], 1)
+    steep = 2.0 * np.sin(wave * (2.0 * math.pi / total))[:, None]
+    slope = np.concatenate([-steep * np.sin(angle), steep * np.cos(angle)], 1)
+    return [jnp.asarray(x.astype(np.float32)) for x in (forward, inverse, slope)]
+
+
+def shards_tiled(tracers, thickness, zonal, meridional, cutoff):
+    count, levels, rows, cols = tracers.shape
+    n = lax.axis_size("lon")
+    me = lax.axis_index("lon").astype(jnp.int32)
+    north = (lax.axis_index("lat") == 0).astype(jnp.int32)
+    inner = rows - BAND
+
+    def pick(a, b):
+        return jnp.where(north == 1, a, b).astype(jnp.int32)
+
+    bandwise = jnp.stack([north, me, pick(0, inner // 8), jnp.int32(cols), jnp.int32(0), jnp.int32(0)])
+    polar = jnp.stack(
+        [north, me, pick(0, inner // 8), pick(0, inner // 8 - 1), pick(PAD // 8, PAD // 8 - 1), 1 - north]
+    )
+    middle = jnp.stack(
+        [north, me, pick(BAND // 8, 0), pick(BAND // 8 - 1, 0), pick(PAD // 8 - 1, PAD // 8), north]
+    )
+    forward, inverse, slope = bases(n, cols)
+
+    def along(value, d):
+        return lax.ppermute(value, "lon", [(i, (i + d) % n) for i in range(n)])
+
+    def to_lower(value):
+        return lax.ppermute(value, "lev", [(0, 1)])
+
+    sent = band_rows(bandwise, zonal, meridional, thickness, n)
+    pieces = [sent[0]] + [along(sent[d], d) for d in range(1, n)]
+    west_cols, east_cols = pack_columns(tracers, thickness, zonal, meridional)
+    east, west = along(west_cols, n - 1), along(east_cols, 1)
+    pole, facing = edge_rows(bandwise, tracers, thickness, zonal, meridional, east, west)
+    pole = along(pole, n // 2)
+    facing = lax.ppermute(facing, "lat", [(0, 1), (1, 0)])
+
+    own = spectra(bandwise, pieces, forward)
+    pieces = [own] + [along(own, d) for d in range(1, n)]
+    above_band = to_lower(sum(p[2 * POLAR :] for p in pieces))
+
+    h0, u0, v0, column = extend_fields(bandwise, thickness, zonal, meridional, east, west, pole, facing)
+    u1, v1, h1, column = first_substep(h0, u0, v0, to_lower(column))
+    tr, h2 = tracer_slab(
+        middle, tracers, (h0, u0, v0, u1, v1), (True,) * 5, east, west, facing, inner, None, 5, "tracers_inner"
+    )
+    winds = last_winds(middle, h1, u1, v1, to_lower(column), True, inner, rows, cols, None, "winds_inner")
+
+    limits = jnp.where(north == 1, cutoff[0], cutoff[1])
+    limits = jnp.broadcast_to(jnp.pad(limits, (0, BAND - POLAR))[:, None], (BAND, LANE))
+    u0b, v0b, u1b, v1b, h1b, column = filtered_band(
+        bandwise, pieces, above_band, limits, inverse, slope, (h0, u0, v0, u1, v1)
+    )
+    above = to_lower(column)
+    tr, h2 = tracer_slab(
+        polar, tracers, (h0, u0b, v0b, u1b, v1b), (True,) + (False,) * 4, east, west, pole, BAND, (tr, h2), 10,
+        "tracers_polar",
+    )
+    u2, v2 = last_winds(polar, h1b, u1b, v1b, above, False, BAND, rows, cols, winds, "winds_polar")
+    return (tr, h2, u2, v2)
+
+
+def tiles_fit(mesh, tracers):
+    count, levels, rows, cols = tracers.shape
+    rows, cols = rows // mesh.shape["lat"], cols // mesh.shape["lon"]
+    count, levels = count // mesh.shape["member"], levels // mesh.shape["lev"]
+    last = (cols - 1) % LANE + 1
+    return (
+        mesh.shape["lat"] == 2
+        and mesh.shape["lev"] == 2
+        and levels == mesh.shape["lon"]
+        and mesh.shape["lon"] % 2 == 0
+        and rows % 8 == 0
+        and rows >= 2 * BAND + 8
+        and last + 4 <= LANE
+        and last >= 2
+        and cols > LANE
+        and 2 * (count + 3) * levels <= LANE
+        and count % 5 == 0
+    )
+
+
 def solution(mesh):
     placed = (
         P("member", "lev", "lat", "lon"),
@@ -158,15 +976,15 @@
         P(("member", "lev"), "lat", "lon"),
         P(),
     )
-    return jax.shard_map(
-        shards,
-        mesh=mesh,
-        in_specs=placed,
-        out_specs=(
-            P("member", "lev", "lat", "lon"),
-            P(("member", "lev"), "lat", "lon"),
-            P(("member", "lev"), "lat", "lon"),
-            P(("member", "lev"), "lat", "lon"),
-        ),
-        check_vma=False,
-    )
+    outs = (
+        P("member", "lev", "lat", "lon"),
+        P(("member", "lev"), "lat", "lon"),
+        P(("member", "lev"), "lat", "lon"),
+        P(("member", "lev"), "lat", "lon"),
+    )
+
+    def program(*args):
+        part = shards_tiled if tiles_fit(mesh, args[0]) else shards
+        return jax.shard_map(part, mesh=mesh, in_specs=placed, out_specs=outs, check_vma=False)(*args)
+
+    return program

time: 682 us -> 398 us (0.58)
  other arithmetic: 429 us -> 1.04 us
  Pallas kernels: 0 us -> 346 us
  local copies, waits for them, and re-layouts: 131 us -> 7.69 us
  waiting for transfers between devices: 67.8 us -> 21.3 us
  matrix products: 20.2 us -> 0 us
  between operations: 14.8 us -> 0.85 us
  starting transfers between devices: 9.63 us -> 20.8 us
    pallas_call x0 -> x11, Pallas kernels: none -> 346 us  [the longest x2 179 us: tracer_slab(): pl.pallas_call(functools.partial(slab_kernel, rim.shape[1], group, rows,...]
    add x5 -> x1, other arithmetic: 112 us -> 1.03 us  [shards_tiled(): above_band = to_lower(sum((p[2 * POLAR:] for p in pieces)))]
    sub x4 -> x0, other arithmetic: 105 us -> none  [the longest x2 96 us: advance_level(): masses[:, 1:-1, 1:-1] - (east_flux[:, :, 1:] - east_flux[:, :, :-1])]
    concatenate x2 -> x0, other arithmetic: 78.4 us -> none  [extended_2(): block = jnp.concatenate([low, block, high], axis=dim)]
    all_gather x2 -> x0, waiting for transfers between devices: 52.1 us -> none  [smooth_winds(): fragment = lax.all_gather(selected, 'lon', axis=1, tiled=True)]
    scatter x4 -> x0, local copies, waits for them, and re-layouts: 47.1 us -> none  [the longest x2 24.8 us: shards(): extended = extended.at[:, :, 0, 1:-1].set(north_rim)]
    mul x3 -> x0, other arithmetic: 37.8 us -> none  [advance_level(): extended[:tracer_count] * thick[None]]
    transpose x2 -> x0, other arithmetic: 33.9 us -> none  [shards(): tracers, thickness, zonal, meridional = advance_all(extended, pressure)]
  transfers between devices with their start and end apart: 12 -> 14, of which waited for: 7 -> 4; matrix products, arithmetic and copies ran while one was open for 30% -> 1% of each run, Pallas kernels for 0% -> 76%
where the time goes in v1:
time: 398 us
  Pallas kernels  346 us (87%)
  waiting for transfers between devices  21.3 us (5%)
  starting transfers between devices  20.8 us (5%)
  local copies, waits for them, and re-layouts  7.69 us (2%)
    pallas_call x2, Pallas kernels, tracer_slab(): pl.pallas_call(functools.partial(slab_kernel, rim.shape[1], group, rows,...  179 us
    pallas_call x1, Pallas kernels, extend_fields(): pl.pallas_call(functools.partial(extend_kernel, fields), grid_spec=pltpu....  44.1 us
    pallas_call x1, Pallas kernels, first_substep(): pl.pallas_call(first_kernel, grid=(levels,), in_specs=[spec] * 3 + [flat]...  35.8 us
    pallas_call x1, Pallas kernels, pack_columns(): pl.pallas_call(functools.partial(pack_kernel, count + 3, cols - LANE * hi...  32.5 us
    pallas_call x2, Pallas kernels, last_winds(): pl.pallas_call(functools.partial(winds_kernel, rows, base is not None), g...  22.4 us
    ppermute x9, waiting for transfers between devices, along(): return lax.ppermute(value, 'lon', [(i, (i + d) % n) for i in range(n)])  20.4 us
    pallas_call x1, Pallas kernels, filtered_band(): pl.pallas_call(functools.partial(filter_kernel, n), grid_spec=pltpu.Prefe...  16.4 us
    ppermute x9, starting transfers between devices, along(): return lax.ppermute(value, 'lon', [(i, (i + d) % n) for i in range(n)])  13 us
  transfers between devices with their start and end apart: 14, of which 4 were waited for; matrix products, arithmetic and copies ran while one was open for 1% of the time, Pallas kernels for 76%

profile of v1, /device:TPU:0, one launch (start us, length us, event | category | flops | bytes accessed | tf_op | source)
XLA Modules:
  0.0 397.8 jit_solution(15025448548556214546)
XLA Ops:
  0.6 32.5 %pack_columns.1 = (f32[360,128]{1,0:T(8,128)}, f32[360,128]{1,0:T(8,128)}) custom-call(f32[10,4,360,360]{3,2,1,0:T(8,128)} %refs_0_.5, f32[10,4,360,360]{3,2,1,0:T(8,128)} %refs_0_.5, f32[4,360,360]{2,1,0:T(8,128)} %refs_11_.1, f32[4,360,360]{2,1,0:T(8,128)} %refs_11_.1, f32[4,360,360]{2,1,0:T(8,128)} %refs_9_.1, f32[4,360,360]{2,1,0:T(8,128)} %refs_9_.1, ...), custom_call_target="tpu_custom_call" | custom-call | flops 10000000 | bytes 19169280 | tf_op jit(solution)/shard_map/pack_columns/pallas_call | solution.py:349
  33.2 5.0 %collective-permute-start = (f32[360,128]{1,0:T(8,128)}, f32[360,128]{1,0:T(8,128)S(1)}, u32[]{:S(2)}, u32[]{:S(2)}) collective-permute-start(f32[360,128]{1,0:T(8,128)} %get-tuple-element.34), channel_id=1, source_target_pairs={{0,12},{4,0},{8,4},{12,8},{1,13},{5,1},{9,5},{13,9},{2,14},{6,2},{... | collective-permute-start | bytes 552968 | tf_op jit(solution)/shard_map/ppermute | solution.py:913
  38.2 0.0 collective-permute-start.1
  38.2 0.7 stack.49.s
  38.9 4.7 %collective-permute-done.e_top.e_bot.east.refs_6_ = f32[360,128]{1,0:T(8,128)S(1)} collective-permute-done((f32[360,128]{1,0:T(8,128)}, f32[360,128]{1,0:T(8,128)S(1)}, u32[]{:S(2)}, u32[]{:S(2)}) %collective-permute-start) | collective-permute-done | bytes 184352 | tf_op jit(solution)/shard_map/ppermute | solution.py:913
  43.6 3.6 collective-permute-done.1.w_top.w_bot.west.refs_7_
  47.2 0.0 copy-done
  47.2 0.7 copy-done.1
  47.9 6.7 %edge_rows.1 = (f32[4,13,2,384]{3,2,1,0:T(2,128)}, f32[4,13,2,384]{3,2,1,0:T(2,128)}) custom-call(s32[6]{0:T(128)} %stack.49.s, f32[10,4,360,360]{3,2,1,0:T(8,128)} %refs_0_.5, f32[10,4,360,360]{3,2,1,0:T(8,128)} %refs_0_.5, f32[4,360,360]{2,1,0:T(8,128)} %refs_11_.1, f32[4,360,360]{2,1,0:T(8,128)} %refs_11_.1, f32[4,360,360]{2,1,0:T(8,128)} %refs_9_.1, ...), custom_call_target="tpu_custom_call" | custom-call | flops 1000000 | bytes 1996800 | tf_op jit(solution)/shard_map/edge_rows/pallas_call | solution.py:401
  54.6 0.8 collective-permute-start.2
  55.4 1.6 collective-permute-start.3
  57.0 3.1 band_rows.1
  60.1 1.6 collective-permute-start.4
  61.6 2.2 collective-permute-start.5
  63.9 1.3 collective-permute-start.6
  65.2 12.1 %collective-permute-done.2.pole.refs_8_ = f32[4,13,2,384]{3,2,1,0:T(2,128)S(1)} collective-permute-done((f32[4,13,2,384]{3,2,1,0:T(2,128)}, f32[4,13,2,384]{3,2,1,0:T(2,128)S(1)}, u32[]{:S(2)}, u32[]{:S(2)}) %collective-permute-start.2) | collective-permute-done | bytes 159776 | tf_op jit(solution)/shard_map/ppermute | solution.py:913
  77.3 0.0 collective-permute-done.3.facing.refs_8_
  77.3 0.7 copy-done.2
  77.9 0.7 copy-done.3
  78.6 44.1 %extend_fields.1 = (f32[4,3,392,128]{3,2,1,0:T(8,128)}, f32[4,3,392,128]{3,2,1,0:T(8,128)}, f32[4,3,392,128]{3,2,1,0:T(8,128)}, f32[3,392,128]{2,1,0:T(8,128)}) custom-call(s32[6]{0:T(128)} %stack.49.s, f32[4,360,360]{2,1,0:T(8,128)} %refs_11_.1, f32[4,360,360]{2,1,0:T(8,128)} %refs_9_.1, f32[4,360,360]{2,1,0:T(8,128)} %refs_10_.1, f32[360,128]{1,0:T(8,128)} %copy-done, ...), custom_call_target="tpu_custom_call" | custom-call | flops 1000000 | bytes 16859136 | tf_op jit(solution)/shard_map/extend_fields/pallas_call | solution.py:462
  122.7 1.3 collective-permute-start.11
  124.0 0.0 collective-permute-done.4.refs_1_
  124.0 0.0 copy-start.9
  124.0 0.0 collective-permute-done.5.refs_2_
  124.1 0.0 copy-start.10
  124.1 0.0 collective-permute-done.6.refs_3_
  124.1 0.0 copy-start.11
  124.1 0.7 copy-done.9
  124.7 0.1 copy-done.10
  124.8 0.1 copy-done.11
  124.9 5.8 %spectra.1.refs_0_ = f32[184,384]{1,0:T(8,128)} custom-call(s32[6]{0:T(128)} %stack.49.s, f32[184,360]{1,0:T(8,128)} %get-tuple-element.39.refs_0_, f32[184,360]{1,0:T(8,128)} %copy-done.9, f32[184,360]{1,0:T(8,128)} %copy-done.10, f32[184,360]{1,0:T(8,128)} %copy-done.11, f32[4,360,384]{2,1,0:T(8,128)} %constant.32.clone.refs_4_.refs_5_.refs_6_.refs_7_, ...), custom_call_target="tpu_custom_call" | custom-call | flops 1220935680 | bytes 3271680 | tf_op jit(solution)/shard_map/spectra/pallas_call | solution.py:302
  130.8 0.0 collective-permute-start.9
  130.8 0.0 collective-permute-start.8
  130.8 2.0 collective-permute-start.7
  132.8 0.0 collective-permute-done.11.above
  132.8 0.8 copy-done.5
  133.6 35.8 %first_substep.1 = (f32[4,3,392,128]{3,2,1,0:T(8,128)}, f32[4,3,392,128]{3,2,1,0:T(8,128)}, f32[4,3,392,128]{3,2,1,0:T(8,128)}, f32[3,392,128]{2,1,0:T(8,128)}) custom-call(f32[4,3,392,128]{3,2,1,0:T(8,128)} %get-tuple-element.38.h.refs_8_.refs_1_, f32[4,3,392,128]{3,2,1,0:T(8,128)} %get-tuple-element.43.u.refs_9_.refs_2_, ...), custom_call_target="tpu_custom_call" | custom-call | flops 48168960 | bytes 18063360 | tf_op jit(solution)/shard_map/first_substep/pallas_call | solution.py:516
  169.4 1.3 collective-permute-start.13
  170.8 0.0 collective-permute-done.9.refs_3_
  170.8 0.0 copy-start.6
  170.8 0.0 collective-permute-done.8.refs_2_
  170.8 0.0 copy-start.7
  170.8 0.0 collective-permute-done.7.refs_1_
  170.8 0.0 copy-start.8
  170.8 1.0 slice_add_fusion
  171.8 1.3 collective-permute-start.10
  173.2 0.0 copy-done.14
  173.2 0.9 collective-permute-done.10.refs_4_
  174.1 0.7 broadcast_in_dim.2.refs_5_
  174.8 0.0 copy-done.7
  174.8 0.0 copy-done.13
  174.8 16.4 %filtered_band.1 = (f32[4,3,96,128]{3,2,1,0:T(8,128)}, f32[4,3,96,128]{3,2,1,0:T(8,128)}, f32[4,3,96,128]{3,2,1,0:T(8,128)}, f32[4,3,96,128]{3,2,1,0:T(8,128)}, ...) custom-call(s32[6]{0:T(128)} %stack.49.s, f32[184,384]{1,0:T(8,128)} %spectra.1.refs_0_, f32[184,384]{1,0:T(8,128)} %copy-done.8, ...), custom_call_target="tpu_custom_call" | custom-call | flops 1811939328 | bytes 5898240 | tf_op jit(solution)/shard_map/filtered_band/pallas_call | solution.py:623
  191.1 2.3 collective-permute-start.12
  193.4 0.6 stack.53.s
  194.0 0.6 stack.48.s
  194.6 149.1 %tracers_inner.1 = (f32[10,4,360,360]{3,2,1,0:T(8,128)}, f32[4,360,360]{2,1,0:T(8,128)}) custom-call(s32[6]{0:T(128)} %stack.53.s, f32[10,4,360,360]{3,2,1,0:T(8,128)} %refs_0_.5, f32[4,3,392,128]{3,2,1,0:T(8,128)} %get-tuple-element.38.h.refs_8_.refs_1_, f32[4,3,392,128]{3,2,1,0:T(8,128)} %get-tuple-element.43.u.refs_9_.refs_2_, ...), custom_call_target="tpu_custom_call" | custom-call | flops 255744000 | bytes 34099200 | tf_op jit(solution)/shard_map/tracers_inner/pallas_call | solution.py:779
  343.7 30.2 %tracers_polar.1 = (f32[10,4,360,360]{3,2,1,0:T(8,128)}, f32[4,360,360]{2,1,0:T(8,128)}) custom-call(s32[6]{0:T(128)} %stack.48.s, f32[10,4,360,360]{3,2,1,0:T(8,128)} %refs_0_.5, f32[4,3,392,128]{3,2,1,0:T(8,128)} %get-tuple-element.38.h.refs_8_.refs_1_, ...), custom_call_target="tpu_custom_call", output_to_operand_aliasing={{0}: (10, {}), {1}: (11, {})} | custom-call | flops 55296000 | bytes 7372800 | tf_op jit(solution)/shard_map/tracers_polar/pallas_call | solution.py:779
  373.9 0.0 collective-permute-done.13.above
  373.9 0.0 copy-start.4
  373.9 0.8 copy-done.4
  374.7 16.4 %winds_inner.1 = (f32[4,360,360]{2,1,0:T(8,128)}, f32[4,360,360]{2,1,0:T(8,128)}) custom-call(s32[6]{0:T(128)} %stack.53.s, f32[4,3,392,128]{3,2,1,0:T(8,128)} %get-tuple-element.58.h, f32[4,3,392,128]{3,2,1,0:T(8,128)} %get-tuple-element.46.refs_11_.refs_4_.u, f32[4,3,392,128]{3,2,1,0:T(8,128)} %get-tuple-element.47.refs_12_.refs_5_.v, f32[3,392,128]{2,1,0:T(8,128)} %copy-done.4), custom_call_target="tpu_custom_call" | custom-call | flops 8524800 | bytes 10229760 | tf_op jit(solution)/shard_map/winds_inner/pallas_call | solution.py:859
  391.2 0.0 collective-permute-done.12.above
  391.2 0.6 copy-done.12
  391.8 6.0 %winds_polar.1 = (f32[4,360,360]{2,1,0:T(8,128)}, f32[4,360,360]{2,1,0:T(8,128)}) custom-call(s32[6]{0:T(128)} %stack.48.s, f32[4,3,96,128]{3,2,1,0:T(8,128)} %get-tuple-element.56.h, f32[4,3,96,128]{3,2,1,0:T(8,128)} %get-tuple-element.50.refs_4_.u, f32[4,3,96,128]{3,2,1,0:T(8,128)} %get-tuple-element.51.refs_5_.v, ...), custom_call_target="tpu_custom_call", output_to_operand_aliasing={{0}: (5, {}), {1}: (6, {})} | custom-call | flops 1843200 | bytes 2211840 | tf_op jit(solution)/shard_map/winds_polar/pallas_call | solution.py:859
  (13 shorter events, 0.0 us)
Async XLA Ops:
  33.2 10.4 %collective-permute-start = (f32[360,128]{1,0:T(8,128)}, f32[360,128]{1,0:T(8,128)S(1)}, u32[]{:S(2)}, u32[]{:S(2)}) collective-permute-start(f32[360,128]{1,0:T(8,128)} %get-tuple-element.34), channel_id=1, source_target_pairs={{0,12},{4,0},{8,4},{12,8},{1,13},{5,1},{9,5},{13,9},{2,14},{6,2},{... | collective-permute-start | bytes 552968 | tf_op jit(solution)/shard_map/ppermute | solution.py:913
  38.2 9.0 %collective-permute-start.1 = (f32[360,128]{1,0:T(8,128)}, f32[360,128]{1,0:T(8,128)S(1)}, u32[]{:S(2)}, u32[]{:S(2)}) collective-permute-start(f32[360,128]{1,0:T(8,128)} %get-tuple-element.35), channel_id=1, source_target_pairs={{0,4},{4,8},{8,12},{12,0},{1,5},{5,9},{9,13},{13,1},{2,6},{6,10},{... | collective-permute-start | bytes 552968 | tf_op jit(solution)/shard_map/ppermute | solution.py:913
  43.6 3.6 copy-start
  47.2 0.7 copy-start.1
  54.6 22.7 %collective-permute-start.2 = (f32[4,13,2,384]{3,2,1,0:T(2,128)}, f32[4,13,2,384]{3,2,1,0:T(2,128)S(1)}, u32[]{:S(2)}, u32[]{:S(2)}) collective-permute-start(f32[4,13,2,384]{3,2,1,0:T(2,128)} %get-tuple-element.36), channel_id=1, source_target_pairs={{0,8},{4,12},{8,0},{12,4},{1,9},{5,13},{9,1},{13,5},{2,10},{6,14},... | collective-permute-start | bytes 479240 | tf_op jit(solution)/shard_map/ppermute | solution.py:913
  55.4 21.9 %collective-permute-start.3 = (f32[4,13,2,384]{3,2,1,0:T(2,128)}, f32[4,13,2,384]{3,2,1,0:T(2,128)S(1)}, u32[]{:S(2)}, u32[]{:S(2)}) collective-permute-start(f32[4,13,2,384]{3,2,1,0:T(2,128)} %get-tuple-element.37), channel_id=1, source_target_pairs={{0,2},{2,0},{1,3},{3,1},{4,6},{6,4},{5,7},{7,5},{8,10},{10,8},{9,1... | collective-permute-start | bytes 479240 | tf_op jit(solution)/shard_map/ppermute | solution.py:924
  60.1 64.0 %collective-permute-start.4 = (f32[184,360]{1,0:T(8,128)}, f32[184,360]{1,0:T(8,128)S(1)}, u32[]{:S(2)}, u32[]{:S(2)}) collective-permute-start(f32[184,360]{1,0:T(8,128)} %get-tuple-element.40), channel_id=1, source_target_pairs={{0,4},{4,8},{8,12},{12,0},{1,5},{5,9},{9,13},{13,1},{2,6},{6,10},{... | collective-permute-start | bytes 794888 | tf_op jit(solution)/shard_map/ppermute | solution.py:913
  61.6 62.4 %collective-permute-start.5 = (f32[184,360]{1,0:T(8,128)}, f32[184,360]{1,0:T(8,128)S(1)}, u32[]{:S(2)}, u32[]{:S(2)}) collective-permute-start(f32[184,360]{1,0:T(8,128)} %get-tuple-element.41), channel_id=1, source_target_pairs={{0,8},{4,12},{8,0},{12,4},{1,9},{5,13},{9,1},{13,5},{2,10},{6,14},... | collective-permute-start | bytes 794888 | tf_op jit(solution)/shard_map/ppermute | solution.py:913
  63.9 60.2 %collective-permute-start.6 = (f32[184,360]{1,0:T(8,128)}, f32[184,360]{1,0:T(8,128)S(1)}, u32[]{:S(2)}, u32[]{:S(2)}) collective-permute-start(f32[184,360]{1,0:T(8,128)} %get-tuple-element.42), channel_id=1, source_target_pairs={{0,12},{4,0},{8,4},{12,8},{1,13},{5,1},{9,5},{13,9},{2,14},{6,2},{... | collective-permute-start | bytes 794888 | tf_op jit(solution)/shard_map/ppermute | solution.py:913
  77.3 0.7 copy-start.2
  77.9 0.7 copy-start.3
  122.7 10.1 %collective-permute-start.11 = (f32[3,392,128]{2,1,0:T(8,128)}, f32[3,392,128]{2,1,0:T(8,128)S(1)}, u32[]{:S(2)}, u32[]{:S(2)}) collective-permute-start(f32[3,392,128]{2,1,0:T(8,128)} %get-tuple-element.45), channel_id=1, source_target_pairs={{0,1},{2,3},{4,5},{6,7},{8,9},{10,11},{12,13},{14,15},{16,17},{18,... | collective-permute-start | bytes 1806344 | tf_op jit(solution)/shard_map/ppermute | solution.py:916
  124.0 0.7 copy-start.9
  124.1 0.8 copy-start.10
  124.1 0.9 copy-start.11
  130.8 40.0 %collective-permute-start.9 = (f32[184,384]{1,0:T(8,128)}, f32[184,384]{1,0:T(8,128)S(1)}, u32[]{:S(2)}, u32[]{:S(2)}) collective-permute-start(f32[184,384]{1,0:T(8,128)} %spectra.1.refs_0_), channel_id=1, source_target_pairs={{0,12},{4,0},{8,4},{12,8},{1,13},{5,1},{9,5},{13,9},{2,14},{6,2},{... | collective-permute-start | bytes 847880 | tf_op jit(solution)/shard_map/ppermute | solution.py:913
  130.8 40.0 %collective-permute-start.8 = (f32[184,384]{1,0:T(8,128)}, f32[184,384]{1,0:T(8,128)S(1)}, u32[]{:S(2)}, u32[]{:S(2)}) collective-permute-start(f32[184,384]{1,0:T(8,128)} %spectra.1.refs_0_), channel_id=1, source_target_pairs={{0,8},{4,12},{8,0},{12,4},{1,9},{5,13},{9,1},{13,5},{2,10},{6,14},... | collective-permute-start | bytes 847880 | tf_op jit(solution)/shard_map/ppermute | solution.py:913
  130.8 40.0 %collective-permute-start.7 = (f32[184,384]{1,0:T(8,128)}, f32[184,384]{1,0:T(8,128)S(1)}, u32[]{:S(2)}, u32[]{:S(2)}) collective-permute-start(f32[184,384]{1,0:T(8,128)} %spectra.1.refs_0_), channel_id=1, source_target_pairs={{0,4},{4,8},{8,12},{12,0},{1,5},{5,9},{9,13},{13,1},{2,6},{6,10},{... | collective-permute-start | bytes 847880 | tf_op jit(solution)/shard_map/ppermute | solution.py:913
  132.8 0.8 copy-start.5
  133.6 39.5 %copy-start.14 = (s32[2,60]{1,0:T(2,128)S(1)}, s32[2,60]{1,0:T(2,128)}, u32[]{:S(2)}) copy-start(s32[2,60]{1,0:T(2,128)} %param.12) | copy-start | bytes 1444
  169.4 204.5 %collective-permute-start.13 = (f32[3,392,128]{2,1,0:T(8,128)}, f32[3,392,128]{2,1,0:T(8,128)S(1)}, u32[]{:S(2)}, u32[]{:S(2)}) collective-permute-start(f32[3,392,128]{2,1,0:T(8,128)} %get-tuple-element.59), channel_id=1, source_target_pairs={{0,1},{2,3},{4,5},{6,7},{8,9},{10,11},{12,13},{14,15},{16,17},{18,... | collective-permute-start | bytes 1806344 | tf_op jit(solution)/shard_map/ppermute | solution.py:916
  170.8 4.0 %copy-start.6 = (f32[184,384]{1,0:T(8,128)}, f32[184,384]{1,0:T(8,128)S(1)}, u32[]{:S(2)}) copy-start(f32[184,384]{1,0:T(8,128)S(1)} %collective-permute-done.9.refs_3_) | copy-start | bytes 847876
  170.8 4.0 copy-start.7
  170.8 4.0 copy-start.8
  171.8 2.2 collective-permute-start.10
  174.1 0.7 copy-start.13
  191.1 200.1 %collective-permute-start.12 = (f32[3,96,128]{2,1,0:T(8,128)}, f32[3,96,128]{2,1,0:T(8,128)S(1)}, u32[]{:S(2)}, u32[]{:S(2)}) collective-permute-start(f32[3,96,128]{2,1,0:T(8,128)} %get-tuple-element.57), channel_id=1, source_target_pairs={{0,1},{2,3},{4,5},{6,7},{8,9},{10,11},{12,13},{14,15},{16,17},{18,... | collective-permute-start | bytes 442376 | tf_op jit(solution)/shard_map/ppermute | solution.py:916
  373.9 0.8 copy-start.4
  391.2 0.6 copy-start.12

commit v2 on v1

--- a/solution.py
+++ b/solution.py
@@ -155,6 +155,7 @@
 
 
 LANE = 128
+UNROLL = dict(step=8, add=8, column=8, bring=8, one=8, two=8)
 PAD = 16
 BAND = 64
 
@@ -171,8 +172,12 @@
     return lax.broadcasted_iota(jnp.int32, (8, LANE), 1)
 
 
+def at_row(row):
+    return pl.ds(row if isinstance(row, int) else pl.multiple_of(row, 8), 8)
+
+
 def eight(index):
-    return pl.ds(pl.multiple_of(8 * index, 8), 8)
+    return at_row(8 * index)
 
 
 def from_east(tiles, lane):
@@ -217,12 +222,25 @@
     return in_e, in_w, in_n, in_s, new
 
 
+def sweep(first, end, body, depth):
+    whole = (end - first) // depth
+
+    def step(k, _):
+        for j in range(depth):
+            body(first + k * depth + j)
+        return 0
+
+    lax.fori_loop(0, whole, step, 0)
+    for i in range(first + whole * depth, end):
+        body(i)
+
+
 def tiles_at(ref, base, count, lead=()):
     return [ref[lead + (c, base, slice(None))] for c in range(count)]
 
 
 def inflows_at(h, u, v, row, count, lead, lane):
-    mid = pl.ds(pl.multiple_of(row, 8), 8)
+    mid = at_row(row)
     up, down = pl.ds(row - 1, 8), pl.ds(row + 1, 8)
     hl, vl = lead
     return inflows(
@@ -322,7 +340,7 @@
     begin = 2 * fields * level
     mine = jnp.logical_and(lane >= begin, lane < begin + 2 * fields)
 
-    def step(i, _):
+    def step(i):
         rows = eight(i)
         got_w = got_e = jnp.zeros((8, LANE), jnp.float32)
         for f in range(fields):
@@ -335,9 +353,8 @@
             got_e = jnp.where(here, pltpu.roll(tile, (2 * f - last + 2) % LANE, 1), got_e)
         west[rows, :] = jnp.where(mine, pltpu.roll(got_w, begin, 1), west[rows, :])
         east[rows, :] = jnp.where(mine, pltpu.roll(got_e, begin, 1), east[rows, :])
-        return 0
-
-    lax.fori_loop(0, west.shape[0] // 8, step, 0)
+
+    sweep(0, west.shape[0] // 8, step, UNROLL["step"])
 
 
 def pack_columns(tracers, h, u, v):
@@ -423,16 +440,15 @@
     for f, (ref, out) in enumerate(((h, h_out), (u, u_out), (v, v_out))):
         plane = fields * level + fields - 3 + f
 
-        def step(i, _):
-            here, there = eight(i), pl.ds(pl.multiple_of(8 * i, 8) + PAD, 8)
+        def step(i):
+            here, there = eight(i), at_row(8 * i + PAD)
             for c in range(count - 1):
                 out[0, c, there, :] = ref[0, here, c * LANE : (c + 1) * LANE]
             out[0, count - 1, there, 0:last] = ref[0, here, LANE * (count - 1) : cols]
             rim = rim_lanes(east[here, :], west[here, :], plane, last, lane)
             out[0, count - 1, there, last:] = rim[:, last:]
-            return 0
-
-        lax.fori_loop(0, rows // 8, step, 0)
+
+        sweep(0, rows // 8, step, UNROLL["step"])
         for c in range(count):
             part = slice(c * LANE, (c + 1) * LANE)
             a = pole[0, fields - 3 + f, :, part]
@@ -440,14 +456,13 @@
             out[0, c, PAD - 2 : PAD, :] = jnp.where(s[0] == 1, a, b)
             out[0, c, PAD + rows : PAD + rows + 2, :] = jnp.where(s[0] == 1, b, a)
 
-    def add(i, _):
+    def add(i):
         here = eight(i)
         for c in range(count):
             now = h_out[0, c, here, :]
             total[c, here, :] = jnp.where(level == 0, now, total[c, here, :] + now)
-        return 0
-
-    lax.fori_loop(0, h_out.shape[2] // 8, add, 0)
+
+    sweep(0, h_out.shape[2] // 8, add, UNROLL["add"])
 
 
 def extend_fields(scalars, h, u, v, east, west, pole, facing):
@@ -480,18 +495,17 @@
     lane = lanes()
     count, tall = h.shape[1:3]
 
-    def column(i, _):
+    def column(i):
         here = eight(i)
         for c in range(count):
             before = jnp.where(level == 0, above[c, here, :], cum[c, here, :])
             now = h[0, c, here, :]
             press[c, here, :] = before + 0.5 * now
             cum[c, here, :] = before + now
-        return 0
-
-    lax.fori_loop(0, tall // 8, column, 0)
-
-    def step(i, _):
+
+    sweep(0, tall // 8, column, UNROLL["column"])
+
+    def step(i):
         row = 8 * i
         here = eight(i)
         p = tiles_at(press, here, count)
@@ -503,9 +517,8 @@
             v_out[0, c, here, :] = v[0, c, here, :] - GRADIENT_COEF * (p_s[c] - p_n[c])
             h_out[0, c, here, :] = new[c]
             total[c, here, :] = jnp.where(level == 0, new[c], total[c, here, :] + new[c])
-        return 0
-
-    lax.fori_loop(1, tall // 8 - 1, step, 0)
+
+    sweep(1, tall // 8 - 1, step, UNROLL["step"])
 
 
 def first_substep(h, u, v, above):
@@ -596,16 +609,15 @@
 
     lane = lanes()
 
-    def step(k, _):
+    def step(k):
         l, i = k // (slab // 8 - 2), lax.rem(k, slab // 8 - 2) + 1
         here = eight(i)
         new = inflows_at(h0, u0_out, v0_out, 8 * i, count, ((l,), (l,)), lane)[4]
         for c in range(count):
             h1_out[l, c, here, :] = new[c]
             total[c, here, :] = jnp.where(l == 0, new[c], total[c, here, :] + new[c])
-        return 0
-
-    lax.fori_loop(0, levels * (slab // 8 - 2), step, 0)
+
+    sweep(0, levels * (slab // 8 - 2), step, UNROLL["step"])
 
 
 def filtered_band(scalars, pieces, above, limits, basis, slope, fields):
@@ -660,7 +672,7 @@
 
     @pl.when(part == 0)
     def _():
-        def one(i, _):
+        def one(i):
             here = eight(i)
             in_e, in_w, in_n, in_s, new = inflows_at(
                 h0, u0, v0, 8 * i + PAD - 8, count, ((0,), (0,)), lane
@@ -671,12 +683,11 @@
                 for k in range(4):
                     early[k + 1, c, here, :] = w[k]
                 early[0, c, here, :] = 1.0 - ((w[0] + w[1]) + (w[2] + w[3]))
-                first_h[c, pl.ds(pl.multiple_of(8 * i, 8) + PAD - 8, 8), :] = new[c]
-            return 0
-
-        lax.fori_loop(0, tiles + 2, one, 0)
-
-        def two(i, _):
+                first_h[c, at_row(8 * i + PAD - 8), :] = new[c]
+
+        sweep(0, tiles + 2, one, UNROLL["one"])
+
+        def two(i):
             here = eight(i)
             in_e, in_w, in_n, in_s, new = inflows_at(
                 first_h, u1, v1, 8 * i + PAD, count, ((), (0,)), lane
@@ -689,13 +700,12 @@
                 late[0, c, here, :] = 1.0 - ((w[0] + w[1]) + (w[2] + w[3]))
                 wide = min(LANE, cols - c * LANE)
                 h_out[0, here, c * LANE : c * LANE + wide] = new[c][:, 0:wide]
-            return 0
-
-        lax.fori_loop(0, tiles, two, 0)
-
-    def bring(i, _):
+
+        sweep(0, tiles, two, UNROLL["two"])
+
+    def bring(i):
         here = eight(i)
-        there = pl.ds(pl.multiple_of(8 * (i + s[4]), 8), 8)
+        there = at_row(8 * (i + s[4]))
         rim_rows = eight(i + s[3])
         e, w = east[rim_rows, :], west[rim_rows, :]
         for j in range(group):
@@ -704,9 +714,8 @@
                 t0[j, c, there, :] = tr[j, 0, here, c * LANE : (c + 1) * LANE]
             t0[j, count - 1, there, 0:last] = tr[j, 0, here, LANE * (count - 1) : cols]
             t0[j, count - 1, there, last:] = rim_lanes(e, w, plane, last, lane)[:, last:]
-        return 0
-
-    lax.fori_loop(0, tiles + 1, bring, 0)
+
+    sweep(0, tiles + 1, bring, UNROLL["bring"])
     for ends in (True, False):
 
         @pl.when(s[5] == int(ends))
@@ -717,7 +726,7 @@
                     t0[j, c, at : at + 2, :] = rim[0, part * group + j, :, c * LANE : (c + 1) * LANE]
 
     def advance(source, j, row, weights):
-        mid = tiles_at(source, pl.ds(pl.multiple_of(row, 8), 8), count, (j,))
+        mid = tiles_at(source, at_row(row), count, (j,))
         up = tiles_at(source, pl.ds(row - 1, 8), count, (j,))
         down = tiles_at(source, pl.ds(row + 1, 8), count, (j,))
         right, left = from_east(mid, lane), from_west(mid, lane)
@@ -730,17 +739,16 @@
             for c in range(count)
         ]
 
-    def one(i, _):
+    def one(i):
         weights = [tiles_at(early, eight(i), count, (k,)) for k in range(5)]
         for j in range(group):
             new = advance(t0, j, 8 * i + PAD - 8, weights)
             for c in range(count):
-                t1[j, c, pl.ds(pl.multiple_of(8 * i, 8) + PAD - 8, 8), :] = new[c]
-        return 0
-
-    lax.fori_loop(0, tiles + 2, one, 0)
-
-    def two(i, _):
+                t1[j, c, at_row(8 * i + PAD - 8), :] = new[c]
+
+    sweep(0, tiles + 2, one, UNROLL["one"])
+
+    def two(i):
         here = eight(i)
         weights = [tiles_at(late, here, count, (k,)) for k in range(5)]
         for j in range(group):
@@ -748,9 +756,8 @@
             for c in range(count):
                 wide = min(LANE, cols - c * LANE)
                 tr_out[j, 0, here, c * LANE : c * LANE + wide] = new[c][:, 0:wide]
-        return 0
-
-    lax.fori_loop(0, tiles, two, 0)
+
+    sweep(0, tiles, two, UNROLL["two"])
 
 
 def tracer_slab(scalars, tracers, slabs, offsets, east, west, rim, rows, base, group, name):
@@ -812,20 +819,19 @@
     count, slab = h.shape[1:3]
     cols = u_out.shape[2]
 
-    def column(i, _):
+    def column(i):
         here = eight(i)
         for c in range(count):
             before = jnp.where(level == 0, above[c, here, :], cum[c, here, :])
             now = h[0, c, here, :]
             press[c, here, :] = before + 0.5 * now
             cum[c, here, :] = before + now
-        return 0
-
-    lax.fori_loop(0, slab // 8, column, 0)
-
-    def step(i, _):
+
+    sweep(0, slab // 8, column, UNROLL["column"])
+
+    def step(i):
         row = 8 * i + PAD
-        mid = pl.ds(pl.multiple_of(row, 8), 8)
+        mid = at_row(row)
         p = tiles_at(press, mid, count)
         p_e, p_w = from_east(p, lane), from_west(p, lane)
         p_n, p_s = tiles_at(press, pl.ds(row - 1, 8), count), tiles_at(press, pl.ds(row + 1, 8), count)
@@ -836,9 +842,8 @@
             north = v[0, c, mid, :] - GRADIENT_COEF * (p_s[c] - p_n[c])
             u_out[0, eight(i), part] = east[:, 0:wide]
             v_out[0, eight(i), part] = north[:, 0:wide]
-        return 0
-
-    lax.fori_loop(0, rows // 8, step, 0)
+
+    sweep(0, rows // 8, step, UNROLL["step"])
 
 
 def last_winds(scalars, h, u, v, above, moves, rows, height, cols, base, name):

time: 398 us -> 199 us (0.50)
  Pallas kernels: 346 us -> 138 us
  waiting for transfers between devices: 21.3 us -> 29.9 us
    pallas_call x2, Pallas kernels: 179 us -> 61.5 us  [tracer_slab(): pl.pallas_call(functools.partial(slab_kernel, rim.shape[1], group, rows,...]
    pallas_call x1, Pallas kernels: 44.1 us -> 10.2 us  [extend_fields(): pl.pallas_call(functools.partial(extend_kernel, fields), grid_spec=pltpu....]
    pallas_call x1, Pallas kernels: 35.8 us -> 11.9 us  [first_substep(): pl.pallas_call(first_kernel, grid=(levels,), in_specs=[spec] * 3 + [flat]...]
    pallas_call x1, Pallas kernels: 32.5 us -> 16.4 us  [pack_columns(): pl.pallas_call(functools.partial(pack_kernel, count + 3, cols - LANE * hi...]
    pallas_call x2, Pallas kernels: 22.4 us -> 11.5 us  [last_winds(): pl.pallas_call(functools.partial(winds_kernel, rows, base is not None), g...]
    ppermute x9, waiting for transfers between devices: 20.4 us -> 29 us  [along(): return lax.ppermute(value, 'lon', [(i, (i + d) % n) for i in range(n)])]
    pallas_call x1, Pallas kernels: 16.4 us -> 10.8 us  [filtered_band(): pl.pallas_call(functools.partial(filter_kernel, n), grid_spec=pltpu.Prefe...]
  transfers between devices with their start and end apart: 14 -> 14, of which waited for: 4 -> 5; matrix products, arithmetic and copies ran while one was open for 1% -> 2% of each run, Pallas kernels for 76% -> 56%
where the time goes in v2:
time: 199 us; the launch traced here: 198 us
  Pallas kernels  138 us (69%)
  waiting for transfers between devices  29.9 us (15%)
  starting transfers between devices  21 us (11%)
  local copies, waits for them, and re-layouts  7.68 us (4%)
    pallas_call x2, Pallas kernels, tracer_slab(): pl.pallas_call(functools.partial(slab_kernel, rim.shape[1], group, rows,...  61.5 us
    ppermute x9, waiting for transfers between devices, along(): return lax.ppermute(value, 'lon', [(i, (i + d) % n) for i in range(n)])  29 us
    pallas_call x1, Pallas kernels, pack_columns(): pl.pallas_call(functools.partial(pack_kernel, count + 3, cols - LANE * hi...  16.4 us
    ppermute x9, starting transfers between devices, along(): return lax.ppermute(value, 'lon', [(i, (i + d) % n) for i in range(n)])  13 us
    pallas_call x1, Pallas kernels, first_substep(): pl.pallas_call(first_kernel, grid=(levels,), in_specs=[spec] * 3 + [flat]...  11.9 us
    pallas_call x2, Pallas kernels, last_winds(): pl.pallas_call(functools.partial(winds_kernel, rows, base is not None), g...  11.5 us
    pallas_call x1, Pallas kernels, filtered_band(): pl.pallas_call(functools.partial(filter_kernel, n), grid_spec=pltpu.Prefe...  10.8 us
    pallas_call x1, Pallas kernels, extend_fields(): pl.pallas_call(functools.partial(extend_kernel, fields), grid_spec=pltpu....  10.2 us
  transfers between devices with their start and end apart: 14, of which 5 were waited for; matrix products, arithmetic and copies ran while one was open for 2% of the time, Pallas kernels for 56%

profile of v2, /device:TPU:0, one launch (start us, length us, event | category | flops | bytes accessed | tf_op | source)
XLA Modules:
  0.0 198.3 jit_solution(852699415542908334)
XLA Ops:
  0.6 16.4 %pack_columns.1 = (f32[360,128]{1,0:T(8,128)}, f32[360,128]{1,0:T(8,128)}) custom-call(f32[10,4,360,360]{3,2,1,0:T(8,128)} %refs_0_.5, f32[10,4,360,360]{3,2,1,0:T(8,128)} %refs_0_.5, f32[4,360,360]{2,1,0:T(8,128)} %refs_11_.1, f32[4,360,360]{2,1,0:T(8,128)} %refs_11_.1, f32[4,360,360]{2,1,0:T(8,128)} %refs_9_.1, f32[4,360,360]{2,1,0:T(8,128)} %refs_9_.1, ...), custom_call_target="tpu_custom_call" | custom-call | flops 10000000 | bytes 19169280 | tf_op jit(solution)/shard_map/pack_columns/pallas_call | solution.py:366
  17.1 5.0 %collective-permute-start = (f32[360,128]{1,0:T(8,128)}, f32[360,128]{1,0:T(8,128)S(1)}, u32[]{:S(2)}, u32[]{:S(2)}) collective-permute-start(f32[360,128]{1,0:T(8,128)} %get-tuple-element.34), channel_id=1, source_target_pairs={{0,12},{4,0},{8,4},{12,8},{1,13},{5,1},{9,5},{13,9},{2,14},{6,2},{... | collective-permute-start | bytes 552968 | tf_op jit(solution)/shard_map/ppermute | solution.py:918
  22.1 0.0 collective-permute-start.1
  22.1 0.7 stack.49.s
  22.8 4.7 %collective-permute-done.e_top.e_bot.east.refs_6_ = f32[360,128]{1,0:T(8,128)S(1)} collective-permute-done((f32[360,128]{1,0:T(8,128)}, f32[360,128]{1,0:T(8,128)S(1)}, u32[]{:S(2)}, u32[]{:S(2)}) %collective-permute-start) | collective-permute-done | bytes 184352 | tf_op jit(solution)/shard_map/ppermute | solution.py:918
  27.5 3.6 %collective-permute-done.1.w_top.w_bot.west.refs_7_ = f32[360,128]{1,0:T(8,128)S(1)} collective-permute-done((f32[360,128]{1,0:T(8,128)}, f32[360,128]{1,0:T(8,128)S(1)}, u32[]{:S(2)}, u32[]{:S(2)}) %collective-permute-start.1) | collective-permute-done | bytes 184352 | tf_op jit(solution)/shard_map/ppermute | solution.py:918
  31.1 0.0 copy-done
  31.1 0.7 copy-done.1
  31.8 6.7 %edge_rows.1 = (f32[4,13,2,384]{3,2,1,0:T(2,128)}, f32[4,13,2,384]{3,2,1,0:T(2,128)}) custom-call(s32[6]{0:T(128)} %stack.49.s, f32[10,4,360,360]{3,2,1,0:T(8,128)} %refs_0_.5, f32[10,4,360,360]{3,2,1,0:T(8,128)} %refs_0_.5, f32[4,360,360]{2,1,0:T(8,128)} %refs_11_.1, f32[4,360,360]{2,1,0:T(8,128)} %refs_11_.1, f32[4,360,360]{2,1,0:T(8,128)} %refs_9_.1, ...), custom_call_target="tpu_custom_call" | custom-call | flops 1000000 | bytes 1996800 | tf_op jit(solution)/shard_map/edge_rows/pallas_call | solution.py:418
  38.4 0.8 collective-permute-start.2
  39.2 1.6 collective-permute-start.3
  40.8 3.1 %band_rows.1 = (f32[184,360]{1,0:T(8,128)}, f32[184,360]{1,0:T(8,128)}, f32[184,360]{1,0:T(8,128)}, f32[184,360]{1,0:T(8,128)}) custom-call(s32[6]{0:T(128)} %stack.49.s, f32[4,360,360]{2,1,0:T(8,128)} %refs_9_.1, f32[4,360,360]{2,1,0:T(8,128)} %refs_10_.1, f32[4,360,360]{2,1,0:T(8,128)} %refs_11_.1, f32[4,360,360]{2,1,0:T(8,128)} %refs_9_.1, ...), custom_call_target="tpu_custom_call" | custom-call | flops 1000000 | bytes 2119680 | tf_op jit(solution)/shard_map/band_rows/pallas_call | solution.py:284
  43.9 1.6 collective-permute-start.4
  45.5 2.2 %collective-permute-start.5 = (f32[184,360]{1,0:T(8,128)}, f32[184,360]{1,0:T(8,128)S(1)}, u32[]{:S(2)}, u32[]{:S(2)}) collective-permute-start(f32[184,360]{1,0:T(8,128)} %get-tuple-element.41), channel_id=1, source_target_pairs={{0,8},{4,12},{8,0},{12,4},{1,9},{5,13},{9,1},{13,5},{2,10},{6,14},... | collective-permute-start | bytes 794888 | tf_op jit(solution)/shard_map/ppermute | solution.py:918
  47.8 1.3 collective-permute-start.6
  49.1 12.1 %collective-permute-done.2.pole.refs_8_ = f32[4,13,2,384]{3,2,1,0:T(2,128)S(1)} collective-permute-done((f32[4,13,2,384]{3,2,1,0:T(2,128)}, f32[4,13,2,384]{3,2,1,0:T(2,128)S(1)}, u32[]{:S(2)}, u32[]{:S(2)}) %collective-permute-start.2) | collective-permute-done | bytes 159776 | tf_op jit(solution)/shard_map/ppermute | solution.py:918
  61.2 0.0 collective-permute-done.3.facing.refs_8_
  61.2 0.7 copy-done.2
  61.8 0.7 copy-done.3
  62.5 10.2 %extend_fields.1 = (f32[4,3,392,128]{3,2,1,0:T(8,128)}, f32[4,3,392,128]{3,2,1,0:T(8,128)}, f32[4,3,392,128]{3,2,1,0:T(8,128)}, f32[3,392,128]{2,1,0:T(8,128)}) custom-call(s32[6]{0:T(128)} %stack.49.s, f32[4,360,360]{2,1,0:T(8,128)} %refs_11_.1, f32[4,360,360]{2,1,0:T(8,128)} %refs_9_.1, f32[4,360,360]{2,1,0:T(8,128)} %refs_10_.1, f32[360,128]{1,0:T(8,128)} %copy-done, ...), custom_call_target="tpu_custom_call" | custom-call | flops 1000000 | bytes 16859136 | tf_op jit(solution)/shard_map/extend_fields/pallas_call | solution.py:477
  72.7 1.3 collective-permute-start.11
  74.0 0.0 collective-permute-done.4.refs_1_
  74.0 0.0 copy-start.9
  74.0 0.0 collective-permute-done.5.refs_2_
  74.1 0.0 copy-start.10
  74.1 0.0 collective-permute-done.6.refs_3_
  74.1 0.0 copy-start.11
  74.1 0.7 copy-done.9
  74.7 0.1 copy-done.10
  74.8 0.1 copy-done.11
  74.9 5.8 %spectra.1.refs_0_ = f32[184,384]{1,0:T(8,128)} custom-call(s32[6]{0:T(128)} %stack.49.s, f32[184,360]{1,0:T(8,128)} %get-tuple-element.39.refs_0_, f32[184,360]{1,0:T(8,128)} %copy-done.9, f32[184,360]{1,0:T(8,128)} %copy-done.10, f32[184,360]{1,0:T(8,128)} %copy-done.11, f32[4,360,384]{2,1,0:T(8,128)} %constant.32.clone.refs_4_.refs_5_.refs_6_.refs_7_, ...), custom_call_target="tpu_custom_call" | custom-call | flops 1220935680 | bytes 3271680 | tf_op jit(solution)/shard_map/spectra/pallas_call | solution.py:320
  80.8 0.0 collective-permute-start.9
  80.8 0.5 collective-permute-start.8
  81.2 1.6 collective-permute-start.7
  82.8 0.0 collective-permute-done.11.above
  82.8 0.8 copy-done.5
  83.6 11.9 %first_substep.1 = (f32[4,3,392,128]{3,2,1,0:T(8,128)}, f32[4,3,392,128]{3,2,1,0:T(8,128)}, f32[4,3,392,128]{3,2,1,0:T(8,128)}, f32[3,392,128]{2,1,0:T(8,128)}) custom-call(f32[4,3,392,128]{3,2,1,0:T(8,128)} %get-tuple-element.38.h.refs_8_.refs_1_, f32[4,3,392,128]{3,2,1,0:T(8,128)} %get-tuple-element.43.u.refs_9_.refs_2_, ...), custom_call_target="tpu_custom_call" | custom-call | flops 48168960 | bytes 18063360 | tf_op jit(solution)/shard_map/first_substep/pallas_call | solution.py:529
  95.5 1.3 collective-permute-start.13
  96.8 0.0 collective-permute-done.9.refs_3_
  96.8 0.0 copy-start.6
  96.8 8.6 %collective-permute-done.8.refs_2_ = f32[184,384]{1,0:T(8,128)S(1)} collective-permute-done((f32[184,384]{1,0:T(8,128)}, f32[184,384]{1,0:T(8,128)S(1)}, u32[]{:S(2)}, u32[]{:S(2)}) %collective-permute-start.8) | collective-permute-done | bytes 282656 | tf_op jit(solution)/shard_map/ppermute | solution.py:918
  105.4 0.0 collective-permute-done.7.refs_1_
  105.4 1.0 slice_add_fusion
  106.5 1.3 collective-permute-start.10
  107.8 0.0 copy-done.14
  107.8 0.9 collective-permute-done.10.refs_4_
  108.7 0.7 broadcast_in_dim.2.refs_5_
  109.4 0.0 copy-done.6
  109.4 0.0 copy-done.7
  109.4 0.0 copy-done.8
  109.4 0.0 copy-done.13
  109.4 10.8 %filtered_band.1 = (f32[4,3,96,128]{3,2,1,0:T(8,128)}, f32[4,3,96,128]{3,2,1,0:T(8,128)}, f32[4,3,96,128]{3,2,1,0:T(8,128)}, f32[4,3,96,128]{3,2,1,0:T(8,128)}, ...) custom-call(s32[6]{0:T(128)} %stack.49.s, f32[184,384]{1,0:T(8,128)} %spectra.1.refs_0_, f32[184,384]{1,0:T(8,128)} %copy-done.8, ...), custom_call_target="tpu_custom_call" | custom-call | flops 1811939328 | bytes 5898240 | tf_op jit(solution)/shard_map/filtered_band/pallas_call | solution.py:635
  120.2 2.4 %collective-permute-start.12 = (f32[3,96,128]{2,1,0:T(8,128)}, f32[3,96,128]{2,1,0:T(8,128)S(1)}, u32[]{:S(2)}, u32[]{:S(2)}) collective-permute-start(f32[3,96,128]{2,1,0:T(8,128)} %get-tuple-element.57), channel_id=1, source_target_pairs={{0,1},{2,3},{4,5},{6,7},{8,9},{10,11},{12,13},{14,15},{16,17},{18,... | collective-permute-start | bytes 442376 | tf_op jit(solution)/shard_map/ppermute | solution.py:921
  122.6 0.6 stack.53.s
  123.2 0.6 stack.48.s
  123.8 47.9 %tracers_inner.1 = (f32[10,4,360,360]{3,2,1,0:T(8,128)}, f32[4,360,360]{2,1,0:T(8,128)}) custom-call(s32[6]{0:T(128)} %stack.53.s, f32[10,4,360,360]{3,2,1,0:T(8,128)} %refs_0_.5, f32[4,3,392,128]{3,2,1,0:T(8,128)} %get-tuple-element.38.h.refs_8_.refs_1_, f32[4,3,392,128]{3,2,1,0:T(8,128)} %get-tuple-element.43.u.refs_9_.refs_2_, ...), custom_call_target="tpu_custom_call" | custom-call | flops 255744000 | bytes 34099200 | tf_op jit(solution)/shard_map/tracers_inner/pallas_call | solution.py:786
  171.7 13.6 %tracers_polar.1 = (f32[10,4,360,360]{3,2,1,0:T(8,128)}, f32[4,360,360]{2,1,0:T(8,128)}) custom-call(s32[6]{0:T(128)} %stack.48.s, f32[10,4,360,360]{3,2,1,0:T(8,128)} %refs_0_.5, f32[4,3,392,128]{3,2,1,0:T(8,128)} %get-tuple-element.38.h.refs_8_.refs_1_, ...), custom_call_target="tpu_custom_call", output_to_operand_aliasing={{0}: (10, {}), {1}: (11, {})} | custom-call | flops 55296000 | bytes 7372800 | tf_op jit(solution)/shard_map/tracers_polar/pallas_call | solution.py:786
  185.3 0.0 collective-permute-done.13.above
  185.3 0.0 copy-start.4
  185.3 0.8 copy-done.4
  186.1 7.0 %winds_inner.1 = (f32[4,360,360]{2,1,0:T(8,128)}, f32[4,360,360]{2,1,0:T(8,128)}) custom-call(s32[6]{0:T(128)} %stack.53.s, f32[4,3,392,128]{3,2,1,0:T(8,128)} %get-tuple-element.58.h, f32[4,3,392,128]{3,2,1,0:T(8,128)} %get-tuple-element.46.refs_11_.refs_4_.u, f32[4,3,392,128]{3,2,1,0:T(8,128)} %get-tuple-element.47.refs_12_.refs_5_.v, f32[3,392,128]{2,1,0:T(8,128)} %copy-done.4), custom_call_target="tpu_custom_call" | custom-call | flops 8524800 | bytes 10229760 | tf_op jit(solution)/shard_map/winds_inner/pallas_call | solution.py:864
  193.1 0.0 collective-permute-done.12.above
  193.1 0.6 copy-done.12
  193.8 4.5 %winds_polar.1 = (f32[4,360,360]{2,1,0:T(8,128)}, f32[4,360,360]{2,1,0:T(8,128)}) custom-call(s32[6]{0:T(128)} %stack.48.s, f32[4,3,96,128]{3,2,1,0:T(8,128)} %get-tuple-element.56.h, f32[4,3,96,128]{3,2,1,0:T(8,128)} %get-tuple-element.50.refs_4_.u, f32[4,3,96,128]{3,2,1,0:T(8,128)} %get-tuple-element.51.refs_5_.v, ...), custom_call_target="tpu_custom_call", output_to_operand_aliasing={{0}: (5, {}), {1}: (6, {})} | custom-call | flops 1843200 | bytes 2211840 | tf_op jit(solution)/shard_map/winds_polar/pallas_call | solution.py:864
  (13 shorter events, 0.0 us)
Async XLA Ops:
  17.1 10.4 %collective-permute-start = (f32[360,128]{1,0:T(8,128)}, f32[360,128]{1,0:T(8,128)S(1)}, u32[]{:S(2)}, u32[]{:S(2)}) collective-permute-start(f32[360,128]{1,0:T(8,128)} %get-tuple-element.34), channel_id=1, source_target_pairs={{0,12},{4,0},{8,4},{12,8},{1,13},{5,1},{9,5},{13,9},{2,14},{6,2},{... | collective-permute-start | bytes 552968 | tf_op jit(solution)/shard_map/ppermute | solution.py:918
  22.1 9.0 %collective-permute-start.1 = (f32[360,128]{1,0:T(8,128)}, f32[360,128]{1,0:T(8,128)S(1)}, u32[]{:S(2)}, u32[]{:S(2)}) collective-permute-start(f32[360,128]{1,0:T(8,128)} %get-tuple-element.35), channel_id=1, source_target_pairs={{0,4},{4,8},{8,12},{12,0},{1,5},{5,9},{9,13},{13,1},{2,6},{6,10},{... | collective-permute-start | bytes 552968 | tf_op jit(solution)/shard_map/ppermute | solution.py:918
  27.5 3.6 %copy-start = (f32[360,128]{1,0:T(8,128)}, f32[360,128]{1,0:T(8,128)S(1)}, u32[]{:S(2)}) copy-start(f32[360,128]{1,0:T(8,128)S(1)} %collective-permute-done.e_top.e_bot.east.refs_6_) | copy-start | bytes 552964
  31.1 0.7 copy-start.1
  38.4 22.7 %collective-permute-start.2 = (f32[4,13,2,384]{3,2,1,0:T(2,128)}, f32[4,13,2,384]{3,2,1,0:T(2,128)S(1)}, u32[]{:S(2)}, u32[]{:S(2)}) collective-permute-start(f32[4,13,2,384]{3,2,1,0:T(2,128)} %get-tuple-element.36), channel_id=1, source_target_pairs={{0,8},{4,12},{8,0},{12,4},{1,9},{5,13},{9,1},{13,5},{2,10},{6,14},... | collective-permute-start | bytes 479240 | tf_op jit(solution)/shard_map/ppermute | solution.py:918
  39.2 21.9 %collective-permute-start.3 = (f32[4,13,2,384]{3,2,1,0:T(2,128)}, f32[4,13,2,384]{3,2,1,0:T(2,128)S(1)}, u32[]{:S(2)}, u32[]{:S(2)}) collective-permute-start(f32[4,13,2,384]{3,2,1,0:T(2,128)} %get-tuple-element.37), channel_id=1, source_target_pairs={{0,2},{2,0},{1,3},{3,1},{4,6},{6,4},{5,7},{7,5},{8,10},{10,8},{9,1... | collective-permute-start | bytes 479240 | tf_op jit(solution)/shard_map/ppermute | solution.py:929
  43.9 30.1 %collective-permute-start.4 = (f32[184,360]{1,0:T(8,128)}, f32[184,360]{1,0:T(8,128)S(1)}, u32[]{:S(2)}, u32[]{:S(2)}) collective-permute-start(f32[184,360]{1,0:T(8,128)} %get-tuple-element.40), channel_id=1, source_target_pairs={{0,4},{4,8},{8,12},{12,0},{1,5},{5,9},{9,13},{13,1},{2,6},{6,10},{... | collective-permute-start | bytes 794888 | tf_op jit(solution)/shard_map/ppermute | solution.py:918
  45.5 28.5 %collective-permute-start.5 = (f32[184,360]{1,0:T(8,128)}, f32[184,360]{1,0:T(8,128)S(1)}, u32[]{:S(2)}, u32[]{:S(2)}) collective-permute-start(f32[184,360]{1,0:T(8,128)} %get-tuple-element.41), channel_id=1, source_target_pairs={{0,8},{4,12},{8,0},{12,4},{1,9},{5,13},{9,1},{13,5},{2,10},{6,14},... | collective-permute-start | bytes 794888 | tf_op jit(solution)/shard_map/ppermute | solution.py:918
  47.8 26.3 %collective-permute-start.6 = (f32[184,360]{1,0:T(8,128)}, f32[184,360]{1,0:T(8,128)S(1)}, u32[]{:S(2)}, u32[]{:S(2)}) collective-permute-start(f32[184,360]{1,0:T(8,128)} %get-tuple-element.42), channel_id=1, source_target_pairs={{0,12},{4,0},{8,4},{12,8},{1,13},{5,1},{9,5},{13,9},{2,14},{6,2},{... | collective-permute-start | bytes 794888 | tf_op jit(solution)/shard_map/ppermute | solution.py:918
  61.1 0.7 copy-start.2
  61.8 0.7 copy-start.3
  72.7 10.1 %collective-permute-start.11 = (f32[3,392,128]{2,1,0:T(8,128)}, f32[3,392,128]{2,1,0:T(8,128)S(1)}, u32[]{:S(2)}, u32[]{:S(2)}) collective-permute-start(f32[3,392,128]{2,1,0:T(8,128)} %get-tuple-element.45), channel_id=1, source_target_pairs={{0,1},{2,3},{4,5},{6,7},{8,9},{10,11},{12,13},{14,15},{16,17},{18,... | collective-permute-start | bytes 1806344 | tf_op jit(solution)/shard_map/ppermute | solution.py:921
  74.0 0.7 copy-start.9
  74.1 0.8 copy-start.10
  74.1 0.9 copy-start.11
  80.8 16.0 %collective-permute-start.9 = (f32[184,384]{1,0:T(8,128)}, f32[184,384]{1,0:T(8,128)S(1)}, u32[]{:S(2)}, u32[]{:S(2)}) collective-permute-start(f32[184,384]{1,0:T(8,128)} %spectra.1.refs_0_), channel_id=1, source_target_pairs={{0,12},{4,0},{8,4},{12,8},{1,13},{5,1},{9,5},{13,9},{2,14},{6,2},{... | collective-permute-start | bytes 847880 | tf_op jit(solution)/shard_map/ppermute | solution.py:918
  80.8 24.7 %collective-permute-start.8 = (f32[184,384]{1,0:T(8,128)}, f32[184,384]{1,0:T(8,128)S(1)}, u32[]{:S(2)}, u32[]{:S(2)}) collective-permute-start(f32[184,384]{1,0:T(8,128)} %spectra.1.refs_0_), channel_id=1, source_target_pairs={{0,8},{4,12},{8,0},{12,4},{1,9},{5,13},{9,1},{13,5},{2,10},{6,14},... | collective-permute-start | bytes 847880 | tf_op jit(solution)/shard_map/ppermute | solution.py:918
  81.2 24.2 %collective-permute-start.7 = (f32[184,384]{1,0:T(8,128)}, f32[184,384]{1,0:T(8,128)S(1)}, u32[]{:S(2)}, u32[]{:S(2)}) collective-permute-start(f32[184,384]{1,0:T(8,128)} %spectra.1.refs_0_), channel_id=1, source_target_pairs={{0,4},{4,8},{8,12},{12,0},{1,5},{5,9},{9,13},{13,1},{2,6},{6,10},{... | collective-permute-start | bytes 847880 | tf_op jit(solution)/shard_map/ppermute | solution.py:918
  82.8 0.8 copy-start.5
  83.6 24.2 %copy-start.14 = (s32[2,60]{1,0:T(2,128)S(1)}, s32[2,60]{1,0:T(2,128)}, u32[]{:S(2)}) copy-start(s32[2,60]{1,0:T(2,128)} %param.12) | copy-start | bytes 1444
  95.5 89.8 %collective-permute-start.13 = (f32[3,392,128]{2,1,0:T(8,128)}, f32[3,392,128]{2,1,0:T(8,128)S(1)}, u32[]{:S(2)}, u32[]{:S(2)}) collective-permute-start(f32[3,392,128]{2,1,0:T(8,128)} %get-tuple-element.59), channel_id=1, source_target_pairs={{0,1},{2,3},{4,5},{6,7},{8,9},{10,11},{12,13},{14,15},{16,17},{18,... | collective-permute-start | bytes 1806344 | tf_op jit(solution)/shard_map/ppermute | solution.py:921
  96.8 12.6 %copy-start.6 = (f32[184,384]{1,0:T(8,128)}, f32[184,384]{1,0:T(8,128)S(1)}, u32[]{:S(2)}) copy-start(f32[184,384]{1,0:T(8,128)S(1)} %collective-permute-done.9.refs_3_) | copy-start | bytes 847876
  105.4 3.9 %copy-start.7 = (f32[184,384]{1,0:T(8,128)}, f32[184,384]{1,0:T(8,128)S(1)}, u32[]{:S(2)}) copy-start(f32[184,384]{1,0:T(8,128)S(1)} %collective-permute-done.8.refs_2_) | copy-start | bytes 847876
  105.4 3.9 %copy-start.8 = (f32[184,384]{1,0:T(8,128)}, f32[184,384]{1,0:T(8,128)S(1)}, u32[]{:S(2)}) copy-start(f32[184,384]{1,0:T(8,128)S(1)} %collective-permute-done.7.refs_1_) | copy-start | bytes 847876
  106.5 2.2 %collective-permute-start.10 = (f32[64,384]{1,0:T(8,128)S(1)}, f32[64,384]{1,0:T(8,128)S(1)}, u32[]{:S(2)}, u32[]{:S(2)}) collective-permute-start(f32[64,384]{1,0:T(8,128)S(1)} %slice_add_fusion), channel_id=1, source_target_pairs={{0,1},{2,3},{4,5},{6,7},{8,9},{10,11},{12,13},{14,15},{16,17},{18,... | collective-permute-start | bytes 294920 | tf_op jit(solution)/shard_map/ppermute | solution.py:921
  108.7 0.7 copy-start.13
  120.2 72.9 %collective-permute-start.12 = (f32[3,96,128]{2,1,0:T(8,128)}, f32[3,96,128]{2,1,0:T(8,128)S(1)}, u32[]{:S(2)}, u32[]{:S(2)}) collective-permute-start(f32[3,96,128]{2,1,0:T(8,128)} %get-tuple-element.57), channel_id=1, source_target_pairs={{0,1},{2,3},{4,5},{6,7},{8,9},{10,11},{12,13},{14,15},{16,17},{18,... | collective-permute-start | bytes 442376 | tf_op jit(solution)/shard_map/ppermute | solution.py:921
  185.3 0.8 copy-start.4
  193.1 0.6 copy-start.12

commit v3 on v2

--- a/solution.py
+++ b/solution.py
@@ -155,13 +155,14 @@
 
 
 LANE = 128
-UNROLL = dict(step=8, add=8, column=8, bring=8, one=8, two=8)
+POLAR_AT, MIDDLE_AT = 2, 6
+UNROLL = dict(step=8, bring=8, coef=8, one=8, two=8)
 PAD = 16
 BAND = 64
 
 
-def cost(flops, moved):
-    return pl.CostEstimate(flops=int(flops), bytes_accessed=int(moved), transcendentals=0)
+def cost(micros):
+    return pl.CostEstimate(flops=0, bytes_accessed=int(micros * 3.3e6), transcendentals=0)
 
 
 def params(mib=56):
@@ -277,7 +278,7 @@
     def spec(d):
         return pl.BlockSpec(
             (pl.Element(1), pl.Element(BAND), pl.Element(cols)),
-            lambda i, s: (lax.rem(s[1] + d, n), s[2] * 8, 0),
+            lambda i, s: (lax.rem(s[1] + d, n), s[POLAR_AT] * 8, 0),
         )
 
     rows = 3 * POLAR + 4
@@ -290,7 +291,7 @@
             out_specs=[pl.BlockSpec((rows, cols), lambda i, s: (0, 0))] * n,
         ),
         out_shape=[jax.ShapeDtypeStruct((rows, cols), jnp.float32)] * n,
-        cost_estimate=cost(1e6, 8 * n * rows * cols),
+        cost_estimate=cost(3),
         compiler_params=params(),
         name="band_rows",
     )(scalars, *([u, v, h] * n))
@@ -326,13 +327,13 @@
             out_specs=pl.BlockSpec((rows, waves), lambda i, s: (0, 0)),
         ),
         out_shape=jax.ShapeDtypeStruct((rows, waves), jnp.float32),
-        cost_estimate=cost(12 * n * rows * cols * waves, 4 * n * cols * (rows + waves)),
+        cost_estimate=cost(6),
         compiler_params=params(),
         name="spectra",
     )(scalars, *pieces, *([basis] * n))
 
 
-def pack_kernel(fields, last, t_lo, t_hi, h_lo, h_hi, u_lo, u_hi, v_lo, v_hi, west, east):
+def pack_kernel(fields, last, s, t_lo, t_hi, h_lo, h_hi, u_lo, u_hi, v_lo, v_hi, west, east):
     level = pl.program_id(0)
     lane = lanes()
     lows = [(t_lo, (f, 0)) for f in range(fields - 3)] + [(h_lo, (0,)), (u_lo, (0,)), (v_lo, (0,))]
@@ -342,37 +343,40 @@
 
     def step(i):
         rows = eight(i)
-        got_w = got_e = jnp.zeros((8, LANE), jnp.float32)
         for f in range(fields):
-            here = lane // 2 == f
+            here = lane >= 2 * f
             ref, lead = lows[f]
             tile = ref[lead + (rows, slice(None))]
-            got_w = jnp.where(here, pltpu.roll(tile, 2 * f, 1) if f else tile, got_w)
+            got_w = jnp.where(here, pltpu.roll(tile, 2 * f, 1), got_w) if f else tile
             ref, lead = highs[f]
             tile = ref[lead + (rows, slice(None))]
-            got_e = jnp.where(here, pltpu.roll(tile, (2 * f - last + 2) % LANE, 1), got_e)
+            turned = pltpu.roll(tile, (2 * f - last + 2) % LANE, 1)
+            got_e = jnp.where(here, turned, got_e) if f else turned
         west[rows, :] = jnp.where(mine, pltpu.roll(got_w, begin, 1), west[rows, :])
         east[rows, :] = jnp.where(mine, pltpu.roll(got_e, begin, 1), east[rows, :])
 
     sweep(0, west.shape[0] // 8, step, UNROLL["step"])
 
 
-def pack_columns(tracers, h, u, v):
+def pack_columns(scalars, tracers, h, u, v):
     count, levels, rows, cols = tracers.shape
     high = (cols - 1) // LANE
-    t_spec = [pl.BlockSpec((count, 1, rows, LANE), lambda l, c=c: (0, l, 0, c)) for c in (0, high)]
-    f_spec = [pl.BlockSpec((1, rows, LANE), lambda l, c=c: (l, 0, c)) for c in (0, high)]
+    t_spec = [pl.BlockSpec((count, 1, rows, LANE), lambda l, s, c=c: (0, l, 0, c)) for c in (0, high)]
+    f_spec = [pl.BlockSpec((1, rows, LANE), lambda l, s, c=c: (l, 0, c)) for c in (0, high)]
     out = jax.ShapeDtypeStruct((rows, LANE), jnp.float32)
     return pl.pallas_call(
         functools.partial(pack_kernel, count + 3, cols - LANE * high),
-        grid=(levels,),
-        in_specs=t_spec + f_spec * 3,
-        out_specs=[pl.BlockSpec((rows, LANE), lambda l: (0, 0))] * 2,
+        grid_spec=pltpu.PrefetchScalarGridSpec(
+            num_scalar_prefetch=1,
+            grid=(levels,),
+            in_specs=t_spec + f_spec * 3,
+            out_specs=[pl.BlockSpec((rows, LANE), lambda l, s: (0, 0))] * 2,
+        ),
         out_shape=[out, out],
-        cost_estimate=cost(1e7, 8 * (count + 3) * levels * rows * LANE),
+        cost_estimate=cost(10),
         compiler_params=params(),
         name="pack_columns",
-    )(tracers, tracers, h, h, u, u, v, v)
+    )(scalars, tracers, tracers, h, h, u, u, v, v)
 
 
 def rows_kernel(fields, s, t_top, t_bot, h_top, h_bot, u_top, u_bot, v_top, v_bot,
@@ -425,135 +429,131 @@
             scratch_shapes=[pltpu.VMEM((8, width), jnp.float32)] * 2,
         ),
         out_shape=[out, out],
-        cost_estimate=cost(1e6, 100 * levels * fields * width),
+        cost_estimate=cost(7),
         compiler_params=params(),
         name="edge_rows",
     )(scalars, tracers, tracers, h, h, u, u, v, v, east, east, west, west)
 
 
-def extend_kernel(fields, s, h, u, v, east, west, pole, facing, h_out, u_out, v_out, total):
-    level = pl.program_id(0)
-    lane = lanes()
-    rows, cols = h.shape[1:]
-    count = h_out.shape[1]
-    last = cols - LANE * (count - 1)
-    for f, (ref, out) in enumerate(((h, h_out), (u, u_out), (v, v_out))):
-        plane = fields * level + fields - 3 + f
-
-        def step(i):
-            here, there = eight(i), at_row(8 * i + PAD)
-            for c in range(count - 1):
-                out[0, c, there, :] = ref[0, here, c * LANE : (c + 1) * LANE]
-            out[0, count - 1, there, 0:last] = ref[0, here, LANE * (count - 1) : cols]
-            rim = rim_lanes(east[here, :], west[here, :], plane, last, lane)
-            out[0, count - 1, there, last:] = rim[:, last:]
-
-        sweep(0, rows // 8, step, UNROLL["step"])
-        for c in range(count):
-            part = slice(c * LANE, (c + 1) * LANE)
-            a = pole[0, fields - 3 + f, :, part]
-            b = facing[0, fields - 3 + f, :, part]
-            out[0, c, PAD - 2 : PAD, :] = jnp.where(s[0] == 1, a, b)
-            out[0, c, PAD + rows : PAD + rows + 2, :] = jnp.where(s[0] == 1, b, a)
-
-    def add(i):
-        here = eight(i)
-        for c in range(count):
-            now = h_out[0, c, here, :]
-            total[c, here, :] = jnp.where(level == 0, now, total[c, here, :] + now)
-
-    sweep(0, h_out.shape[2] // 8, add, UNROLL["add"])
-
-
-def extend_fields(scalars, h, u, v, east, west, pole, facing):
-    levels, rows, cols = h.shape
-    fields = pole.shape[1]
-    count = (cols - 1) // LANE + 1
-    tall = rows + 2 * PAD
-    f_spec = pl.BlockSpec((1, rows, cols), lambda l, s: (l, 0, 0))
-    c_spec = pl.BlockSpec((rows, LANE), lambda l, s: (0, 0))
-    r_spec = pl.BlockSpec((1, fields, 2, count * LANE), lambda l, s: (l, 0, 0, 0))
-    out = jax.ShapeDtypeStruct((levels, count, tall, LANE), jnp.float32)
-    return pl.pallas_call(
-        functools.partial(extend_kernel, fields),
-        grid_spec=pltpu.PrefetchScalarGridSpec(
-            num_scalar_prefetch=1,
-            grid=(levels,),
-            in_specs=[f_spec] * 3 + [c_spec] * 2 + [r_spec] * 2,
-            out_specs=[pl.BlockSpec((1, count, tall, LANE), lambda l, s: (l, 0, 0, 0))] * 3
-            + [pl.BlockSpec((count, tall, LANE), lambda l, s: (0, 0, 0))],
-        ),
-        out_shape=[out] * 3 + [jax.ShapeDtypeStruct((count, tall, LANE), jnp.float32)],
-        cost_estimate=cost(1e6, 28 * levels * tall * count * LANE),
-        compiler_params=params(),
-        name="extend_fields",
-    )(scalars, h, u, v, east, west, pole, facing)
-
-
-def first_kernel(h, u, v, above, u_out, v_out, h_out, total, cum, press):
-    level = pl.program_id(0)
-    lane = lanes()
-    count, tall = h.shape[1:3]
-
-    def column(i):
+def bring_rows(plane, source, target, here, there, rim, count, last):
+    (ref, lead), (out, at) = source, target
+    for c in range(count - 1):
+        out[at + (c, there, slice(None))] = ref[lead + (here, slice(c * LANE, (c + 1) * LANE))]
+    out[at + (count - 1, there, slice(0, last))] = ref[lead + (here, slice(LANE * (count - 1), None))]
+    out[at + (count - 1, there, slice(last, None))] = rim(plane)[:, last:]
+
+
+def pressure_rows(level, above, cum, press, h, count, tall):
+    def body(i):
         here = eight(i)
         for c in range(count):
             before = jnp.where(level == 0, above[c, here, :], cum[c, here, :])
-            now = h[0, c, here, :]
+            now = h[c, here, :]
             press[c, here, :] = before + 0.5 * now
             cum[c, here, :] = before + now
 
-    sweep(0, tall // 8, column, UNROLL["column"])
-
-    def step(i):
-        row = 8 * i
-        here = eight(i)
-        p = tiles_at(press, here, count)
-        p_e, p_w = from_east(p, lane), from_west(p, lane)
-        p_n, p_s = tiles_at(press, pl.ds(row - 1, 8), count), tiles_at(press, pl.ds(row + 1, 8), count)
-        new = inflows_at(h, u, v, row, count, ((0,), (0,)), lane)[4]
-        for c in range(count):
-            u_out[0, c, here, :] = u[0, c, here, :] - GRADIENT_COEF * (p_e[c] - p_w[c])
-            v_out[0, c, here, :] = v[0, c, here, :] - GRADIENT_COEF * (p_s[c] - p_n[c])
-            h_out[0, c, here, :] = new[c]
-            total[c, here, :] = jnp.where(level == 0, new[c], total[c, here, :] + new[c])
-
-    sweep(1, tall // 8 - 1, step, UNROLL["step"])
-
-
-def first_substep(h, u, v, above):
-    levels, count, tall, _ = h.shape
-    spec = pl.BlockSpec((1, count, tall, LANE), lambda l: (l, 0, 0, 0))
-    flat = pl.BlockSpec((count, tall, LANE), lambda l: (0, 0, 0))
-    out = jax.ShapeDtypeStruct(h.shape, jnp.float32)
+    sweep(0, tall // 8, body, 8)
+
+
+def gradient(press, row, count, lane):
+    p = tiles_at(press, at_row(row), count)
+    p_e, p_w = from_east(p, lane), from_west(p, lane)
+    p_n, p_s = tiles_at(press, pl.ds(row - 1, 8), count), tiles_at(press, pl.ds(row + 1, 8), count)
+    zonal = [GRADIENT_COEF * (p_e[c] - p_w[c]) for c in range(count)]
+    return zonal, [GRADIENT_COEF * (p_s[c] - p_n[c]) for c in range(count)]
+
+
+def column_kernel(fields, s, h, east, west, facing, total):
+    lane = lanes()
+    levels, rows, cols = h.shape
+    count = total.shape[0]
+    last = cols - LANE * (count - 1)
+
+    def body(i):
+        here, there = eight(i), at_row(8 * i + PAD)
+        e, w = east[here, :], west[here, :]
+        for c in range(count - 1):
+            total[c, there, :] = sum(h[l, here, c * LANE : (c + 1) * LANE] for l in range(levels))
+        total[count - 1, there, 0:last] = sum(h[l, here, LANE * (count - 1) :] for l in range(levels))
+        rim = sum(rim_lanes(e, w, fields * l + fields - 3, last, lane)[:, last:] for l in range(levels))
+        total[count - 1, there, last:] = rim
+
+    sweep(0, rows // 8, body, 5)
+    for c in range(count):
+        part = slice(c * LANE, (c + 1) * LANE)
+        edge = sum(facing[l, fields - 3, :, part] for l in range(levels))
+        total[c, PAD - 2 : PAD, :] = edge
+        total[c, PAD + rows : PAD + rows + 2, :] = edge
+
+
+def column_sum(scalars, h, east, west, facing):
+    _, rows, cols = h.shape
+    count, tall = (cols - 1) // LANE + 1, rows + 2 * PAD
     return pl.pallas_call(
-        first_kernel,
-        grid=(levels,),
-        in_specs=[spec] * 3 + [flat],
-        out_specs=[spec] * 3 + [flat],
-        out_shape=[out] * 3 + [jax.ShapeDtypeStruct((count, tall, LANE), jnp.float32)],
-        scratch_shapes=[pltpu.VMEM((count, tall, LANE), jnp.float32)] * 2,
-        cost_estimate=cost(80 * h.size, 30 * h.size),
+        functools.partial(column_kernel, facing.shape[1]),
+        grid_spec=pltpu.PrefetchScalarGridSpec(
+            num_scalar_prefetch=1,
+            grid=(1,),
+            in_specs=[pl.BlockSpec(x.shape, lambda i, s, k=x.ndim: (0,) * k) for x in (h, east, west, facing)],
+            out_specs=pl.BlockSpec((count, tall, LANE), lambda i, s: (0, 0, 0)),
+        ),
+        out_shape=jax.ShapeDtypeStruct((count, tall, LANE), jnp.float32),
+        cost_estimate=cost(4),
         compiler_params=params(),
-        name="first_substep",
-    )(h, u, v, above)
+        name="column_sum",
+    )(scalars, h, east, west, facing)
 
 
 def filter_kernel(n, s, *refs):
     pieces = refs[:n]
-    above, limits, basis, slope, h0, u0, v0, u1, v1 = refs[n : n + 9]
-    u0_out, v0_out, u1_out, v1_out, h1_out, total = refs[n + 9 : n + 15]
-    held, lhs, rhs = refs[n + 15 :]
-    levels, count, slab = u0.shape[:3]
+    above, limits, basis, slope, column, h, u, v, east, west, pole = refs[n : n + 11]
+    h0_out, u0_out, v0_out, u1_out, v1_out, h1_out, total = refs[n + 11 : n + 18]
+    held, lhs, rhs, cum, press = refs[n + 18 :]
+    levels, count, slab = u0_out.shape[:3]
+    cols = h.shape[2]
+    last = cols - LANE * (count - 1)
+    fields = pole.shape[1]
+    lane = lanes()
+
+    for l in range(levels):
+
+        def bring(i):
+            here, there = eight(i), at_row(8 * (i + s[POLAR_AT + 2]))
+            rim_at = eight(i + s[POLAR_AT + 1])
+            e, w = east[rim_at, :], west[rim_at, :]
+            for f, (ref, out) in enumerate(((h, h0_out), (u, u0_out), (v, v0_out))):
+                bring_rows(
+                    fields * l + fields - 3 + f, (ref, (l,)), (out, (l,)), here, there,
+                    lambda p: rim_lanes(e, w, p, last, lane), count, last,
+                )
+
+        sweep(0, BAND // 8 + 1, bring, 9)
+        for ends in (True, False):
+
+            @pl.when(s[0] == int(not ends))
+            def _():
+                at = PAD + BAND if ends else PAD - 2
+                for c in range(count):
+                    h0_out[l, c, at : at + 2, :] = pole[l, fields - 3, :, c * LANE : (c + 1) * LANE]
+
+        pressure_rows(jnp.int32(l), column, cum, press, h0_out.at[l], count, slab)
+
+        def later(i):
+            row = 8 * i
+            zonal, merid = gradient(press, row, count, lane)
+            for c in range(count):
+                u1_out[l, c, at_row(row), :] = u0_out[l, c, at_row(row), :] - zonal[c]
+                v1_out[l, c, at_row(row), :] = v0_out[l, c, at_row(row), :] - merid[c]
+
+        sweep(1, slab // 8 - 1, later, 5)
+
     waves = basis.shape[1]
     for d in range(n):
         held[lax.rem(s[1] + n - d, n)] = pieces[d][...]
-    for raw, out in ((u0, u0_out), (v0, v0_out), (u1, u1_out), (v1, v1_out)):
-        out[...] = raw[...]
     half = waves // 2
     wave = lax.broadcasted_iota(jnp.int32, (POLAR, waves), 1)
     wave = jnp.where(wave < half, wave, wave - half)
-    scale = jnp.where(wave == 0, 1.0, 2.0) / (n * s[3]).astype(jnp.float32)
+    scale = jnp.where(wave == 0, 1.0, 2.0) / (n * cols)
     keep = jnp.where(wave <= limits[0:POLAR, 0:1], scale, 0.0)
     turn = jnp.where(lax.rem(wave[0:2], 2) == 0, 1.0, -1.0)
     one = turn[0:1]
@@ -607,12 +607,10 @@
 
             lax.fori_loop(0, levels, level_step, above[0 : POLAR + 1, :])
 
-    lane = lanes()
-
     def step(k):
         l, i = k // (slab // 8 - 2), lax.rem(k, slab // 8 - 2) + 1
         here = eight(i)
-        new = inflows_at(h0, u0_out, v0_out, 8 * i, count, ((l,), (l,)), lane)[4]
+        new = inflows_at(h0_out, u0_out, v0_out, 8 * i, count, ((l,), (l,)), lane)[4]
         for c in range(count):
             h1_out[l, c, here, :] = new[c]
             total[c, here, :] = jnp.where(l == 0, new[c], total[c, here, :] + new[c])
@@ -620,16 +618,15 @@
     sweep(0, levels * (slab // 8 - 2), step, UNROLL["step"])
 
 
-def filtered_band(scalars, pieces, above, limits, basis, slope, fields):
+def filtered_band(scalars, pieces, above, limits, basis, slope, column, h, u, v, east, west, pole):
     n = len(pieces)
     rows, waves = pieces[0].shape
     width = basis.shape[2]
-    levels, count = fields[0].shape[:2]
+    levels, height, cols = h.shape
+    count = column.shape[0]
     slab = BAND + 2 * PAD
-    window = pl.BlockSpec(
-        (pl.Element(levels), pl.Element(count), pl.Element(slab), pl.Element(LANE)),
-        lambda i, s: (0, 0, s[2] * 8, 0),
-    )
+    E = pl.Element
+    raw = pl.BlockSpec((E(levels), E(BAND + 8), E(cols)), lambda i, s: (0, s[POLAR_AT + 1] * 8, 0))
     out = jax.ShapeDtypeStruct((levels, count, slab, LANE), jnp.float32)
     whole = pl.BlockSpec((levels, count, slab, LANE), lambda i, s: (0, 0, 0, 0))
     return pl.pallas_call(
@@ -643,87 +640,128 @@
                 pl.BlockSpec(limits.shape, lambda i, s: (0, 0)),
                 pl.BlockSpec((1, waves, width), lambda i, s: (s[1], 0, 0)),
                 pl.BlockSpec((1, waves, width), lambda i, s: (s[1], 0, 0)),
+                pl.BlockSpec((E(count), E(slab), E(LANE)), lambda i, s: (0, s[POLAR_AT] * 8, 0)),
             ]
-            + [window] * 5,
-            out_specs=[whole] * 5 + [pl.BlockSpec((count, slab, LANE), lambda i, s: (0, 0, 0))],
+            + [raw] * 3
+            + [pl.BlockSpec((height, LANE), lambda i, s: (0, 0))] * 2
+            + [pl.BlockSpec(pole.shape, lambda i, s: (0, 0, 0, 0))],
+            out_specs=[whole] * 6 + [pl.BlockSpec((count, slab, LANE), lambda i, s: (0, 0, 0))],
             scratch_shapes=[
                 pltpu.VMEM((n, rows, waves), jnp.float32),
                 pltpu.VMEM((3 * POLAR + 12, waves), jnp.float32),
                 pltpu.VMEM((BAND, waves), jnp.float32),
-            ],
+            ]
+            + [pltpu.VMEM((count, slab, LANE), jnp.float32)] * 2,
         ),
-        out_shape=[out] * 5 + [jax.ShapeDtypeStruct((count, slab, LANE), jnp.float32)],
-        cost_estimate=cost(12 * levels * 256 * waves * width, 40 * levels * count * slab * LANE),
+        out_shape=[out] * 6 + [jax.ShapeDtypeStruct((count, slab, LANE), jnp.float32)],
+        cost_estimate=cost(12),
         compiler_params=params(),
         name="filtered_band",
-    )(scalars, *pieces, above, limits, basis, slope, *fields)
-
-
-def slab_kernel(fields, group, rows, has_base, s, *refs):
-    (tr, h0, u0, v0, u1, v1, east, west, rim) = refs[:9]
-    refs = refs[11:] if has_base else refs[9:]
-    tr_out, h_out, early, late, first_h, t0, t1 = refs
+    )(scalars, *pieces, above, limits, basis, slope, column, h, u, v, east, west, pole)
+
+
+def slab_kernel(fields, group, rows, place, inner, s, *refs):
+    if inner:
+        tr, h, u, v, above, east, west, rim = refs[:8]
+        tr_out, h_out, h1, u1, v1, total = refs[8:14]
+        early, late, t0, t1, h0, u0, v0, cum, press = refs[14:]
+        lead = ((), ())
+        lead_one = (0,)
+    else:
+        tr, h0, u0, v0, u1, v1, east, west, rim = refs[:9]
+        tr_out, h_out = refs[11:13]
+        early, late, t0, t1, h1 = refs[13:]
+        lead = ((0,), (0,))
+        lead_one = ()
     level, part = pl.program_id(0), pl.program_id(1)
     lane = lanes()
-    count = h0.shape[1]
+    count = early.shape[1]
     cols = h_out.shape[2]
     last = cols - LANE * (count - 1)
     tiles = rows // 8
 
+    def window(i):
+        rim_at = eight(i + s[place + 1])
+        e, w = east[rim_at, :], west[rim_at, :]
+        return eight(i), at_row(8 * (i + s[place + 2])), lambda p: rim_lanes(e, w, p, last, lane)
+
+    def rims(store):
+        for ends in (True, False):
+
+            @pl.when(s[place + 3] == int(ends))
+            def _():
+                at = PAD + rows if ends else PAD - 2
+                for c in range(count):
+                    store(c, slice(at, at + 2), slice(c * LANE, (c + 1) * LANE))
+
+    def weights_from(target, here, flows, new):
+        for c in range(count):
+            inv = 1.0 / new[c]
+            w = [x[c] * inv for x in flows]
+            for k in range(4):
+                target[k + 1, c, here, :] = w[k]
+            target[0, c, here, :] = 1.0 - ((w[0] + w[1]) + (w[2] + w[3]))
+
     @pl.when(part == 0)
     def _():
+        if inner:
+
+            def bring(i):
+                here, there, rim_of = window(i)
+                for f, (ref, out) in enumerate(((h, h0), (u, u0), (v, v0))):
+                    bring_rows(
+                        fields * level + fields - 3 + f, (ref, (0,)), (out, ()), here, there, rim_of, count, last
+                    )
+
+            sweep(0, tiles + 1, bring, UNROLL["bring"])
+
+            def store(c, at, part):
+                for f, out in enumerate((h0, u0, v0)):
+                    out[c, at, :] = rim[0, fields - 3 + f, :, part]
+
+            rims(store)
+            pressure_rows(level, above, cum, press, h0, count, rows + 2 * PAD)
+
         def one(i):
-            here = eight(i)
-            in_e, in_w, in_n, in_s, new = inflows_at(
-                h0, u0, v0, 8 * i + PAD - 8, count, ((0,), (0,)), lane
-            )
+            row = 8 * i + PAD - 8
+            there = at_row(row)
+            *flows, new = inflows_at(h0, u0, v0, row, count, lead, lane)
+            weights_from(early, eight(i), flows, new)
             for c in range(count):
-                inv = 1.0 / new[c]
-                w = [x[c] * inv for x in (in_e, in_w, in_n, in_s)]
-                for k in range(4):
-                    early[k + 1, c, here, :] = w[k]
-                early[0, c, here, :] = 1.0 - ((w[0] + w[1]) + (w[2] + w[3]))
-                first_h[c, at_row(8 * i + PAD - 8), :] = new[c]
-
-        sweep(0, tiles + 2, one, UNROLL["one"])
+                h1[lead_one + (c, there, slice(None))] = new[c]
+            if inner:
+                zonal, merid = gradient(press, row, count, lane)
+                for c in range(count):
+                    total[c, there, :] = jnp.where(level == 0, new[c], total[c, there, :] + new[c])
+                    u1[0, c, there, :] = u0[c, there, :] - zonal[c]
+                    v1[0, c, there, :] = v0[c, there, :] - merid[c]
+
+        sweep(0, tiles + 2, one, UNROLL["coef"])
 
         def two(i):
             here = eight(i)
-            in_e, in_w, in_n, in_s, new = inflows_at(
-                first_h, u1, v1, 8 * i + PAD, count, ((), (0,)), lane
-            )
+            *flows, new = inflows_at(h1, u1, v1, 8 * i + PAD, count, (lead_one, (0,)), lane)
+            weights_from(late, here, flows, new)
             for c in range(count):
-                inv = 1.0 / new[c]
-                w = [x[c] * inv for x in (in_e, in_w, in_n, in_s)]
-                for k in range(4):
-                    late[k + 1, c, here, :] = w[k]
-                late[0, c, here, :] = 1.0 - ((w[0] + w[1]) + (w[2] + w[3]))
                 wide = min(LANE, cols - c * LANE)
                 h_out[0, here, c * LANE : c * LANE + wide] = new[c][:, 0:wide]
 
-        sweep(0, tiles, two, UNROLL["two"])
+        sweep(0, tiles, two, UNROLL["coef"])
 
     def bring(i):
-        here = eight(i)
-        there = at_row(8 * (i + s[4]))
-        rim_rows = eight(i + s[3])
-        e, w = east[rim_rows, :], west[rim_rows, :]
+        here, there, rim_of = window(i)
         for j in range(group):
-            plane = fields * level + part * group + j
-            for c in range(count - 1):
-                t0[j, c, there, :] = tr[j, 0, here, c * LANE : (c + 1) * LANE]
-            t0[j, count - 1, there, 0:last] = tr[j, 0, here, LANE * (count - 1) : cols]
-            t0[j, count - 1, there, last:] = rim_lanes(e, w, plane, last, lane)[:, last:]
+            bring_rows(
+                fields * level + part * group + j, (tr, (j, 0)), (t0, (j,)), here, there, rim_of, count, last
+            )
 
     sweep(0, tiles + 1, bring, UNROLL["bring"])
-    for ends in (True, False):
-
-        @pl.when(s[5] == int(ends))
-        def _():
-            at = PAD + rows if ends else PAD - 2
-            for j in range(group):
-                for c in range(count):
-                    t0[j, c, at : at + 2, :] = rim[0, part * group + j, :, c * LANE : (c + 1) * LANE]
+
+    def store(c, at, lanes_of):
+        for j in range(group):
+            t0[j, c, at, :] = rim[0, part * group + j, :, lanes_of]
+
+    rims(store)
 
     def advance(source, j, row, weights):
         mid = tiles_at(source, at_row(row), count, (j,))
@@ -760,53 +798,65 @@
     sweep(0, tiles, two, UNROLL["two"])
 
 
-def tracer_slab(scalars, tracers, slabs, offsets, east, west, rim, rows, base, group, name):
+def tracer_slab(scalars, place, rows, group, tracers, fields, east, west, rim, base, micros, name):
     count, levels, height, cols = tracers.shape
-    tiles = slabs[0].shape[1]
+    tiles = (cols - 1) // LANE + 1
     slab = rows + 2 * PAD
+    inner = base is None
     E = pl.Element
-
-    def spec(moves):
-        return pl.BlockSpec(
-            (E(1), E(tiles), E(slab), E(LANE)), lambda l, g, s: (l, 0, s[2] * 8 if moves else 0, 0)
+    slabs = pl.BlockSpec((1, tiles, slab, LANE), lambda l, g, s: (l, 0, 0, 0))
+    flat = pl.BlockSpec((tiles, slab, LANE), lambda l, g, s: (0, 0, 0))
+    in_specs = [
+        pl.BlockSpec(
+            (E(group), E(1), E(rows + 8), E(cols)), lambda l, g, s: (g * group, l, s[place + 1] * 8, 0)
         )
-
-    in_specs = [
-        pl.BlockSpec((E(group), E(1), E(rows + 8), E(cols)), lambda l, g, s: (g * group, l, s[3] * 8, 0))
     ]
-    in_specs += [spec(m) for m in offsets]
+    if inner:
+        in_specs += [pl.BlockSpec((E(1), E(rows + 8), E(cols)), lambda l, g, s: (l, s[place + 1] * 8, 0))] * 3
+        in_specs += [pl.BlockSpec((E(tiles), E(slab), E(LANE)), lambda l, g, s: (0, s[place] * 8, 0))]
+    else:
+        in_specs += [slabs] * 5
     in_specs += [pl.BlockSpec((height, LANE), lambda l, g, s: (0, 0))] * 2
     in_specs += [pl.BlockSpec((1,) + rim.shape[1:], lambda l, g, s: (l, 0, 0, 0))]
-    operands = [tracers, *slabs, east, west, rim]
+    operands = [tracers, *fields, east, west, rim]
+    out_specs = [
+        pl.BlockSpec((E(group), E(1), E(rows), E(cols)), lambda l, g, s: (g * group, l, s[place] * 8, 0)),
+        pl.BlockSpec((E(1), E(rows), E(cols)), lambda l, g, s: (l, s[place] * 8, 0)),
+    ]
+    out_shape = [
+        jax.ShapeDtypeStruct(tracers.shape, jnp.float32),
+        jax.ShapeDtypeStruct((levels, height, cols), jnp.float32),
+    ]
+    scratch = [
+        pltpu.VMEM((5, tiles, rows + 16, LANE), jnp.float32),
+        pltpu.VMEM((5, tiles, rows, LANE), jnp.float32),
+        pltpu.VMEM((group, tiles, slab, LANE), jnp.float32),
+        pltpu.VMEM((group, tiles, slab, LANE), jnp.float32),
+    ]
+    plane = pltpu.VMEM((tiles, slab, LANE), jnp.float32)
     aliases = {}
-    if base is not None:
+    if inner:
+        out_specs += [slabs] * 3 + [flat]
+        out_shape += [jax.ShapeDtypeStruct((levels, tiles, slab, LANE), jnp.float32)] * 3
+        out_shape += [jax.ShapeDtypeStruct((tiles, slab, LANE), jnp.float32)]
+        scratch += [plane] * 5
+    else:
         in_specs += [pl.BlockSpec(memory_space=pl.ANY)] * 2
         operands += list(base)
         aliases = {len(operands) - 1: 0, len(operands): 1}
+        scratch += [plane]
     return pl.pallas_call(
-        functools.partial(slab_kernel, rim.shape[1], group, rows, base is not None),
+        functools.partial(slab_kernel, rim.shape[1], group, rows, place, inner),
         grid_spec=pltpu.PrefetchScalarGridSpec(
             num_scalar_prefetch=1,
             grid=(levels, count // group),
             in_specs=in_specs,
-            out_specs=[
-                pl.BlockSpec((E(group), E(1), E(rows), E(cols)), lambda l, g, s: (g * group, l, s[2] * 8, 0)),
-                pl.BlockSpec((E(1), E(rows), E(cols)), lambda l, g, s: (l, s[2] * 8, 0)),
-            ],
-            scratch_shapes=[
-                pltpu.VMEM((5, tiles, rows + 16, LANE), jnp.float32),
-                pltpu.VMEM((5, tiles, rows, LANE), jnp.float32),
-                pltpu.VMEM((tiles, slab, LANE), jnp.float32),
-                pltpu.VMEM((group, tiles, slab, LANE), jnp.float32),
-                pltpu.VMEM((group, tiles, slab, LANE), jnp.float32),
-            ],
+            out_specs=out_specs,
+            scratch_shapes=scratch,
         ),
-        out_shape=[
-            jax.ShapeDtypeStruct(tracers.shape, jnp.float32),
-            jax.ShapeDtypeStruct((levels, height, cols), jnp.float32),
-        ],
+        out_shape=out_shape,
         input_output_aliases=aliases,
-        cost_estimate=cost(60 * count * levels * rows * cols, 8 * count * levels * rows * cols),
+        cost_estimate=cost(micros),
         compiler_params=params(),
         name=name,
     )(scalars, *operands)
@@ -814,47 +864,29 @@
 
 def winds_kernel(rows, has_base, s, h, u, v, above, *refs):
     u_out, v_out, cum, press = refs[2:] if has_base else refs
-    level = pl.program_id(0)
     lane = lanes()
     count, slab = h.shape[1:3]
     cols = u_out.shape[2]
-
-    def column(i):
-        here = eight(i)
-        for c in range(count):
-            before = jnp.where(level == 0, above[c, here, :], cum[c, here, :])
-            now = h[0, c, here, :]
-            press[c, here, :] = before + 0.5 * now
-            cum[c, here, :] = before + now
-
-    sweep(0, slab // 8, column, UNROLL["column"])
+    pressure_rows(pl.program_id(0), above, cum, press, h.at[0], count, slab)
 
     def step(i):
         row = 8 * i + PAD
-        mid = at_row(row)
-        p = tiles_at(press, mid, count)
-        p_e, p_w = from_east(p, lane), from_west(p, lane)
-        p_n, p_s = tiles_at(press, pl.ds(row - 1, 8), count), tiles_at(press, pl.ds(row + 1, 8), count)
+        zonal, merid = gradient(press, row, count, lane)
         for c in range(count):
             wide = min(LANE, cols - c * LANE)
             part = slice(c * LANE, c * LANE + wide)
-            east = u[0, c, mid, :] - GRADIENT_COEF * (p_e[c] - p_w[c])
-            north = v[0, c, mid, :] - GRADIENT_COEF * (p_s[c] - p_n[c])
-            u_out[0, eight(i), part] = east[:, 0:wide]
-            v_out[0, eight(i), part] = north[:, 0:wide]
+            u_out[0, eight(i), part] = (u[0, c, at_row(row), :] - zonal[c])[:, 0:wide]
+            v_out[0, eight(i), part] = (v[0, c, at_row(row), :] - merid[c])[:, 0:wide]
 
     sweep(0, rows // 8, step, UNROLL["step"])
 
 
-def last_winds(scalars, h, u, v, above, moves, rows, height, cols, base, name):
-    levels, tiles = h.shape[:2]
-    slab = rows + 2 * PAD
+def last_winds(scalars, place, rows, h, u, v, above, height, cols, base, micros, name):
+    levels, tiles, slab = h.shape[:3]
     E = pl.Element
-    spec = pl.BlockSpec(
-        (E(1), E(tiles), E(slab), E(LANE)), lambda l, s: (l, 0, s[2] * 8 if moves else 0, 0)
-    )
-    flat = pl.BlockSpec((E(tiles), E(slab), E(LANE)), lambda l, s: (0, s[2] * 8 if moves else 0, 0))
-    out_spec = pl.BlockSpec((E(1), E(rows), E(cols)), lambda l, s: (l, s[2] * 8, 0))
+    spec = pl.BlockSpec((1, tiles, slab, LANE), lambda l, s: (l, 0, 0, 0))
+    flat = pl.BlockSpec((tiles, slab, LANE), lambda l, s: (0, 0, 0))
+    out_spec = pl.BlockSpec((E(1), E(rows), E(cols)), lambda l, s: (l, s[place] * 8, 0))
     out = jax.ShapeDtypeStruct((levels, height, cols), jnp.float32)
     in_specs, operands, aliases = [spec] * 3 + [flat], [h, u, v, above], {}
     if base is not None:
@@ -872,7 +904,7 @@
         ),
         out_shape=[out, out],
         input_output_aliases=aliases,
-        cost_estimate=cost(20 * levels * rows * cols, 24 * levels * rows * cols),
+        cost_estimate=cost(micros),
         compiler_params=params(),
         name=name,
     )(scalars, *operands)
@@ -899,20 +931,19 @@
     count, levels, rows, cols = tracers.shape
     n = lax.axis_size("lon")
     me = lax.axis_index("lon").astype(jnp.int32)
-    north = (lax.axis_index("lat") == 0).astype(jnp.int32)
+    is_north = lax.axis_index("lat") == 0
     inner = rows - BAND
 
-    def pick(a, b):
-        return jnp.where(north == 1, a, b).astype(jnp.int32)
-
-    bandwise = jnp.stack([north, me, pick(0, inner // 8), jnp.int32(cols), jnp.int32(0), jnp.int32(0)])
-    polar = jnp.stack(
-        [north, me, pick(0, inner // 8), pick(0, inner // 8 - 1), pick(PAD // 8, PAD // 8 - 1), 1 - north]
-    )
-    middle = jnp.stack(
-        [north, me, pick(BAND // 8, 0), pick(BAND // 8 - 1, 0), pick(PAD // 8 - 1, PAD // 8), north]
-    )
+    band_at = rows // 8 - BAND // 8
+    scalars = jnp.where(
+        is_north,
+        jnp.array([1, 0, 0, 0, PAD // 8, 0, BAND // 8, BAND // 8 - 1, PAD // 8 - 1, 1], jnp.int32),
+        jnp.array([0, 0, band_at, band_at - 1, PAD // 8 - 1, 1, 0, 0, PAD // 8, 0], jnp.int32),
+    )
+    scalars = scalars + jnp.where(jnp.arange(10) == 1, me, 0)
     forward, inverse, slope = bases(n, cols)
+    limits = jnp.where(is_north, cutoff[0], cutoff[1])
+    limits = jnp.broadcast_to(jnp.pad(limits, (0, BAND - POLAR))[:, None], (BAND, LANE))
 
     def along(value, d):
         return lax.ppermute(value, "lon", [(i, (i + d) % n) for i in range(n)])
@@ -920,36 +951,41 @@
     def to_lower(value):
         return lax.ppermute(value, "lev", [(0, 1)])
 
-    sent = band_rows(bandwise, zonal, meridional, thickness, n)
+    sent = band_rows(scalars, zonal, meridional, thickness, n)
+    scalars, sent = lax.optimization_barrier((scalars, sent))
     pieces = [sent[0]] + [along(sent[d], d) for d in range(1, n)]
-    west_cols, east_cols = pack_columns(tracers, thickness, zonal, meridional)
-    east, west = along(west_cols, n - 1), along(east_cols, 1)
-    pole, facing = edge_rows(bandwise, tracers, thickness, zonal, meridional, east, west)
+    packed = pack_columns(scalars, tracers, thickness, zonal, meridional)
+    scalars, packed = lax.optimization_barrier((scalars, packed))
+    east, west = along(packed[0], n - 1), along(packed[1], 1)
+
+    own = spectra(scalars, pieces, forward)
+    scalars, own = lax.optimization_barrier((scalars, own))
+    pieces = [own] + [along(own, d) for d in range(1, n)]
+
+    pole, facing = edge_rows(scalars, tracers, thickness, zonal, meridional, east, west)
+    facing = lax.ppermute(facing, "lat", [(0, 1), (1, 0)])
     pole = along(pole, n // 2)
-    facing = lax.ppermute(facing, "lat", [(0, 1), (1, 0)])
-
-    own = spectra(bandwise, pieces, forward)
-    pieces = [own] + [along(own, d) for d in range(1, n)]
+    column = column_sum(scalars, thickness, east, west, facing)
+    column = to_lower(column)
+    tr, h2, h1, u1, v1, total = tracer_slab(
+        scalars, MIDDLE_AT, inner, 5, tracers, (thickness, zonal, meridional, column), east, west, facing, None,
+        50, "tracers_inner",
+    )
+    scalars, total, pieces = lax.optimization_barrier((scalars, total, pieces))
+    total = to_lower(total)
     above_band = to_lower(sum(p[2 * POLAR :] for p in pieces))
-
-    h0, u0, v0, column = extend_fields(bandwise, thickness, zonal, meridional, east, west, pole, facing)
-    u1, v1, h1, column = first_substep(h0, u0, v0, to_lower(column))
+    h0, u0, v0, u1b, v1b, h1b, band_total = filtered_band(
+        scalars, pieces, above_band, limits, inverse, slope, column, thickness, zonal, meridional, east, west, pole
+    )
+    band_total = to_lower(band_total)
+    winds = last_winds(scalars, MIDDLE_AT, inner, h1, u1, v1, total, rows, cols, None, 7, "winds_inner")
     tr, h2 = tracer_slab(
-        middle, tracers, (h0, u0, v0, u1, v1), (True,) * 5, east, west, facing, inner, None, 5, "tracers_inner"
-    )
-    winds = last_winds(middle, h1, u1, v1, to_lower(column), True, inner, rows, cols, None, "winds_inner")
-
-    limits = jnp.where(north == 1, cutoff[0], cutoff[1])
-    limits = jnp.broadcast_to(jnp.pad(limits, (0, BAND - POLAR))[:, None], (BAND, LANE))
-    u0b, v0b, u1b, v1b, h1b, column = filtered_band(
-        bandwise, pieces, above_band, limits, inverse, slope, (h0, u0, v0, u1, v1)
-    )
-    above = to_lower(column)
-    tr, h2 = tracer_slab(
-        polar, tracers, (h0, u0b, v0b, u1b, v1b), (True,) + (False,) * 4, east, west, pole, BAND, (tr, h2), 10,
+        scalars, POLAR_AT, BAND, 10, tracers, (h0, u0, v0, u1b, v1b), east, west, pole, (tr, h2), 13,
         "tracers_polar",
     )
-    u2, v2 = last_winds(polar, h1b, u1b, v1b, above, False, BAND, rows, cols, winds, "winds_polar")
+    u2, v2 = last_winds(
+        scalars, POLAR_AT, BAND, h1b, u1b, v1b, band_total, rows, cols, winds, 4, "winds_polar"
+    )
     return (tr, h2, u2, v2)
 
 

time: 199 us -> 170 us (0.85)
  waiting for transfers between devices: 29.9 us -> 5.1 us
  Pallas kernels: 138 us -> 126 us
  starting transfers between devices: 21 us -> 30 us
    ppermute x9, waiting for transfers between devices: 29 us -> 0.34 us  [along(): return lax.ppermute(value, 'lon', [(i, (i + d) % n) for i in range(n)])]
    pallas_call x2 -> x1, Pallas kernels: 22 us -> 4.22 us  [column_sum(): pl.pallas_call(functools.partial(column_kernel, facing.shape[1]), grid_sp...]
    ppermute x9, starting transfers between devices: 13 us -> 22 us  [along(): return lax.ppermute(value, 'lon', [(i, (i + d) % n) for i in range(n)])]
    pallas_call x2, Pallas kernels: 61.5 us -> 65.8 us  [tracer_slab(): pl.pallas_call(functools.partial(slab_kernel, rim.shape[1], group, rows,...]
    ppermute x1, waiting for transfers between devices: 0.01 us -> 3.89 us  [shards_tiled(): facing = lax.ppermute(facing, 'lat', [(0, 1), (1, 0)])]
    unnamed x30 -> x34, local copies, waits for them, and re-layouts: 5.16 us -> 5.49 us
  transfers between devices with their start and end apart: 14 -> 14, of which waited for: 5 -> 3; matrix products, arithmetic and copies ran while one was open for 2% -> 0% of each run, Pallas kernels for 56% -> 63%
where the time goes in v3:
time: 170 us
  Pallas kernels  126 us (74%)
  starting transfers between devices  30 us (18%)
  local copies, waits for them, and re-layouts  6.16 us (4%)
  waiting for transfers between devices  5.1 us (3%)
    pallas_call x2, Pallas kernels, tracer_slab(): pl.pallas_call(functools.partial(slab_kernel, rim.shape[1], group, rows,...  65.8 us
    ppermute x9, starting transfers between devices, along(): return lax.ppermute(value, 'lon', [(i, (i + d) % n) for i in range(n)])  22 us
    pallas_call x1, Pallas kernels, pack_columns(): pl.pallas_call(functools.partial(pack_kernel, count + 3, cols - LANE * hi...  17 us
    pallas_call x1, Pallas kernels, filtered_band(): pl.pallas_call(functools.partial(filter_kernel, n), grid_spec=pltpu.Prefe...  12 us
    pallas_call x2, Pallas kernels, last_winds(): pl.pallas_call(functools.partial(winds_kernel, rows, base is not None), g...  11.6 us
    pallas_call x1, Pallas kernels, edge_rows(): pl.pallas_call(functools.partial(rows_kernel, fields), grid_spec=pltpu.Pr...  6.7 us
    ppermute x4, starting transfers between devices, to_lower(): return lax.ppermute(value, 'lev', [(0, 1)])  6.38 us
    pallas_call x1, Pallas kernels, spectra(): pl.pallas_call(functools.partial(spectrum_kernel, n), grid_spec=pltpu.Pre...  5.83 us
  transfers between devices with their start and end apart: 14, of which 3 were waited for; matrix products, arithmetic and copies ran while one was open for 0% of the time, Pallas kernels for 63%

profile of v3, /device:TPU:0, one launch (start us, length us, event | category | flops | bytes accessed | tf_op | source)
XLA Modules:
  0.0 169.7 jit_solution(10133160530835513012)
XLA Ops:
  0.6 1.3 fusion.s
  1.9 3.1 %band_rows.1 = (f32[184,360]{1,0:T(8,128)}, f32[184,360]{1,0:T(8,128)}, f32[184,360]{1,0:T(8,128)}, f32[184,360]{1,0:T(8,128)}) custom-call(s32[10]{0:T(128)} %fusion.s, f32[4,360,360]{2,1,0:T(8,128)} %refs_10_.3, f32[4,360,360]{2,1,0:T(8,128)} %refs_11_.3, f32[4,360,360]{2,1,0:T(8,128)} %refs_9_.3, f32[4,360,360]{2,1,0:T(8,128)} %refs_10_.3, ...), custom_call_target="tpu_custom_call" | custom-call | bytes 9900000 | tf_op jit(solution)/shard_map/band_rows/pallas_call | solution.py:285
  5.0 3.0 %collective-permute-start = (f32[184,360]{1,0:T(8,128)}, f32[184,360]{1,0:T(8,128)S(1)}, u32[]{:S(2)}, u32[]{:S(2)}) collective-permute-start(f32[184,360]{1,0:T(8,128)} %get-tuple-element.56), channel_id=1, source_target_pairs={{0,4},{4,8},{8,12},{12,0},{1,5},{5,9},{9,13},{13,1},{2,6},{6,10},{... | collective-permute-start | bytes 794888 | tf_op jit(solution)/shard_map/ppermute | solution.py:949
  8.0 2.6 %collective-permute-start.1 = (f32[184,360]{1,0:T(8,128)}, f32[184,360]{1,0:T(8,128)S(1)}, u32[]{:S(2)}, u32[]{:S(2)}) collective-permute-start(f32[184,360]{1,0:T(8,128)} %get-tuple-element.57), channel_id=1, source_target_pairs={{0,8},{4,12},{8,0},{12,4},{1,9},{5,13},{9,1},{13,5},{2,10},{6,14},... | collective-permute-start | bytes 794888 | tf_op jit(solution)/shard_map/ppermute | solution.py:949
  10.6 1.3 collective-permute-start.2
  12.0 17.0 %pack_columns.1 = (f32[360,128]{1,0:T(8,128)}, f32[360,128]{1,0:T(8,128)}) custom-call(s32[10]{0:T(128)} %fusion.s, f32[10,4,360,360]{3,2,1,0:T(8,128)} %refs_0_.5, f32[10,4,360,360]{3,2,1,0:T(8,128)} %refs_0_.5, f32[4,360,360]{2,1,0:T(8,128)} %refs_9_.3, f32[4,360,360]{2,1,0:T(8,128)} %refs_9_.3, f32[4,360,360]{2,1,0:T(8,128)} %refs_10_.3, ...), custom_call_target="tpu_custom_call" | custom-call | bytes 33000000 | tf_op jit(solution)/shard_map/pack_columns/pallas_call | solution.py:367
  29.0 0.4 collective-permute-start.3
  29.4 1.6 collective-permute-start.4
  31.0 0.0 collective-permute-done.refs_1_
  31.0 0.0 collective-permute-done.1.refs_2_
  31.0 0.0 copy-start.11
  31.0 0.0 collective-permute-done.2.refs_3_
  31.1 0.7 copy-done.10
  31.7 0.1 copy-done.11
  31.8 0.7 copy-done.12
  32.5 5.8 %spectra.1.refs_0_ = f32[184,384]{1,0:T(8,128)} custom-call(s32[10]{0:T(128)} %fusion.s, f32[184,360]{1,0:T(8,128)} %get-tuple-element.55.refs_0_, f32[184,360]{1,0:T(8,128)} %copy-done.10, f32[184,360]{1,0:T(8,128)} %copy-done.11, f32[184,360]{1,0:T(8,128)} %copy-done.12, f32[4,360,384]{2,1,0:T(8,128)} %constant.25.clone.refs_4_.refs_5_.refs_6_.refs_7_, ...), custom_call_target="tpu_custom_call" | custom-call | bytes 19800000 | tf_op jit(solution)/shard_map/spectra/pallas_call | solution.py:321
  38.4 0.0 collective-permute-done.3.e_top.e_bot.east.refs_5_.refs_12_.refs_6_
  38.4 0.3 collective-permute-done.4.w_top.w_bot.west.refs_6_.refs_13_.refs_7_
  38.7 0.4 copy-done
  39.1 0.7 copy-done.1
  39.7 6.7 %edge_rows.1 = (f32[4,13,2,384]{3,2,1,0:T(2,128)}, f32[4,13,2,384]{3,2,1,0:T(2,128)}) custom-call(s32[10]{0:T(128)} %fusion.s, f32[10,4,360,360]{3,2,1,0:T(8,128)} %refs_0_.5, f32[10,4,360,360]{3,2,1,0:T(8,128)} %refs_0_.5, f32[4,360,360]{2,1,0:T(8,128)} %refs_9_.3, f32[4,360,360]{2,1,0:T(8,128)} %refs_9_.3, f32[4,360,360]{2,1,0:T(8,128)} %refs_10_.3, ...), custom_call_target="tpu_custom_call" | custom-call | bytes 23100000 | tf_op jit(solution)/shard_map/edge_rows/pallas_call | solution.py:422
  46.4 0.0 copy-start.3
  46.4 0.0 copy-start.16
  46.4 1.7 collective-permute-start.5
  48.1 3.9 %collective-permute-done.5.facing.refs_7_ = f32[4,13,2,384]{3,2,1,0:T(2,128)S(1)} collective-permute-done((f32[4,13,2,384]{3,2,1,0:T(2,128)}, f32[4,13,2,384]{3,2,1,0:T(2,128)S(1)}, u32[]{:S(2)}, u32[]{:S(2)}) %collective-permute-start.5) | collective-permute-done | bytes 159776 | tf_op jit(solution)/shard_map/ppermute | solution.py:966
  52.0 0.7 copy-done.5
  52.7 4.2 %column_sum.1 = f32[3,392,128]{2,1,0:T(8,128)} custom-call(s32[10]{0:T(128)} %fusion.s, f32[4,360,360]{2,1,0:T(8,128)} %refs_9_.3, f32[360,128]{1,0:T(8,128)} %copy-done, f32[360,128]{1,0:T(8,128)} %copy-done.1, f32[4,13,2,384]{3,2,1,0:T(2,128)} %copy-done.5), custom_call_target="tpu_custom_call" | custom-call | bytes 13200000 | tf_op jit(solution)/shard_map/column_sum/pallas_call | solution.py:492
  56.9 1.3 collective-permute-start.6
  58.2 0.0 copy-done.3
  58.2 8.7 %collective-permute-start.7 = (f32[184,384]{1,0:T(8,128)S(1)}, f32[184,384]{1,0:T(8,128)S(1)}, u32[]{:S(2)}, u32[]{:S(2)}) collective-permute-start(f32[184,384]{1,0:T(8,128)S(1)} %copy-done.3), channel_id=1, source_target_pairs={{0,4},{4,8},{8,12},{12,0},{1,5},{5,9},{9,13},{13,1},{2,6},{6,10},{... | collective-permute-start | bytes 847880 | tf_op jit(solution)/shard_map/ppermute | solution.py:949
  66.9 2.7 %collective-permute-start.8 = (f32[184,384]{1,0:T(8,128)S(1)}, f32[184,384]{1,0:T(8,128)S(1)}, u32[]{:S(2)}, u32[]{:S(2)}) collective-permute-start(f32[184,384]{1,0:T(8,128)S(1)} %copy-done.3), channel_id=1, source_target_pairs={{0,8},{4,12},{8,0},{12,4},{1,9},{5,13},{9,1},{13,5},{2,10},{6,14},... | collective-permute-start | bytes 847880 | tf_op jit(solution)/shard_map/ppermute | solution.py:949
  69.6 0.0 collective-permute-start.9
  69.6 0.0 copy-done.16
  69.6 1.5 collective-permute-start.11
  71.2 0.0 collective-permute-done.6.refs_4_.refs_8_
  71.2 0.8 copy-done.2
  72.0 52.2 %tracers_inner.1 = (f32[10,4,360,360]{3,2,1,0:T(8,128)}, f32[4,360,360]{2,1,0:T(8,128)}, f32[4,3,328,128]{3,2,1,0:T(8,128)}, f32[4,3,328,128]{3,2,1,0:T(8,128)},...) custom-call(s32[10]{0:T(128)} %fusion.s, f32[10,4,360,360]{3,2,1,0:T(8,128)} %refs_0_.5, f32[4,360,360]{2,1,0:T(8,128)} %refs_9_.3, ...), custom_call_target="tpu_custom_call" | custom-call | bytes 165000000 | tf_op jit(solution)/shard_map/tracers_inner/pallas_call | solution.py:848
  124.2 0.0 collective-permute-done.7.refs_1_
  124.2 0.0 copy-start.6
  124.3 0.0 collective-permute-done.8.refs_2_
  124.3 0.0 copy-start.7
  124.3 0.0 collective-permute-done.9.refs_3_
  124.3 0.0 copy-start.8
  124.3 1.3 collective-permute-start.13
  125.7 1.3 collective-permute-start.10
  127.0 0.0 copy-done.15
  127.0 0.0 collective-permute-done.11.refs_14_.refs_8_
  127.0 0.0 copy-start.4
  127.0 0.9 collective-permute-done.10.refs_4_
  127.9 0.7 broadcast_in_dim.16.refs_5_
  128.6 0.0 copy-done.6
  128.6 0.0 copy-done.7
  128.6 0.0 copy-done.8
  128.6 0.0 copy-done.4
  128.6 12.0 %filtered_band.1 = (f32[4,3,96,128]{3,2,1,0:T(8,128)}, f32[4,3,96,128]{3,2,1,0:T(8,128)}, f32[4,3,96,128]{3,2,1,0:T(8,128)}, f32[4,3,96,128]{3,2,1,0:T(8,128)}, ...) custom-call(s32[10]{0:T(128)} %fusion.s, f32[184,384]{1,0:T(8,128)} %spectra.1.refs_0_, ...), custom_call_target="tpu_custom_call" | custom-call | bytes 39600000 | tf_op jit(solution)/shard_map/filtered_band/pallas_call | solution.py:632
  140.6 2.4 %collective-permute-start.12 = (f32[3,96,128]{2,1,0:T(8,128)}, f32[3,96,128]{2,1,0:T(8,128)S(1)}, u32[]{:S(2)}, u32[]{:S(2)}) collective-permute-start(f32[3,96,128]{2,1,0:T(8,128)} %get-tuple-element.81), channel_id=1, source_target_pairs={{0,1},{2,3},{4,5},{6,7},{8,9},{10,11},{12,13},{14,15},{16,17},{18,... | collective-permute-start | bytes 442376 | tf_op jit(solution)/shard_map/ppermute | solution.py:952
  143.1 13.5 %tracers_polar.1 = (f32[10,4,360,360]{3,2,1,0:T(8,128)}, f32[4,360,360]{2,1,0:T(8,128)}) custom-call(s32[10]{0:T(128)} %fusion.s, f32[10,4,360,360]{3,2,1,0:T(8,128)} %refs_0_.5, f32[4,3,96,128]{3,2,1,0:T(8,128)} %get-tuple-element.71.refs_1_, f32[4,3,96,128]{3,2,1,0:T(8,128)} %get-tuple-element.72.refs_2_, ...), custom_call_target="tpu_custom_call", output_to_operand_aliasing={{0}: (10, {}), {1}: (11, {})} | custom-call | bytes 42900000 | tf_op jit(solution)/shard_map/tracers_polar/pallas_call | solution.py:848
  156.6 0.0 collective-permute-done.13.above
  156.6 0.0 copy-start.9
  156.6 0.8 copy-done.9
  157.4 7.1 %winds_inner.1 = (f32[4,360,360]{2,1,0:T(8,128)}, f32[4,360,360]{2,1,0:T(8,128)}) custom-call(s32[10]{0:T(128)} %fusion.s, f32[4,3,328,128]{3,2,1,0:T(8,128)} %get-tuple-element.82.h, f32[4,3,328,128]{3,2,1,0:T(8,128)} %get-tuple-element.83.u, f32[4,3,328,128]{3,2,1,0:T(8,128)} %get-tuple-element.84.v, f32[3,328,128]{2,1,0:T(8,128)} %copy-done.9), custom_call_target="tpu_custom_call" | custom-call | bytes 23100000 | tf_op jit(solution)/shard_map/winds_inner/pallas_call | solution.py:896
  164.5 0.0 collective-permute-done.12.above
  164.5 0.6 copy-done.13
  165.2 4.5 %winds_polar.1 = (f32[4,360,360]{2,1,0:T(8,128)}, f32[4,360,360]{2,1,0:T(8,128)}) custom-call(s32[10]{0:T(128)} %fusion.s, f32[4,3,96,128]{3,2,1,0:T(8,128)} %get-tuple-element.80.h, f32[4,3,96,128]{3,2,1,0:T(8,128)} %get-tuple-element.74.refs_4_.u, f32[4,3,96,128]{3,2,1,0:T(8,128)} %get-tuple-element.75.refs_5_.v, ...), custom_call_target="tpu_custom_call", output_to_operand_aliasing={{0}: (5, {}), {1}: (6, {})} | custom-call | bytes 13200000 | tf_op jit(solution)/shard_map/winds_polar/pallas_call | solution.py:896
  (13 shorter events, 0.1 us)
Async XLA Ops:
  5.0 26.0 %collective-permute-start = (f32[184,360]{1,0:T(8,128)}, f32[184,360]{1,0:T(8,128)S(1)}, u32[]{:S(2)}, u32[]{:S(2)}) collective-permute-start(f32[184,360]{1,0:T(8,128)} %get-tuple-element.56), channel_id=1, source_target_pairs={{0,4},{4,8},{8,12},{12,0},{1,5},{5,9},{9,13},{13,1},{2,6},{6,10},{... | collective-permute-start | bytes 794888 | tf_op jit(solution)/shard_map/ppermute | solution.py:949
  8.0 23.0 %collective-permute-start.1 = (f32[184,360]{1,0:T(8,128)}, f32[184,360]{1,0:T(8,128)S(1)}, u32[]{:S(2)}, u32[]{:S(2)}) collective-permute-start(f32[184,360]{1,0:T(8,128)} %get-tuple-element.57), channel_id=1, source_target_pairs={{0,8},{4,12},{8,0},{12,4},{1,9},{5,13},{9,1},{13,5},{2,10},{6,14},... | collective-permute-start | bytes 794888 | tf_op jit(solution)/shard_map/ppermute | solution.py:949
  10.6 20.4 %collective-permute-start.2 = (f32[184,360]{1,0:T(8,128)}, f32[184,360]{1,0:T(8,128)S(1)}, u32[]{:S(2)}, u32[]{:S(2)}) collective-permute-start(f32[184,360]{1,0:T(8,128)} %get-tuple-element.58), channel_id=1, source_target_pairs={{0,12},{4,0},{8,4},{12,8},{1,13},{5,1},{9,5},{13,9},{2,14},{6,2},{... | collective-permute-start | bytes 794888 | tf_op jit(solution)/shard_map/ppermute | solution.py:949
  29.0 9.4 %collective-permute-start.3 = (f32[360,128]{1,0:T(8,128)}, f32[360,128]{1,0:T(8,128)S(1)}, u32[]{:S(2)}, u32[]{:S(2)}) collective-permute-start(f32[360,128]{1,0:T(8,128)} %get-tuple-element.60), channel_id=1, source_target_pairs={{0,12},{4,0},{8,4},{12,8},{1,13},{5,1},{9,5},{13,9},{2,14},{6,2},{... | collective-permute-start | bytes 552968 | tf_op jit(solution)/shard_map/ppermute | solution.py:949
  29.4 9.2 %collective-permute-start.4 = (f32[360,128]{1,0:T(8,128)}, f32[360,128]{1,0:T(8,128)S(1)}, u32[]{:S(2)}, u32[]{:S(2)}) collective-permute-start(f32[360,128]{1,0:T(8,128)} %get-tuple-element.61), channel_id=1, source_target_pairs={{0,4},{4,8},{8,12},{12,0},{1,5},{5,9},{9,13},{13,1},{2,6},{6,10},{... | collective-permute-start | bytes 552968 | tf_op jit(solution)/shard_map/ppermute | solution.py:949
  31.0 0.7 copy-start.10
  31.0 0.8 copy-start.11
  31.8 0.7 copy-start.12
  38.4 0.7 copy-start
  39.1 0.7 copy-start.1
  46.4 11.8 %copy-start.3 = (f32[184,384]{1,0:T(8,128)S(1)}, f32[184,384]{1,0:T(8,128)}, u32[]{:S(2)}) copy-start(f32[184,384]{1,0:T(8,128)} %spectra.1.refs_0_) | copy-start | bytes 847876
  46.4 23.2 %copy-start.16 = (f32[4,13,2,384]{3,2,1,0:T(2,128)S(1)}, f32[4,13,2,384]{3,2,1,0:T(2,128)}, u32[]{:S(2)}) copy-start(f32[4,13,2,384]{3,2,1,0:T(2,128)} %get-tuple-element.70) | copy-start | bytes 479236
  46.4 5.6 %collective-permute-start.5 = (f32[4,13,2,384]{3,2,1,0:T(2,128)}, f32[4,13,2,384]{3,2,1,0:T(2,128)S(1)}, u32[]{:S(2)}, u32[]{:S(2)}) collective-permute-start(f32[4,13,2,384]{3,2,1,0:T(2,128)} %get-tuple-element.62), channel_id=1, source_target_pairs={{0,2},{2,0},{1,3},{3,1},{4,6},{6,4},{5,7},{7,5},{8,10},{10,8},{9,1... | collective-permute-start | bytes 479240 | tf_op jit(solution)/shard_map/ppermute | solution.py:966
  52.0 0.7 copy-start.5
  56.9 14.3 %collective-permute-start.6 = (f32[3,392,128]{2,1,0:T(8,128)}, f32[3,392,128]{2,1,0:T(8,128)S(1)}, u32[]{:S(2)}, u32[]{:S(2)}) collective-permute-start(f32[3,392,128]{2,1,0:T(8,128)} %column_sum.1), channel_id=1, source_target_pairs={{0,1},{2,3},{4,5},{6,7},{8,9},{10,11},{12,13},{14,15},{16,17},{18,... | collective-permute-start | bytes 1806344 | tf_op jit(solution)/shard_map/ppermute | solution.py:952
  58.2 66.0 %collective-permute-start.7 = (f32[184,384]{1,0:T(8,128)S(1)}, f32[184,384]{1,0:T(8,128)S(1)}, u32[]{:S(2)}, u32[]{:S(2)}) collective-permute-start(f32[184,384]{1,0:T(8,128)S(1)} %copy-done.3), channel_id=1, source_target_pairs={{0,4},{4,8},{8,12},{12,0},{1,5},{5,9},{9,13},{13,1},{2,6},{6,10},{... | collective-permute-start | bytes 847880 | tf_op jit(solution)/shard_map/ppermute | solution.py:949
  66.9 57.3 %collective-permute-start.8 = (f32[184,384]{1,0:T(8,128)S(1)}, f32[184,384]{1,0:T(8,128)S(1)}, u32[]{:S(2)}, u32[]{:S(2)}) collective-permute-start(f32[184,384]{1,0:T(8,128)S(1)} %copy-done.3), channel_id=1, source_target_pairs={{0,8},{4,12},{8,0},{12,4},{1,9},{5,13},{9,1},{13,5},{2,10},{6,14},... | collective-permute-start | bytes 847880 | tf_op jit(solution)/shard_map/ppermute | solution.py:949
  69.6 54.6 %collective-permute-start.9 = (f32[184,384]{1,0:T(8,128)S(1)}, f32[184,384]{1,0:T(8,128)S(1)}, u32[]{:S(2)}, u32[]{:S(2)}) collective-permute-start(f32[184,384]{1,0:T(8,128)S(1)} %copy-done.3), channel_id=1, source_target_pairs={{0,12},{4,0},{8,4},{12,8},{1,13},{5,1},{9,5},{13,9},{2,14},{6,2},{... | collective-permute-start | bytes 847880 | tf_op jit(solution)/shard_map/ppermute | solution.py:949
  69.6 57.3 %copy-start.15 = (s32[2,60]{1,0:T(2,128)S(1)}, s32[2,60]{1,0:T(2,128)}, u32[]{:S(2)}) copy-start(s32[2,60]{1,0:T(2,128)} %param.14) | copy-start | bytes 1444
  69.6 57.3 %collective-permute-start.11 = (f32[4,13,2,384]{3,2,1,0:T(2,128)S(1)}, f32[4,13,2,384]{3,2,1,0:T(2,128)S(1)}, u32[]{:S(2)}, u32[]{:S(2)}) collective-permute-start(f32[4,13,2,384]{3,2,1,0:T(2,128)S(1)} %copy-done.16), channel_id=1, source_target_pairs={{0,8},{4,12},{8,0},{12,4},{1,9},{5,13},{9,1},{13,5},{2,10},{6,14},... | collective-permute-start | bytes 479240 | tf_op jit(solution)/shard_map/ppermute | solution.py:949
  71.2 0.8 copy-start.2
  124.2 4.3 %copy-start.6 = (f32[184,384]{1,0:T(8,128)}, f32[184,384]{1,0:T(8,128)S(1)}, u32[]{:S(2)}) copy-start(f32[184,384]{1,0:T(8,128)S(1)} %collective-permute-done.7.refs_1_) | copy-start | bytes 847876
  124.3 4.3 %copy-start.7 = (f32[184,384]{1,0:T(8,128)}, f32[184,384]{1,0:T(8,128)S(1)}, u32[]{:S(2)}) copy-start(f32[184,384]{1,0:T(8,128)S(1)} %collective-permute-done.8.refs_2_) | copy-start | bytes 847876
  124.3 4.3 %copy-start.8 = (f32[184,384]{1,0:T(8,128)}, f32[184,384]{1,0:T(8,128)S(1)}, u32[]{:S(2)}) copy-start(f32[184,384]{1,0:T(8,128)S(1)} %collective-permute-done.9.refs_3_) | copy-start | bytes 847876
  124.3 32.3 %collective-permute-start.13 = (f32[3,328,128]{2,1,0:T(8,128)}, f32[3,328,128]{2,1,0:T(8,128)S(1)}, u32[]{:S(2)}, u32[]{:S(2)}) collective-permute-start(f32[3,328,128]{2,1,0:T(8,128)} %get-tuple-element.85), channel_id=1, source_target_pairs={{0,1},{2,3},{4,5},{6,7},{8,9},{10,11},{12,13},{14,15},{16,17},{18,... | collective-permute-start | bytes 1511432 | tf_op jit(solution)/shard_map/ppermute | solution.py:952
  125.7 2.2 %collective-permute-start.10 = (f32[64,384]{1,0:T(8,128)S(1)}, f32[64,384]{1,0:T(8,128)S(1)}, u32[]{:S(2)}, u32[]{:S(2)}) collective-permute-start(f32[64,384]{1,0:T(8,128)S(1)} %slice_add_fusion), channel_id=1, source_target_pairs={{0,1},{2,3},{4,5},{6,7},{8,9},{10,11},{12,13},{14,15},{16,17},{18,... | collective-permute-start | bytes 294920 | tf_op jit(solution)/shard_map/ppermute | solution.py:952
  127.0 1.6 copy-start.4
  127.9 0.7 copy-start.14
  140.6 23.9 %collective-permute-start.12 = (f32[3,96,128]{2,1,0:T(8,128)}, f32[3,96,128]{2,1,0:T(8,128)S(1)}, u32[]{:S(2)}, u32[]{:S(2)}) collective-permute-start(f32[3,96,128]{2,1,0:T(8,128)} %get-tuple-element.81), channel_id=1, source_target_pairs={{0,1},{2,3},{4,5},{6,7},{8,9},{10,11},{12,13},{14,15},{16,17},{18,... | collective-permute-start | bytes 442376 | tf_op jit(solution)/shard_map/ppermute | solution.py:952
  156.6 0.8 copy-start.9
  164.5 0.6 copy-start.13

commit v4 on v3

--- a/solution.py
+++ b/solution.py
@@ -223,6 +223,20 @@
     return in_e, in_w, in_n, in_s, new
 
 
+def halves(x):
+    high = x.astype(jnp.bfloat16)
+    return high, (x - high.astype(jnp.float32)).astype(jnp.bfloat16)
+
+
+def dot3(a, b):
+    (a_hi, a_lo), (b_hi, b_lo) = halves(a), halves(b)
+
+    def one(x, y):
+        return jnp.dot(x, y, preferred_element_type=jnp.float32)
+
+    return one(a_hi, b_hi) + (one(a_hi, b_lo) + one(a_lo, b_hi))
+
+
 def sweep(first, end, body, depth):
     whole = (end - first) // depth
 
@@ -300,12 +314,7 @@
 def spectrum_kernel(n, s, *refs):
     total = None
     for d in range(n):
-        part = jnp.dot(
-            refs[d][...],
-            refs[n + d][0],
-            precision=lax.Precision.HIGHEST,
-            preferred_element_type=jnp.float32,
-        )
+        part = dot3(refs[d][...], refs[n + d][0])
         total = part if total is None else total + part
     refs[2 * n][...] = total
 
@@ -334,43 +343,48 @@
 
 
 def pack_kernel(fields, last, s, t_lo, t_hi, h_lo, h_hi, u_lo, u_hi, v_lo, v_hi, west, east):
-    level = pl.program_id(0)
     lane = lanes()
-    lows = [(t_lo, (f, 0)) for f in range(fields - 3)] + [(h_lo, (0,)), (u_lo, (0,)), (v_lo, (0,))]
-    highs = [(t_hi, (f, 0)) for f in range(fields - 3)] + [(h_hi, (0,)), (u_hi, (0,)), (v_hi, (0,))]
-    begin = 2 * fields * level
-    mine = jnp.logical_and(lane >= begin, lane < begin + 2 * fields)
+    count, levels = t_lo.shape[:2]
+    gap = last - 2
 
     def step(i):
-        rows = eight(i)
-        for f in range(fields):
-            here = lane >= 2 * f
-            ref, lead = lows[f]
-            tile = ref[lead + (rows, slice(None))]
-            got_w = jnp.where(here, pltpu.roll(tile, 2 * f, 1), got_w) if f else tile
-            ref, lead = highs[f]
-            tile = ref[lead + (rows, slice(None))]
-            turned = pltpu.roll(tile, (2 * f - last + 2) % LANE, 1)
-            got_e = jnp.where(here, turned, got_e) if f else turned
-        west[rows, :] = jnp.where(mine, pltpu.roll(got_w, begin, 1), west[rows, :])
-        east[rows, :] = jnp.where(mine, pltpu.roll(got_e, begin, 1), east[rows, :])
-
-    sweep(0, west.shape[0] // 8, step, UNROLL["step"])
+        here = eight(i)
+        got_w = got_e = None
+        for l in range(levels):
+            sources = [(t_lo, t_hi, (f, l)) for f in range(count)]
+            sources += [(h_lo, h_hi, (l,)), (u_lo, u_hi, (l,)), (v_lo, v_hi, (l,))]
+            got = None
+            for f, (lo, hi, lead) in enumerate(sources):
+                at = lead + (here, slice(None))
+                both = jnp.where(lane < LANE // 2, lo[at], hi[at])
+                turned = pltpu.roll(both, 2 * f, 1) if f else both
+                mine = jnp.logical_or(jnp.logical_and(lane >= 2 * f, lane < LANE // 2), lane >= gap + 2 * f)
+                got = jnp.where(mine, turned, got) if f else turned
+            base = 2 * fields * l
+            to_w = pltpu.roll(got, base, 1) if l else got
+            to_e = pltpu.roll(got, (base - gap) % LANE, 1)
+            got_w = jnp.where(lane >= base, to_w, got_w) if l else to_w
+            got_e = jnp.where(lane >= base, to_e, got_e) if l else to_e
+        west[here, :] = got_w
+        east[here, :] = got_e
+
+    sweep(0, west.shape[0] // 8, step, 3)
 
 
 def pack_columns(scalars, tracers, h, u, v):
     count, levels, rows, cols = tracers.shape
     high = (cols - 1) // LANE
-    t_spec = [pl.BlockSpec((count, 1, rows, LANE), lambda l, s, c=c: (0, l, 0, c)) for c in (0, high)]
-    f_spec = [pl.BlockSpec((1, rows, LANE), lambda l, s, c=c: (l, 0, c)) for c in (0, high)]
+    part = rows // 5
+    t_spec = [pl.BlockSpec((count, levels, part, LANE), lambda r, s, c=c: (0, 0, r, c)) for c in (0, high)]
+    f_spec = [pl.BlockSpec((levels, part, LANE), lambda r, s, c=c: (0, r, c)) for c in (0, high)]
     out = jax.ShapeDtypeStruct((rows, LANE), jnp.float32)
     return pl.pallas_call(
         functools.partial(pack_kernel, count + 3, cols - LANE * high),
         grid_spec=pltpu.PrefetchScalarGridSpec(
             num_scalar_prefetch=1,
-            grid=(levels,),
+            grid=(5,),
             in_specs=t_spec + f_spec * 3,
-            out_specs=[pl.BlockSpec((rows, LANE), lambda l, s: (0, 0))] * 2,
+            out_specs=[pl.BlockSpec((part, LANE), lambda r, s: (r, 0))] * 2,
         ),
         out_shape=[out, out],
         cost_estimate=cost(10),
@@ -384,30 +398,32 @@
     level = pl.program_id(0)
     lane = lanes()
     cols = h_top.shape[2]
-    tail = top.shape[1] - LANE
+    tail = top.shape[2] - LANE
     last = cols - tail
     refs = [(t_top, t_bot, (f, 0)) for f in range(fields - 3)]
     refs += [(h_top, h_bot, (0,)), (u_top, u_bot, (0,)), (v_top, v_bot, (0,))]
     for f in range(fields):
         plane = fields * level + f
         a, b, lead = refs[f]
-        top[:, 0:cols] = a[lead]
-        bot[:, 0:cols] = b[lead]
-        top[:, cols:] = rim_lanes(e_top[...], w_top[...], plane, last, lane)[:, last:]
-        bot[:, cols:] = rim_lanes(e_bot[...], w_bot[...], plane, last, lane)[:, last:]
-        flip = -1.0 if f == fields - 1 else 1.0
-
-        @pl.when(s[0] == 1)
-        def _():
-            pole[0, f, 0:1, :] = flip * top[1:2, :]
-            pole[0, f, 1:2, :] = flip * top[0:1, :]
-            facing[0, f] = bot[6:8, :]
-
-        @pl.when(s[0] == 0)
-        def _():
-            pole[0, f, 0:1, :] = flip * bot[7:8, :]
-            pole[0, f, 1:2, :] = flip * bot[6:7, :]
-            facing[0, f] = top[0:2, :]
+        top[f, :, 0:cols] = a[lead]
+        bot[f, :, 0:cols] = b[lead]
+        top[f, :, cols:] = rim_lanes(e_top[...], w_top[...], plane, last, lane)[:, last:]
+        bot[f, :, cols:] = rim_lanes(e_bot[...], w_bot[...], plane, last, lane)[:, last:]
+    flips = [1.0] * (fields - 1) + [-1.0]
+
+    @pl.when(s[0] == 1)
+    def _():
+        for f, flip in enumerate(flips):
+            pole[0, f, 0:1, :] = flip * top[f, 1:2, :]
+            pole[0, f, 1:2, :] = flip * top[f, 0:1, :]
+            facing[0, f] = bot[f, 6:8, :]
+
+    @pl.when(s[0] == 0)
+    def _():
+        for f, flip in enumerate(flips):
+            pole[0, f, 0:1, :] = flip * bot[f, 7:8, :]
+            pole[0, f, 1:2, :] = flip * bot[f, 6:7, :]
+            facing[0, f] = top[f, 0:2, :]
 
 
 def edge_rows(scalars, tracers, h, u, v, east, west):
@@ -426,7 +442,7 @@
             grid=(levels,),
             in_specs=t_spec + f_spec * 3 + c_spec * 2,
             out_specs=[pl.BlockSpec((1, fields, 2, width), lambda l, s: (l, 0, 0, 0))] * 2,
-            scratch_shapes=[pltpu.VMEM((8, width), jnp.float32)] * 2,
+            scratch_shapes=[pltpu.VMEM((fields, 8, width), jnp.float32)] * 2,
         ),
         out_shape=[out, out],
         cost_estimate=cost(7),
@@ -586,12 +602,8 @@
                     at = 3 * POLAR + 2 * k
                     lhs[at : at + 1, :] = sign * one * a
                     lhs[at + 1 : at + 2, :] = sign * one * b
-                back = jnp.dot(
-                    lhs[...], basis[0], precision=lax.Precision.HIGHEST, preferred_element_type=jnp.float32
-                )
-                grad = jnp.dot(
-                    rhs[...], slope[0], precision=lax.Precision.HIGHEST, preferred_element_type=jnp.float32
-                )
+                back = dot3(lhs[...], basis[0])
+                grad = dot3(rhs[...], slope[0])
                 zonal = back[0:POLAR]
                 later = zonal - GRADIENT_COEF * grad[0:POLAR]
                 for c in range(count):
@@ -862,52 +874,52 @@
     )(scalars, *operands)
 
 
-def winds_kernel(rows, has_base, s, h, u, v, above, *refs):
-    u_out, v_out, cum, press = refs[2:] if has_base else refs
+def winds_kernel(s, *refs):
+    u_out, v_out = refs[8:10]
     lane = lanes()
-    count, slab = h.shape[1:3]
     cols = u_out.shape[2]
-    pressure_rows(pl.program_id(0), above, cum, press, h.at[0], count, slab)
-
-    def step(i):
-        row = 8 * i + PAD
-        zonal, merid = gradient(press, row, count, lane)
-        for c in range(count):
-            wide = min(LANE, cols - c * LANE)
-            part = slice(c * LANE, c * LANE + wide)
-            u_out[0, eight(i), part] = (u[0, c, at_row(row), :] - zonal[c])[:, 0:wide]
-            v_out[0, eight(i), part] = (v[0, c, at_row(row), :] - merid[c])[:, 0:wide]
-
-    sweep(0, rows // 8, step, UNROLL["step"])
-
-
-def last_winds(scalars, place, rows, h, u, v, above, height, cols, base, micros, name):
-    levels, tiles, slab = h.shape[:3]
-    E = pl.Element
-    spec = pl.BlockSpec((1, tiles, slab, LANE), lambda l, s: (l, 0, 0, 0))
-    flat = pl.BlockSpec((tiles, slab, LANE), lambda l, s: (0, 0, 0))
-    out_spec = pl.BlockSpec((E(1), E(rows), E(cols)), lambda l, s: (l, s[place] * 8, 0))
-    out = jax.ShapeDtypeStruct((levels, height, cols), jnp.float32)
-    in_specs, operands, aliases = [spec] * 3 + [flat], [h, u, v, above], {}
-    if base is not None:
-        in_specs += [pl.BlockSpec(memory_space=pl.ANY)] * 2
-        operands += list(base)
-        aliases = {5: 0, 6: 1}
+    for k, place in enumerate((MIDDLE_AT, POLAR_AT)):
+        h, u, v, above = refs[4 * k : 4 * k + 4]
+        cum, press = refs[10 + 2 * k : 12 + 2 * k]
+        count, slab = h.shape[1:3]
+        pressure_rows(pl.program_id(0), above, cum, press, h.at[0], count, slab)
+
+        def step(i):
+            row = 8 * i + PAD
+            to = eight(i + s[place])
+            zonal, merid = gradient(press, row, count, lane)
+            for c in range(count):
+                wide = min(LANE, cols - c * LANE)
+                part = slice(c * LANE, c * LANE + wide)
+                u_out[0, to, part] = (u[0, c, at_row(row), :] - zonal[c])[:, 0:wide]
+                v_out[0, to, part] = (v[0, c, at_row(row), :] - merid[c])[:, 0:wide]
+
+        sweep(0, slab // 8 - 4, step, UNROLL["step"])
+
+
+def last_winds(scalars, slabs, rows, cols):
+    levels, tiles = slabs[0][0].shape[:2]
+    in_specs, scratch = [], []
+    for h, _, _, _ in slabs:
+        tall = h.shape[2]
+        in_specs += [pl.BlockSpec((1, tiles, tall, LANE), lambda l, s: (l, 0, 0, 0))] * 3
+        in_specs += [pl.BlockSpec((tiles, tall, LANE), lambda l, s: (0, 0, 0))]
+        scratch += [pltpu.VMEM((tiles, tall, LANE), jnp.float32)] * 2
+    out = jax.ShapeDtypeStruct((levels, rows, cols), jnp.float32)
     return pl.pallas_call(
-        functools.partial(winds_kernel, rows, base is not None),
+        winds_kernel,
         grid_spec=pltpu.PrefetchScalarGridSpec(
             num_scalar_prefetch=1,
             grid=(levels,),
             in_specs=in_specs,
-            out_specs=[out_spec] * 2,
-            scratch_shapes=[pltpu.VMEM((tiles, slab, LANE), jnp.float32)] * 2,
+            out_specs=[pl.BlockSpec((1, rows, cols), lambda l, s: (l, 0, 0))] * 2,
+            scratch_shapes=scratch,
         ),
         out_shape=[out, out],
-        input_output_aliases=aliases,
-        cost_estimate=cost(micros),
+        cost_estimate=cost(8),
         compiler_params=params(),
-        name=name,
-    )(scalars, *operands)
+        name="last_winds",
+    )(scalars, *slabs[0], *slabs[1])
 
 
 def bases(n, cols):
@@ -978,14 +990,11 @@
         scalars, pieces, above_band, limits, inverse, slope, column, thickness, zonal, meridional, east, west, pole
     )
     band_total = to_lower(band_total)
-    winds = last_winds(scalars, MIDDLE_AT, inner, h1, u1, v1, total, rows, cols, None, 7, "winds_inner")
     tr, h2 = tracer_slab(
         scalars, POLAR_AT, BAND, 10, tracers, (h0, u0, v0, u1b, v1b), east, west, pole, (tr, h2), 13,
         "tracers_polar",
     )
-    u2, v2 = last_winds(
-        scalars, POLAR_AT, BAND, h1b, u1b, v1b, band_total, rows, cols, winds, 4, "winds_polar"
-    )
+    u2, v2 = last_winds(scalars, ((h1, u1, v1, total), (h1b, u1b, v1b, band_total)), rows, cols)
     return (tr, h2, u2, v2)
 
 
@@ -999,10 +1008,11 @@
         and mesh.shape["lev"] == 2
         and levels == mesh.shape["lon"]
         and mesh.shape["lon"] % 2 == 0
-        and rows % 8 == 0
+        and rows % 40 == 0
         and rows >= 2 * BAND + 8
         and last + 4 <= LANE
-        and last >= 2
+        and last - 2 >= LANE // 2
+        and last + 2 * (count + 2) <= LANE
         and cols > LANE
         and 2 * (count + 3) * levels <= LANE
         and count % 5 == 0

time: 170 us -> 160 us (0.941)
  Pallas kernels: 126 us -> 112 us
  waiting for transfers between devices: 5.1 us -> 10.7 us
    pallas_call x1, Pallas kernels: 17 us -> 11.4 us  [pack_columns(): pl.pallas_call(functools.partial(pack_kernel, count + 3, cols - LANE * hi...]
    ppermute x9, waiting for transfers between devices: 0.34 us -> 5.81 us  [along(): return lax.ppermute(value, 'lon', [(i, (i + d) % n) for i in range(n)])]
    pallas_call x2 -> x1, Pallas kernels: 11.6 us -> 8.2 us  [last_winds(): pl.pallas_call(winds_kernel, grid_spec=pltpu.PrefetchScalarGridSpec(num_s...]
    pallas_call x1, Pallas kernels: 6.7 us -> 4.3 us  [edge_rows(): pl.pallas_call(functools.partial(rows_kernel, fields), grid_spec=pltpu.Pr...]
    pallas_call x1, Pallas kernels: 12 us -> 10.1 us  [filtered_band(): pl.pallas_call(functools.partial(filter_kernel, n), grid_spec=pltpu.Prefe...]
  transfers between devices with their start and end apart: 14 -> 14, of which waited for: 3 -> 4; matrix products, arithmetic and copies ran while one was open for 0% -> 0% of each run, Pallas kernels for 63% -> 57%
where the time goes in v4:
time: 160 us
  Pallas kernels  112 us (70%)
  starting transfers between devices  30.3 us (19%)
  waiting for transfers between devices  10.7 us (7%)
  local copies, waits for them, and re-layouts  5.16 us (3%)
    pallas_call x2, Pallas kernels, tracer_slab(): pl.pallas_call(functools.partial(slab_kernel, rim.shape[1], group, rows,...  65.8 us
    ppermute x9, starting transfers between devices, along(): return lax.ppermute(value, 'lon', [(i, (i + d) % n) for i in range(n)])  22.5 us
    pallas_call x1, Pallas kernels, pack_columns(): pl.pallas_call(functools.partial(pack_kernel, count + 3, cols - LANE * hi...  11.4 us
    pallas_call x1, Pallas kernels, filtered_band(): pl.pallas_call(functools.partial(filter_kernel, n), grid_spec=pltpu.Prefe...  10.1 us
    pallas_call x1, Pallas kernels, last_winds(): pl.pallas_call(winds_kernel, grid_spec=pltpu.PrefetchScalarGridSpec(num_s...  8.2 us
    ppermute x4, starting transfers between devices, to_lower(): return lax.ppermute(value, 'lev', [(0, 1)])  6.2 us
    ppermute x9, waiting for transfers between devices, along(): return lax.ppermute(value, 'lon', [(i, (i + d) % n) for i in range(n)])  5.81 us
    pallas_call x1, Pallas kernels, spectra(): pl.pallas_call(functools.partial(spectrum_kernel, n), grid_spec=pltpu.Pre...  4.51 us
  transfers between devices with their start and end apart: 14, of which 4 were waited for; matrix products, arithmetic and copies ran while one was open for 0% of the time, Pallas kernels for 57%

profile of v4, /device:TPU:0, one launch (start us, length us, event | category | flops | bytes accessed | tf_op | source)
XLA Modules:
  0.0 159.8 jit_solution(15646617036623858577)
XLA Ops:
  0.6 1.2 fusion.s
  1.8 3.1 %band_rows.1 = (f32[184,360]{1,0:T(8,128)}, f32[184,360]{1,0:T(8,128)}, f32[184,360]{1,0:T(8,128)}, f32[184,360]{1,0:T(8,128)}) custom-call(s32[10]{0:T(128)} %fusion.s, f32[4,360,360]{2,1,0:T(8,128)} %refs_10_.3, f32[4,360,360]{2,1,0:T(8,128)} %refs_11_.3, f32[4,360,360]{2,1,0:T(8,128)} %refs_9_.3, f32[4,360,360]{2,1,0:T(8,128)} %refs_10_.3, ...), custom_call_target="tpu_custom_call" | custom-call | bytes 9900000 | tf_op jit(solution)/shard_map/band_rows/pallas_call | solution.py:299
  4.9 3.0 %collective-permute-start = (f32[184,360]{1,0:T(8,128)}, f32[184,360]{1,0:T(8,128)S(1)}, u32[]{:S(2)}, u32[]{:S(2)}) collective-permute-start(f32[184,360]{1,0:T(8,128)} %get-tuple-element.54), channel_id=1, source_target_pairs={{0,4},{4,8},{8,12},{12,0},{1,5},{5,9},{9,13},{13,1},{2,6},{6,10},{... | collective-permute-start | bytes 794888 | tf_op jit(solution)/shard_map/ppermute | solution.py:961
  8.0 2.6 %collective-permute-start.1 = (f32[184,360]{1,0:T(8,128)}, f32[184,360]{1,0:T(8,128)S(1)}, u32[]{:S(2)}, u32[]{:S(2)}) collective-permute-start(f32[184,360]{1,0:T(8,128)} %get-tuple-element.55), channel_id=1, source_target_pairs={{0,8},{4,12},{8,0},{12,4},{1,9},{5,13},{9,1},{13,5},{2,10},{6,14},... | collective-permute-start | bytes 794888 | tf_op jit(solution)/shard_map/ppermute | solution.py:961
  10.5 1.3 collective-permute-start.2
  11.9 11.4 %pack_columns.1 = (f32[360,128]{1,0:T(8,128)}, f32[360,128]{1,0:T(8,128)}) custom-call(s32[10]{0:T(128)} %fusion.s, f32[10,4,360,360]{3,2,1,0:T(8,128)} %refs_0_.5, f32[10,4,360,360]{3,2,1,0:T(8,128)} %refs_0_.5, f32[4,360,360]{2,1,0:T(8,128)} %refs_9_.3, f32[4,360,360]{2,1,0:T(8,128)} %refs_9_.3, f32[4,360,360]{2,1,0:T(8,128)} %refs_10_.3, ...), custom_call_target="tpu_custom_call" | custom-call | bytes 33000000 | tf_op jit(solution)/shard_map/pack_columns/pallas_call | solution.py:381
  23.3 0.5 collective-permute-start.3
  23.8 1.6 collective-permute-start.4
  25.4 0.0 collective-permute-done.refs_1_
  25.4 3.8 %collective-permute-done.1.refs_2_ = f32[184,360]{1,0:T(8,128)S(1)} collective-permute-done((f32[184,360]{1,0:T(8,128)}, f32[184,360]{1,0:T(8,128)S(1)}, u32[]{:S(2)}, u32[]{:S(2)}) %collective-permute-start.1) | collective-permute-done | bytes 264992 | tf_op jit(solution)/shard_map/ppermute | solution.py:961
  29.2 0.0 collective-permute-done.2.refs_3_
  29.2 0.0 copy-done.10
  29.2 0.7 copy-done.11
  29.9 0.7 copy-done.12
  30.6 4.5 %spectra.1.refs_0_ = f32[184,384]{1,0:T(8,128)} custom-call(s32[10]{0:T(128)} %fusion.s, f32[184,360]{1,0:T(8,128)} %get-tuple-element.53.refs_0_, f32[184,360]{1,0:T(8,128)} %copy-done.10, f32[184,360]{1,0:T(8,128)} %copy-done.11, f32[184,360]{1,0:T(8,128)} %copy-done.12, f32[4,360,384]{2,1,0:T(8,128)} %constant.25.clone.refs_4_.refs_5_.refs_6_.refs_7_, ...), custom_call_target="tpu_custom_call" | custom-call | bytes 19800000 | tf_op jit(solution)/shard_map/spectra/pallas_call | solution.py:330
  35.2 0.0 collective-permute-done.3.e_top.e_bot.east.refs_5_.refs_12_.refs_6_
  35.2 2.0 %collective-permute-done.4.w_top.w_bot.west.refs_6_.refs_13_.refs_7_ = f32[360,128]{1,0:T(8,128)S(1)} collective-permute-done((f32[360,128]{1,0:T(8,128)}, f32[360,128]{1,0:T(8,128)S(1)}, u32[]{:S(2)}, u32[]{:S(2)}) %collective-permute-start.4) | collective-permute-done | bytes 184352 | tf_op jit(solution)/shard_map/ppermute | solution.py:961
  37.1 0.0 copy-done
  37.1 0.7 copy-done.1
  37.8 4.3 %edge_rows.1 = (f32[4,13,2,384]{3,2,1,0:T(2,128)}, f32[4,13,2,384]{3,2,1,0:T(2,128)}) custom-call(s32[10]{0:T(128)} %fusion.s, f32[10,4,360,360]{3,2,1,0:T(8,128)} %refs_0_.5, f32[10,4,360,360]{3,2,1,0:T(8,128)} %refs_0_.5, f32[4,360,360]{2,1,0:T(8,128)} %refs_9_.3, f32[4,360,360]{2,1,0:T(8,128)} %refs_9_.3, f32[4,360,360]{2,1,0:T(8,128)} %refs_10_.3, ...), custom_call_target="tpu_custom_call" | custom-call | bytes 23100000 | tf_op jit(solution)/shard_map/edge_rows/pallas_call | solution.py:438
  42.1 0.0 copy-start.3
  42.1 0.0 copy-start.16
  42.1 1.6 collective-permute-start.5
  43.7 4.0 %collective-permute-done.5.facing.refs_7_ = f32[4,13,2,384]{3,2,1,0:T(2,128)S(1)} collective-permute-done((f32[4,13,2,384]{3,2,1,0:T(2,128)}, f32[4,13,2,384]{3,2,1,0:T(2,128)S(1)}, u32[]{:S(2)}, u32[]{:S(2)}) %collective-permute-start.5) | collective-permute-done | bytes 159776 | tf_op jit(solution)/shard_map/ppermute | solution.py:978
  47.7 0.7 copy-done.5
  48.3 4.2 %column_sum.1 = f32[3,392,128]{2,1,0:T(8,128)} custom-call(s32[10]{0:T(128)} %fusion.s, f32[4,360,360]{2,1,0:T(8,128)} %refs_9_.3, f32[360,128]{1,0:T(8,128)} %copy-done, f32[360,128]{1,0:T(8,128)} %copy-done.1, f32[4,13,2,384]{3,2,1,0:T(2,128)} %copy-done.5), custom_call_target="tpu_custom_call" | custom-call | bytes 13200000 | tf_op jit(solution)/shard_map/column_sum/pallas_call | solution.py:508
  52.6 1.3 collective-permute-start.6
  53.9 0.0 copy-done.3
  53.9 9.3 %collective-permute-start.7 = (f32[184,384]{1,0:T(8,128)S(1)}, f32[184,384]{1,0:T(8,128)S(1)}, u32[]{:S(2)}, u32[]{:S(2)}) collective-permute-start(f32[184,384]{1,0:T(8,128)S(1)} %copy-done.3), channel_id=1, source_target_pairs={{0,4},{4,8},{8,12},{12,0},{1,5},{5,9},{9,13},{13,1},{2,6},{6,10},{... | collective-permute-start | bytes 847880 | tf_op jit(solution)/shard_map/ppermute | solution.py:961
  63.2 2.7 %collective-permute-start.8 = (f32[184,384]{1,0:T(8,128)S(1)}, f32[184,384]{1,0:T(8,128)S(1)}, u32[]{:S(2)}, u32[]{:S(2)}) collective-permute-start(f32[184,384]{1,0:T(8,128)S(1)} %copy-done.3), channel_id=1, source_target_pairs={{0,8},{4,12},{8,0},{12,4},{1,9},{5,13},{9,1},{13,5},{2,10},{6,14},... | collective-permute-start | bytes 847880 | tf_op jit(solution)/shard_map/ppermute | solution.py:961
  65.8 0.0 collective-permute-start.9
  65.8 0.0 copy-done.16
  65.8 1.5 collective-permute-start.11
  67.4 0.0 collective-permute-done.6.refs_4_.refs_8_
  67.4 0.8 copy-done.2
  68.2 52.2 %tracers_inner.1 = (f32[10,4,360,360]{3,2,1,0:T(8,128)}, f32[4,360,360]{2,1,0:T(8,128)}, f32[4,3,328,128]{3,2,1,0:T(8,128)}, f32[4,3,328,128]{3,2,1,0:T(8,128)},...) custom-call(s32[10]{0:T(128)} %fusion.s, f32[10,4,360,360]{3,2,1,0:T(8,128)} %refs_0_.5, f32[4,360,360]{2,1,0:T(8,128)} %refs_9_.3, ...), custom_call_target="tpu_custom_call" | custom-call | bytes 165000000 | tf_op jit(solution)/shard_map/tracers_inner/pallas_call | solution.py:860
  120.4 0.0 collective-permute-done.7.refs_1_
  120.4 0.0 copy-start.6
  120.4 0.0 collective-permute-done.8.refs_2_
  120.5 0.0 copy-start.7
  120.5 0.0 collective-permute-done.9.refs_3_
  120.5 0.0 copy-start.8
  120.5 1.3 collective-permute-start.12
  121.8 1.3 collective-permute-start.10
  123.1 0.0 copy-done.15
  123.2 0.0 collective-permute-done.11.refs_14_.refs_8_
  123.2 0.0 copy-start.4
  123.2 0.9 collective-permute-done.10.refs_4_
  124.1 0.7 broadcast_in_dim.16.refs_5_
  124.7 0.0 copy-done.6
  124.7 0.0 copy-done.7
  124.8 0.0 copy-done.8
  124.8 0.0 copy-done.4
  124.8 0.0 copy-done.14
  124.8 10.1 %filtered_band.1 = (f32[4,3,96,128]{3,2,1,0:T(8,128)}, f32[4,3,96,128]{3,2,1,0:T(8,128)}, f32[4,3,96,128]{3,2,1,0:T(8,128)}, f32[4,3,96,128]{3,2,1,0:T(8,128)}, ...) custom-call(s32[10]{0:T(128)} %fusion.s, f32[184,384]{1,0:T(8,128)} %spectra.1.refs_0_, ...), custom_call_target="tpu_custom_call" | custom-call | bytes 39600000 | tf_op jit(solution)/shard_map/filtered_band/pallas_call | solution.py:644
  134.9 2.3 %collective-permute-start.13 = (f32[3,96,128]{2,1,0:T(8,128)}, f32[3,96,128]{2,1,0:T(8,128)S(1)}, u32[]{:S(2)}, u32[]{:S(2)}) collective-permute-start(f32[3,96,128]{2,1,0:T(8,128)} %get-tuple-element.83), channel_id=1, source_target_pairs={{0,1},{2,3},{4,5},{6,7},{8,9},{10,11},{12,13},{14,15},{16,17},{18,... | collective-permute-start | bytes 442376 | tf_op jit(solution)/shard_map/ppermute | solution.py:964
  137.1 13.5 %tracers_polar.1 = (f32[10,4,360,360]{3,2,1,0:T(8,128)}, f32[4,360,360]{2,1,0:T(8,128)}) custom-call(s32[10]{0:T(128)} %fusion.s, f32[10,4,360,360]{3,2,1,0:T(8,128)} %refs_0_.5, f32[4,3,96,128]{3,2,1,0:T(8,128)} %get-tuple-element.69.refs_1_, f32[4,3,96,128]{3,2,1,0:T(8,128)} %get-tuple-element.70.refs_2_, ...), custom_call_target="tpu_custom_call", output_to_operand_aliasing={{0}: (10, {}), {1}: (11, {})} | custom-call | bytes 42900000 | tf_op jit(solution)/shard_map/tracers_polar/pallas_call | solution.py:860
  150.7 0.0 collective-permute-done.13.refs_7_
  150.7 0.0 copy-start.13
  150.7 0.0 collective-permute-done.12.refs_3_
  150.7 0.0 copy-start.9
  150.7 0.6 copy-done.13
  151.3 0.3 copy-done.9
  151.6 8.2 %last_winds.1 = (f32[4,360,360]{2,1,0:T(8,128)}, f32[4,360,360]{2,1,0:T(8,128)}) custom-call(s32[10]{0:T(128)} %fusion.s, f32[4,3,328,128]{3,2,1,0:T(8,128)} %get-tuple-element.78.refs_0_, f32[4,3,328,128]{3,2,1,0:T(8,128)} %get-tuple-element.79.refs_1_, f32[4,3,328,128]{3,2,1,0:T(8,128)} %get-tuple-element.80.refs_2_, f32[3,328,128]{2,1,0:T(8,128)} %copy-done.9, ...), custom_call_target="tpu_custom_call" | custom-call | bytes 26400000 | tf_op jit(solution)/shard_map/last_winds/pallas_call | solution.py:909
  (12 shorter events, 0.1 us)
Async XLA Ops:
  4.9 20.5 %collective-permute-start = (f32[184,360]{1,0:T(8,128)}, f32[184,360]{1,0:T(8,128)S(1)}, u32[]{:S(2)}, u32[]{:S(2)}) collective-permute-start(f32[184,360]{1,0:T(8,128)} %get-tuple-element.54), channel_id=1, source_target_pairs={{0,4},{4,8},{8,12},{12,0},{1,5},{5,9},{9,13},{13,1},{2,6},{6,10},{... | collective-permute-start | bytes 794888 | tf_op jit(solution)/shard_map/ppermute | solution.py:961
  8.0 21.3 %collective-permute-start.1 = (f32[184,360]{1,0:T(8,128)}, f32[184,360]{1,0:T(8,128)S(1)}, u32[]{:S(2)}, u32[]{:S(2)}) collective-permute-start(f32[184,360]{1,0:T(8,128)} %get-tuple-element.55), channel_id=1, source_target_pairs={{0,8},{4,12},{8,0},{12,4},{1,9},{5,13},{9,1},{13,5},{2,10},{6,14},... | collective-permute-start | bytes 794888 | tf_op jit(solution)/shard_map/ppermute | solution.py:961
  10.5 18.7 %collective-permute-start.2 = (f32[184,360]{1,0:T(8,128)}, f32[184,360]{1,0:T(8,128)S(1)}, u32[]{:S(2)}, u32[]{:S(2)}) collective-permute-start(f32[184,360]{1,0:T(8,128)} %get-tuple-element.56), channel_id=1, source_target_pairs={{0,12},{4,0},{8,4},{12,8},{1,13},{5,1},{9,5},{13,9},{2,14},{6,2},{... | collective-permute-start | bytes 794888 | tf_op jit(solution)/shard_map/ppermute | solution.py:961
  23.3 11.8 %collective-permute-start.3 = (f32[360,128]{1,0:T(8,128)}, f32[360,128]{1,0:T(8,128)S(1)}, u32[]{:S(2)}, u32[]{:S(2)}) collective-permute-start(f32[360,128]{1,0:T(8,128)} %get-tuple-element.58), channel_id=1, source_target_pairs={{0,12},{4,0},{8,4},{12,8},{1,13},{5,1},{9,5},{13,9},{2,14},{6,2},{... | collective-permute-start | bytes 552968 | tf_op jit(solution)/shard_map/ppermute | solution.py:961
  23.8 13.3 %collective-permute-start.4 = (f32[360,128]{1,0:T(8,128)}, f32[360,128]{1,0:T(8,128)S(1)}, u32[]{:S(2)}, u32[]{:S(2)}) collective-permute-start(f32[360,128]{1,0:T(8,128)} %get-tuple-element.59), channel_id=1, source_target_pairs={{0,4},{4,8},{8,12},{12,0},{1,5},{5,9},{9,13},{13,1},{2,6},{6,10},{... | collective-permute-start | bytes 552968 | tf_op jit(solution)/shard_map/ppermute | solution.py:961
  25.4 3.8 %copy-start.10 = (f32[184,360]{1,0:T(8,128)}, f32[184,360]{1,0:T(8,128)S(1)}, u32[]{:S(2)}) copy-start(f32[184,360]{1,0:T(8,128)S(1)} %collective-permute-done.refs_1_) | copy-start | bytes 794884
  29.2 0.7 copy-start.11
  29.9 0.7 copy-start.12
  35.2 2.0 %copy-start = (f32[360,128]{1,0:T(8,128)}, f32[360,128]{1,0:T(8,128)S(1)}, u32[]{:S(2)}) copy-start(f32[360,128]{1,0:T(8,128)S(1)} %collective-permute-done.3.e_top.e_bot.east.refs_5_.refs_12_.refs_6_) | copy-start | bytes 552964
  37.1 0.7 copy-start.1
  42.1 11.8 %copy-start.3 = (f32[184,384]{1,0:T(8,128)S(1)}, f32[184,384]{1,0:T(8,128)}, u32[]{:S(2)}) copy-start(f32[184,384]{1,0:T(8,128)} %spectra.1.refs_0_) | copy-start | bytes 847876
  42.1 23.7 %copy-start.16 = (f32[4,13,2,384]{3,2,1,0:T(2,128)S(1)}, f32[4,13,2,384]{3,2,1,0:T(2,128)}, u32[]{:S(2)}) copy-start(f32[4,13,2,384]{3,2,1,0:T(2,128)} %get-tuple-element.68) | copy-start | bytes 479236
  42.1 5.6 %collective-permute-start.5 = (f32[4,13,2,384]{3,2,1,0:T(2,128)}, f32[4,13,2,384]{3,2,1,0:T(2,128)S(1)}, u32[]{:S(2)}, u32[]{:S(2)}) collective-permute-start(f32[4,13,2,384]{3,2,1,0:T(2,128)} %get-tuple-element.60), channel_id=1, source_target_pairs={{0,2},{2,0},{1,3},{3,1},{4,6},{6,4},{5,7},{7,5},{8,10},{10,8},{9,1... | collective-permute-start | bytes 479240 | tf_op jit(solution)/shard_map/ppermute | solution.py:978
  47.7 0.7 copy-start.5
  52.6 14.8 %collective-permute-start.6 = (f32[3,392,128]{2,1,0:T(8,128)}, f32[3,392,128]{2,1,0:T(8,128)S(1)}, u32[]{:S(2)}, u32[]{:S(2)}) collective-permute-start(f32[3,392,128]{2,1,0:T(8,128)} %column_sum.1), channel_id=1, source_target_pairs={{0,1},{2,3},{4,5},{6,7},{8,9},{10,11},{12,13},{14,15},{16,17},{18,... | collective-permute-start | bytes 1806344 | tf_op jit(solution)/shard_map/ppermute | solution.py:964
  53.9 66.5 %collective-permute-start.7 = (f32[184,384]{1,0:T(8,128)S(1)}, f32[184,384]{1,0:T(8,128)S(1)}, u32[]{:S(2)}, u32[]{:S(2)}) collective-permute-start(f32[184,384]{1,0:T(8,128)S(1)} %copy-done.3), channel_id=1, source_target_pairs={{0,4},{4,8},{8,12},{12,0},{1,5},{5,9},{9,13},{13,1},{2,6},{6,10},{... | collective-permute-start | bytes 847880 | tf_op jit(solution)/shard_map/ppermute | solution.py:961
  63.2 57.3 %collective-permute-start.8 = (f32[184,384]{1,0:T(8,128)S(1)}, f32[184,384]{1,0:T(8,128)S(1)}, u32[]{:S(2)}, u32[]{:S(2)}) collective-permute-start(f32[184,384]{1,0:T(8,128)S(1)} %copy-done.3), channel_id=1, source_target_pairs={{0,8},{4,12},{8,0},{12,4},{1,9},{5,13},{9,1},{13,5},{2,10},{6,14},... | collective-permute-start | bytes 847880 | tf_op jit(solution)/shard_map/ppermute | solution.py:961
  65.8 54.6 %collective-permute-start.9 = (f32[184,384]{1,0:T(8,128)S(1)}, f32[184,384]{1,0:T(8,128)S(1)}, u32[]{:S(2)}, u32[]{:S(2)}) collective-permute-start(f32[184,384]{1,0:T(8,128)S(1)} %copy-done.3), channel_id=1, source_target_pairs={{0,12},{4,0},{8,4},{12,8},{1,13},{5,1},{9,5},{13,9},{2,14},{6,2},{... | collective-permute-start | bytes 847880 | tf_op jit(solution)/shard_map/ppermute | solution.py:961
  65.8 57.3 %copy-start.15 = (s32[2,60]{1,0:T(2,128)S(1)}, s32[2,60]{1,0:T(2,128)}, u32[]{:S(2)}) copy-start(s32[2,60]{1,0:T(2,128)} %param.14) | copy-start | bytes 1444
  65.8 57.3 %collective-permute-start.11 = (f32[4,13,2,384]{3,2,1,0:T(2,128)S(1)}, f32[4,13,2,384]{3,2,1,0:T(2,128)S(1)}, u32[]{:S(2)}, u32[]{:S(2)}) collective-permute-start(f32[4,13,2,384]{3,2,1,0:T(2,128)S(1)} %copy-done.16), channel_id=1, source_target_pairs={{0,8},{4,12},{8,0},{12,4},{1,9},{5,13},{9,1},{13,5},{2,10},{6,14},... | collective-permute-start | bytes 479240 | tf_op jit(solution)/shard_map/ppermute | solution.py:961
  67.4 0.8 copy-start.2
  120.4 4.3 %copy-start.6 = (f32[184,384]{1,0:T(8,128)}, f32[184,384]{1,0:T(8,128)S(1)}, u32[]{:S(2)}) copy-start(f32[184,384]{1,0:T(8,128)S(1)} %collective-permute-done.7.refs_1_) | copy-start | bytes 847876
  120.5 4.3 %copy-start.7 = (f32[184,384]{1,0:T(8,128)}, f32[184,384]{1,0:T(8,128)S(1)}, u32[]{:S(2)}) copy-start(f32[184,384]{1,0:T(8,128)S(1)} %collective-permute-done.8.refs_2_) | copy-start | bytes 847876
  120.5 4.3 %copy-start.8 = (f32[184,384]{1,0:T(8,128)}, f32[184,384]{1,0:T(8,128)S(1)}, u32[]{:S(2)}) copy-start(f32[184,384]{1,0:T(8,128)S(1)} %collective-permute-done.9.refs_3_) | copy-start | bytes 847876
  120.5 30.2 %collective-permute-start.12 = (f32[3,328,128]{2,1,0:T(8,128)}, f32[3,328,128]{2,1,0:T(8,128)S(1)}, u32[]{:S(2)}, u32[]{:S(2)}) collective-permute-start(f32[3,328,128]{2,1,0:T(8,128)} %get-tuple-element.81), channel_id=1, source_target_pairs={{0,1},{2,3},{4,5},{6,7},{8,9},{10,11},{12,13},{14,15},{16,17},{18,... | collective-permute-start | bytes 1511432 | tf_op jit(solution)/shard_map/ppermute | solution.py:964
  121.8 2.2 %collective-permute-start.10 = (f32[64,384]{1,0:T(8,128)S(1)}, f32[64,384]{1,0:T(8,128)S(1)}, u32[]{:S(2)}, u32[]{:S(2)}) collective-permute-start(f32[64,384]{1,0:T(8,128)S(1)} %slice_add_fusion), channel_id=1, source_target_pairs={{0,1},{2,3},{4,5},{6,7},{8,9},{10,11},{12,13},{14,15},{16,17},{18,... | collective-permute-start | bytes 294920 | tf_op jit(solution)/shard_map/ppermute | solution.py:964
  123.2 1.6 copy-start.4
  124.1 0.7 copy-start.14
  134.9 15.8 %collective-permute-start.13 = (f32[3,96,128]{2,1,0:T(8,128)}, f32[3,96,128]{2,1,0:T(8,128)S(1)}, u32[]{:S(2)}, u32[]{:S(2)}) collective-permute-start(f32[3,96,128]{2,1,0:T(8,128)} %get-tuple-element.83), channel_id=1, source_target_pairs={{0,1},{2,3},{4,5},{6,7},{8,9},{10,11},{12,13},{14,15},{16,17},{18,... | collective-permute-start | bytes 442376 | tf_op jit(solution)/shard_map/ppermute | solution.py:964
  150.7 0.6 copy-start.13
  150.7 0.9 copy-start.9

commit v5 on v4

--- a/solution.py
+++ b/solution.py
@@ -156,7 +156,7 @@
 
 LANE = 128
 POLAR_AT, MIDDLE_AT = 2, 6
-UNROLL = dict(step=8, bring=8, coef=8, one=8, two=8)
+UNROLL = dict(step=13, bring=13, coef=8, one=13, two=12)
 PAD = 16
 BAND = 64
 
@@ -167,6 +167,9 @@
 
 def params(mib=56):
     return pltpu.CompilerParams(vmem_limit_bytes=mib * 1024 * 1024)
+
+
+HELD = pl.BlockSpec(memory_space=pltpu.VMEM)
 
 
 def lanes():
@@ -198,9 +201,8 @@
 
 
 def rim_lanes(east, west, plane, last, lane):
-    to_east = lax.rem(last + LANE - 2 * plane, LANE)
-    to_west = lax.rem(2 * LANE - 2 - 2 * plane, LANE)
-    return jnp.where(lane < last + 2, pltpu.roll(east, to_east, 1), pltpu.roll(west, to_west, 1))
+    both = jnp.where(lane < 2 * plane + 2, east, west)
+    return pltpu.roll(both, lax.rem(last + LANE - 2 * plane, LANE), 1)
 
 
 def inflows(h, u, v, h_n, h_s, v_n, v_s, lane):
@@ -332,7 +334,7 @@
         grid_spec=pltpu.PrefetchScalarGridSpec(
             num_scalar_prefetch=1,
             grid=(1,),
-            in_specs=[pl.BlockSpec((rows, cols), lambda i, s: (0, 0))] * n + [spec(d) for d in range(n)],
+            in_specs=[HELD] * n + [spec(d) for d in range(n)],
             out_specs=pl.BlockSpec((rows, waves), lambda i, s: (0, 0)),
         ),
         out_shape=jax.ShapeDtypeStruct((rows, waves), jnp.float32),
@@ -362,9 +364,9 @@
                 got = jnp.where(mine, turned, got) if f else turned
             base = 2 * fields * l
             to_w = pltpu.roll(got, base, 1) if l else got
-            to_e = pltpu.roll(got, (base - gap) % LANE, 1)
+            to_e = pltpu.roll(got, (base - gap + LANE - 2 - last) % LANE, 1)
             got_w = jnp.where(lane >= base, to_w, got_w) if l else to_w
-            got_e = jnp.where(lane >= base, to_e, got_e) if l else to_e
+            got_e = jnp.where(lane >= base + LANE - 2 - last, to_e, got_e) if l else to_e
         west[here, :] = got_w
         east[here, :] = got_e
 
@@ -394,12 +396,15 @@
 
 
 def rows_kernel(fields, s, t_top, t_bot, h_top, h_bot, u_top, u_bot, v_top, v_bot,
-                e_top, e_bot, w_top, w_bot, pole, facing, top, bot):
+                east, west, pole, facing, top, bot):
     level = pl.program_id(0)
     lane = lanes()
     cols = h_top.shape[2]
     tail = top.shape[2] - LANE
     last = cols - tail
+    height = east.shape[0]
+    e_top, e_bot = east[0:8, :], east[height - 8 :, :]
+    w_top, w_bot = west[0:8, :], west[height - 8 :, :]
     refs = [(t_top, t_bot, (f, 0)) for f in range(fields - 3)]
     refs += [(h_top, h_bot, (0,)), (u_top, u_bot, (0,)), (v_top, v_bot, (0,))]
     for f in range(fields):
@@ -407,8 +412,8 @@
         a, b, lead = refs[f]
         top[f, :, 0:cols] = a[lead]
         bot[f, :, 0:cols] = b[lead]
-        top[f, :, cols:] = rim_lanes(e_top[...], w_top[...], plane, last, lane)[:, last:]
-        bot[f, :, cols:] = rim_lanes(e_bot[...], w_bot[...], plane, last, lane)[:, last:]
+        top[f, :, cols:] = rim_lanes(e_top, w_top, plane, last, lane)[:, last:]
+        bot[f, :, cols:] = rim_lanes(e_bot, w_bot, plane, last, lane)[:, last:]
     flips = [1.0] * (fields - 1) + [-1.0]
 
     @pl.when(s[0] == 1)
@@ -433,22 +438,21 @@
     ends = (0, rows // 8 - 1)
     t_spec = [pl.BlockSpec((count, 1, 8, cols), lambda l, s, r=r: (0, l, r, 0)) for r in ends]
     f_spec = [pl.BlockSpec((1, 8, cols), lambda l, s, r=r: (l, r, 0)) for r in ends]
-    c_spec = [pl.BlockSpec((8, LANE), lambda l, s, r=r: (r, 0)) for r in ends]
     out = jax.ShapeDtypeStruct((levels, fields, 2, width), jnp.float32)
     return pl.pallas_call(
         functools.partial(rows_kernel, fields),
         grid_spec=pltpu.PrefetchScalarGridSpec(
             num_scalar_prefetch=1,
             grid=(levels,),
-            in_specs=t_spec + f_spec * 3 + c_spec * 2,
+            in_specs=t_spec + f_spec * 3 + [HELD] * 2,
             out_specs=[pl.BlockSpec((1, fields, 2, width), lambda l, s: (l, 0, 0, 0))] * 2,
             scratch_shapes=[pltpu.VMEM((fields, 8, width), jnp.float32)] * 2,
         ),
         out_shape=[out, out],
-        cost_estimate=cost(7),
+        cost_estimate=cost(4),
         compiler_params=params(),
         name="edge_rows",
-    )(scalars, tracers, tracers, h, h, u, u, v, v, east, east, west, west)
+    )(scalars, tracers, tracers, h, h, u, u, v, v, east, west)
 
 
 def bring_rows(plane, source, target, here, there, rim, count, last):
@@ -479,22 +483,48 @@
     return zonal, [GRADIENT_COEF * (p_s[c] - p_n[c]) for c in range(count)]
 
 
-def column_kernel(fields, s, h, east, west, facing, total):
-    lane = lanes()
+def column_kernel(h, total):
     levels, rows, cols = h.shape
     count = total.shape[0]
+
+    def body(i):
+        here, there = eight(i), at_row(8 * i + PAD)
+        for c in range(count):
+            wide = min(LANE, cols - c * LANE)
+            part = slice(c * LANE, c * LANE + wide)
+            total[c, there, 0:wide] = sum(h[l, here, part] for l in range(levels))
+
+    sweep(0, rows // 8, body, 9)
+
+
+def column_sum(h):
+    _, rows, cols = h.shape
+    shape = ((cols - 1) // LANE + 1, rows + 2 * PAD, LANE)
+    return pl.pallas_call(
+        column_kernel,
+        out_shape=jax.ShapeDtypeStruct(shape, jnp.float32),
+        in_specs=[pl.BlockSpec(memory_space=pltpu.VMEM)],
+        out_specs=pl.BlockSpec(memory_space=pltpu.VMEM),
+        cost_estimate=cost(3),
+        compiler_params=params(),
+        name="column_sum",
+    )(h)
+
+
+def rims_kernel(fields, cols, s, own, east, west, facing, total):
+    lane = lanes()
+    levels, rows = facing.shape[0], east.shape[0]
+    count = total.shape[0]
     last = cols - LANE * (count - 1)
+    total[0 : count - 1] = own[0 : count - 1]
 
     def body(i):
         here, there = eight(i), at_row(8 * i + PAD)
         e, w = east[here, :], west[here, :]
-        for c in range(count - 1):
-            total[c, there, :] = sum(h[l, here, c * LANE : (c + 1) * LANE] for l in range(levels))
-        total[count - 1, there, 0:last] = sum(h[l, here, LANE * (count - 1) :] for l in range(levels))
-        rim = sum(rim_lanes(e, w, fields * l + fields - 3, last, lane)[:, last:] for l in range(levels))
-        total[count - 1, there, last:] = rim
-
-    sweep(0, rows // 8, body, 5)
+        rim = sum(rim_lanes(e, w, fields * l + fields - 3, last, lane) for l in range(levels))
+        total[count - 1, there, :] = jnp.where(lane < last, own[count - 1, there, :], rim)
+
+    sweep(0, rows // 8, body, 9)
     for c in range(count):
         part = slice(c * LANE, (c + 1) * LANE)
         edge = sum(facing[l, fields - 3, :, part] for l in range(levels))
@@ -502,22 +532,20 @@
         total[c, PAD + rows : PAD + rows + 2, :] = edge
 
 
-def column_sum(scalars, h, east, west, facing):
-    _, rows, cols = h.shape
-    count, tall = (cols - 1) // LANE + 1, rows + 2 * PAD
+def column_rims(scalars, own, cols, east, west, facing):
     return pl.pallas_call(
-        functools.partial(column_kernel, facing.shape[1]),
+        functools.partial(rims_kernel, facing.shape[1], cols),
         grid_spec=pltpu.PrefetchScalarGridSpec(
             num_scalar_prefetch=1,
             grid=(1,),
-            in_specs=[pl.BlockSpec(x.shape, lambda i, s, k=x.ndim: (0,) * k) for x in (h, east, west, facing)],
-            out_specs=pl.BlockSpec((count, tall, LANE), lambda i, s: (0, 0, 0)),
+            in_specs=[HELD] * 4,
+            out_specs=pl.BlockSpec(own.shape, lambda i, s: (0, 0, 0)),
         ),
-        out_shape=jax.ShapeDtypeStruct((count, tall, LANE), jnp.float32),
-        cost_estimate=cost(4),
+        out_shape=jax.ShapeDtypeStruct(own.shape, jnp.float32),
+        cost_estimate=cost(2),
         compiler_params=params(),
-        name="column_sum",
-    )(scalars, h, east, west, facing)
+        name="column_rims",
+    )(scalars, own, east, west, facing)
 
 
 def filter_kernel(n, s, *refs):
@@ -646,17 +674,14 @@
         grid_spec=pltpu.PrefetchScalarGridSpec(
             num_scalar_prefetch=1,
             grid=(1,),
-            in_specs=[pl.BlockSpec((rows, waves), lambda i, s: (0, 0))] * n
+            in_specs=[HELD] * (n + 2)
             + [
-                pl.BlockSpec(above.shape, lambda i, s: (0, 0)),
-                pl.BlockSpec(limits.shape, lambda i, s: (0, 0)),
                 pl.BlockSpec((1, waves, width), lambda i, s: (s[1], 0, 0)),
                 pl.BlockSpec((1, waves, width), lambda i, s: (s[1], 0, 0)),
                 pl.BlockSpec((E(count), E(slab), E(LANE)), lambda i, s: (0, s[POLAR_AT] * 8, 0)),
             ]
             + [raw] * 3
-            + [pl.BlockSpec((height, LANE), lambda i, s: (0, 0))] * 2
-            + [pl.BlockSpec(pole.shape, lambda i, s: (0, 0, 0, 0))],
+            + [HELD] * 3,
             out_specs=[whole] * 6 + [pl.BlockSpec((count, slab, LANE), lambda i, s: (0, 0, 0))],
             scratch_shapes=[
                 pltpu.VMEM((n, rows, waves), jnp.float32),
@@ -729,7 +754,7 @@
 
             def store(c, at, part):
                 for f, out in enumerate((h0, u0, v0)):
-                    out[c, at, :] = rim[0, fields - 3 + f, :, part]
+                    out[c, at, :] = rim[level, fields - 3 + f, :, part]
 
             rims(store)
             pressure_rows(level, above, cum, press, h0, count, rows + 2 * PAD)
@@ -771,7 +796,7 @@
 
     def store(c, at, lanes_of):
         for j in range(group):
-            t0[j, c, at, :] = rim[0, part * group + j, :, lanes_of]
+            t0[j, c, at, :] = rim[level, part * group + j, :, lanes_of]
 
     rims(store)
 
@@ -828,8 +853,7 @@
         in_specs += [pl.BlockSpec((E(tiles), E(slab), E(LANE)), lambda l, g, s: (0, s[place] * 8, 0))]
     else:
         in_specs += [slabs] * 5
-    in_specs += [pl.BlockSpec((height, LANE), lambda l, g, s: (0, 0))] * 2
-    in_specs += [pl.BlockSpec((1,) + rim.shape[1:], lambda l, g, s: (l, 0, 0, 0))]
+    in_specs += [HELD] * 3
     operands = [tracers, *fields, east, west, rim]
     out_specs = [
         pl.BlockSpec((E(group), E(1), E(rows), E(cols)), lambda l, g, s: (g * group, l, s[place] * 8, 0)),
@@ -903,7 +927,7 @@
     for h, _, _, _ in slabs:
         tall = h.shape[2]
         in_specs += [pl.BlockSpec((1, tiles, tall, LANE), lambda l, s: (l, 0, 0, 0))] * 3
-        in_specs += [pl.BlockSpec((tiles, tall, LANE), lambda l, s: (0, 0, 0))]
+        in_specs += [HELD]
         scratch += [pltpu.VMEM((tiles, tall, LANE), jnp.float32)] * 2
     out = jax.ShapeDtypeStruct((levels, rows, cols), jnp.float32)
     return pl.pallas_call(
@@ -963,25 +987,27 @@
     def to_lower(value):
         return lax.ppermute(value, "lev", [(0, 1)])
 
+    fields = (thickness, zonal, meridional)
     sent = band_rows(scalars, zonal, meridional, thickness, n)
     scalars, sent = lax.optimization_barrier((scalars, sent))
     pieces = [sent[0]] + [along(sent[d], d) for d in range(1, n)]
-    packed = pack_columns(scalars, tracers, thickness, zonal, meridional)
-    scalars, packed = lax.optimization_barrier((scalars, packed))
+
+    packed = pack_columns(scalars, tracers, *fields)
+    scalars, packed, deep = lax.optimization_barrier((scalars, packed, thickness))
     east, west = along(packed[0], n - 1), along(packed[1], 1)
+    column = column_sum(deep)
+    scalars, column = lax.optimization_barrier((scalars, column))
 
     own = spectra(scalars, pieces, forward)
     scalars, own = lax.optimization_barrier((scalars, own))
     pieces = [own] + [along(own, d) for d in range(1, n)]
 
-    pole, facing = edge_rows(scalars, tracers, thickness, zonal, meridional, east, west)
+    pole, facing = edge_rows(scalars, tracers, *fields, east, west)
     facing = lax.ppermute(facing, "lat", [(0, 1), (1, 0)])
     pole = along(pole, n // 2)
-    column = column_sum(scalars, thickness, east, west, facing)
-    column = to_lower(column)
+    column = to_lower(column_rims(scalars, column, cols, east, west, facing))
     tr, h2, h1, u1, v1, total = tracer_slab(
-        scalars, MIDDLE_AT, inner, 5, tracers, (thickness, zonal, meridional, column), east, west, facing, None,
-        50, "tracers_inner",
+        scalars, MIDDLE_AT, inner, 5, tracers, (*fields, column), east, west, facing, None, 50, "tracers_inner"
     )
     scalars, total, pieces = lax.optimization_barrier((scalars, total, pieces))
     total = to_lower(total)
@@ -1014,7 +1040,7 @@
         and last - 2 >= LANE // 2
         and last + 2 * (count + 2) <= LANE
         and cols > LANE
-        and 2 * (count + 3) * levels <= LANE
+        and 2 * (count + 3) * levels <= last + 2
         and count % 5 == 0
     )
 

time: 160 us -> 153 us (0.956)
  Pallas kernels: 112 us -> 107 us
  waiting for transfers between devices: 10.7 us -> 8.06 us
    pallas_call x2, Pallas kernels: 65.8 us -> 59.7 us  [tracer_slab(): pl.pallas_call(functools.partial(slab_kernel, rim.shape[1], group, rows,...]
    ppermute x9, waiting for transfers between devices: 5.81 us -> 3.21 us  [along(): return lax.ppermute(value, 'lon', [(i, (i + d) % n) for i in range(n)])]
    pallas_call x1 -> x2, Pallas kernels: 4.22 us -> 5.89 us  [the longest x1 3.3 us: column_rims(): pl.pallas_call(functools.partial(rims_kernel, facing.shape[1], cols), gri...]
    unnamed x34 -> x32, local copies, waits for them, and re-layouts: 4.48 us -> 4.5 us
  transfers between devices with their start and end apart: 14 -> 14, of which waited for: 4 -> 4; matrix products, arithmetic and copies ran while one was open for 0% -> 0% of each run, Pallas kernels for 57% -> 58%
where the time goes in v5:
time: 153 us; the launch traced here: 152 us
  Pallas kernels  107 us (70%)
  starting transfers between devices  30.3 us (20%)
  waiting for transfers between devices  8.06 us (5%)
  local copies, waits for them, and re-layouts  5.18 us (3%)
    pallas_call x2, Pallas kernels, tracer_slab(): pl.pallas_call(functools.partial(slab_kernel, rim.shape[1], group, rows,...  59.7 us
    ppermute x9, starting transfers between devices, along(): return lax.ppermute(value, 'lon', [(i, (i + d) % n) for i in range(n)])  22.5 us
    pallas_call x1, Pallas kernels, pack_columns(): pl.pallas_call(functools.partial(pack_kernel, count + 3, cols - LANE * hi...  11.5 us
    pallas_call x1, Pallas kernels, filtered_band(): pl.pallas_call(functools.partial(filter_kernel, n), grid_spec=pltpu.Prefe...  9.72 us
    pallas_call x1, Pallas kernels, last_winds(): pl.pallas_call(winds_kernel, grid_spec=pltpu.PrefetchScalarGridSpec(num_s...  7.79 us
    ppermute x4, starting transfers between devices, to_lower(): return lax.ppermute(value, 'lev', [(0, 1)])  6.19 us
    pallas_call x1, Pallas kernels, edge_rows(): pl.pallas_call(functools.partial(rows_kernel, fields), grid_spec=pltpu.Pr...  4.55 us
    unnamed x32, local copies, waits for them, and re-layouts  4.5 us
  transfers between devices with their start and end apart: 14, of which 4 were waited for; matrix products, arithmetic and copies ran while one was open for 0% of the time, Pallas kernels for 58%

profile of v5, /device:TPU:0, one launch (start us, length us, event | category | flops | bytes accessed | tf_op | source)
XLA Modules:
  0.0 152.3 jit_solution(7600109711530314184)
XLA Ops:
  0.6 1.2 fusion.s
  1.8 3.1 %band_rows.1 = (f32[184,360]{1,0:T(8,128)}, f32[184,360]{1,0:T(8,128)}, f32[184,360]{1,0:T(8,128)}, f32[184,360]{1,0:T(8,128)}) custom-call(s32[10]{0:T(128)} %fusion.s, f32[4,360,360]{2,1,0:T(8,128)} %refs_10_.3, f32[4,360,360]{2,1,0:T(8,128)} %refs_11_.3, f32[4,360,360]{2,1,0:T(8,128)} %refs_9_.3, f32[4,360,360]{2,1,0:T(8,128)} %refs_10_.3, ...), custom_call_target="tpu_custom_call" | custom-call | bytes 9900000 | tf_op jit(solution)/shard_map/band_rows/pallas_call | solution.py:301
  4.9 3.0 %collective-permute-start = (f32[184,360]{1,0:T(8,128)}, f32[184,360]{1,0:T(8,128)S(1)}, u32[]{:S(2)}, u32[]{:S(2)}) collective-permute-start(f32[184,360]{1,0:T(8,128)} %get-tuple-element.59), channel_id=1, source_target_pairs={{0,4},{4,8},{8,12},{12,0},{1,5},{5,9},{9,13},{13,1},{2,6},{6,10},{... | collective-permute-start | bytes 794888 | tf_op jit(solution)/shard_map/ppermute | solution.py:985
  7.9 2.6 %collective-permute-start.1 = (f32[184,360]{1,0:T(8,128)}, f32[184,360]{1,0:T(8,128)S(1)}, u32[]{:S(2)}, u32[]{:S(2)}) collective-permute-start(f32[184,360]{1,0:T(8,128)} %get-tuple-element.60), channel_id=1, source_target_pairs={{0,8},{4,12},{8,0},{12,4},{1,9},{5,13},{9,1},{13,5},{2,10},{6,14},... | collective-permute-start | bytes 794888 | tf_op jit(solution)/shard_map/ppermute | solution.py:985
  10.5 1.3 collective-permute-start.2
  11.9 11.5 %pack_columns.1 = (f32[360,128]{1,0:T(8,128)}, f32[360,128]{1,0:T(8,128)}) custom-call(s32[10]{0:T(128)} %fusion.s, f32[10,4,360,360]{3,2,1,0:T(8,128)} %refs_0_.5, f32[10,4,360,360]{3,2,1,0:T(8,128)} %refs_0_.5, f32[4,360,360]{2,1,0:T(8,128)} %refs_9_.3, f32[4,360,360]{2,1,0:T(8,128)} %refs_9_.3, f32[4,360,360]{2,1,0:T(8,128)} %refs_10_.3, ...), custom_call_target="tpu_custom_call" | custom-call | bytes 33000000 | tf_op jit(solution)/shard_map/pack_columns/pallas_call | solution.py:383
  23.3 0.5 collective-permute-start.3
  23.8 1.6 %collective-permute-start.4 = (f32[360,128]{1,0:T(8,128)}, f32[360,128]{1,0:T(8,128)S(1)}, u32[]{:S(2)}, u32[]{:S(2)}) collective-permute-start(f32[360,128]{1,0:T(8,128)} %get-tuple-element.65), channel_id=1, source_target_pairs={{0,4},{4,8},{8,12},{12,0},{1,5},{5,9},{9,13},{13,1},{2,6},{6,10},{... | collective-permute-start | bytes 552968 | tf_op jit(solution)/shard_map/ppermute | solution.py:985
  25.4 2.6 %column_sum.1.own = f32[3,392,128]{2,1,0:T(8,128)} custom-call(f32[4,360,360]{2,1,0:T(8,128)} %refs_9_.3), custom_call_target="tpu_custom_call" | custom-call | bytes 9900000 | tf_op jit(solution)/shard_map/column_sum/pallas_call | solution.py:503
  28.0 0.0 collective-permute-done.refs_1_
  28.0 0.0 copy-start.10
  28.0 1.2 collective-permute-done.1.refs_2_
  29.2 0.0 copy-start.11
  29.2 0.0 collective-permute-done.2.refs_3_
  29.2 0.0 copy-done.10
  29.2 0.7 copy-done.11
  29.9 0.7 copy-done.12
  30.7 4.5 %spectra.1.refs_0_ = f32[184,384]{1,0:T(8,128)} custom-call(s32[10]{0:T(128)} %fusion.s, f32[184,360]{1,0:T(8,128)} %get-tuple-element.58.refs_0_, f32[184,360]{1,0:T(8,128)} %copy-done.10, f32[184,360]{1,0:T(8,128)} %copy-done.11, f32[184,360]{1,0:T(8,128)} %copy-done.12, f32[4,360,384]{2,1,0:T(8,128)} %constant.25.clone.refs_4_.refs_5_.refs_6_.refs_7_, ...), custom_call_target="tpu_custom_call" | custom-call | bytes 19800000 | tf_op jit(solution)/shard_map/spectra/pallas_call | solution.py:332
  35.2 0.0 collective-permute-done.3.east.refs_5_.refs_12_.refs_6_
  35.2 2.0 %collective-permute-done.4.west.refs_6_.refs_13_.refs_7_ = f32[360,128]{1,0:T(8,128)S(1)} collective-permute-done((f32[360,128]{1,0:T(8,128)}, f32[360,128]{1,0:T(8,128)S(1)}, u32[]{:S(2)}, u32[]{:S(2)}) %collective-permute-start.4) | collective-permute-done | bytes 184352 | tf_op jit(solution)/shard_map/ppermute | solution.py:985
  37.1 0.0 copy-done
  37.1 0.7 copy-done.1
  37.8 4.5 %edge_rows.1 = (f32[4,13,2,384]{3,2,1,0:T(2,128)}, f32[4,13,2,384]{3,2,1,0:T(2,128)}) custom-call(s32[10]{0:T(128)} %fusion.s, f32[10,4,360,360]{3,2,1,0:T(8,128)} %refs_0_.5, f32[10,4,360,360]{3,2,1,0:T(8,128)} %refs_0_.5, f32[4,360,360]{2,1,0:T(8,128)} %refs_9_.3, f32[4,360,360]{2,1,0:T(8,128)} %refs_9_.3, f32[4,360,360]{2,1,0:T(8,128)} %refs_10_.3, ...), custom_call_target="tpu_custom_call" | custom-call | bytes 13200000 | tf_op jit(solution)/shard_map/edge_rows/pallas_call | solution.py:442
  42.4 1.6 %collective-permute-start.5 = (f32[4,13,2,384]{3,2,1,0:T(2,128)}, f32[4,13,2,384]{3,2,1,0:T(2,128)S(1)}, u32[]{:S(2)}, u32[]{:S(2)}) collective-permute-start(f32[4,13,2,384]{3,2,1,0:T(2,128)} %get-tuple-element.66), channel_id=1, source_target_pairs={{0,2},{2,0},{1,3},{3,1},{4,6},{6,4},{5,7},{7,5},{8,10},{10,8},{9,1... | collective-permute-start | bytes 479240 | tf_op jit(solution)/shard_map/ppermute | solution.py:1006
  43.9 4.0 %collective-permute-done.5.facing.refs_7_ = f32[4,13,2,384]{3,2,1,0:T(2,128)S(1)} collective-permute-done((f32[4,13,2,384]{3,2,1,0:T(2,128)}, f32[4,13,2,384]{3,2,1,0:T(2,128)S(1)}, u32[]{:S(2)}, u32[]{:S(2)}) %collective-permute-start.5) | collective-permute-done | bytes 159776 | tf_op jit(solution)/shard_map/ppermute | solution.py:1006
  47.9 0.7 copy-done.5
  48.6 3.3 %column_rims.1 = f32[3,392,128]{2,1,0:T(8,128)} custom-call(s32[10]{0:T(128)} %fusion.s, f32[3,392,128]{2,1,0:T(8,128)} %column_sum.1.own, f32[360,128]{1,0:T(8,128)} %copy-done, f32[360,128]{1,0:T(8,128)} %copy-done.1, f32[4,13,2,384]{3,2,1,0:T(2,128)} %copy-done.5), custom_call_target="tpu_custom_call" | custom-call | bytes 6600000 | tf_op jit(solution)/shard_map/column_rims/pallas_call | solution.py:536
  51.9 1.3 collective-permute-start.6
  53.2 0.0 copy-done.3
  53.2 9.3 %collective-permute-start.7 = (f32[184,384]{1,0:T(8,128)S(1)}, f32[184,384]{1,0:T(8,128)S(1)}, u32[]{:S(2)}, u32[]{:S(2)}) collective-permute-start(f32[184,384]{1,0:T(8,128)S(1)} %copy-done.3), channel_id=1, source_target_pairs={{0,4},{4,8},{8,12},{12,0},{1,5},{5,9},{9,13},{13,1},{2,6},{6,10},{... | collective-permute-start | bytes 847880 | tf_op jit(solution)/shard_map/ppermute | solution.py:985
  62.5 2.7 %collective-permute-start.8 = (f32[184,384]{1,0:T(8,128)S(1)}, f32[184,384]{1,0:T(8,128)S(1)}, u32[]{:S(2)}, u32[]{:S(2)}) collective-permute-start(f32[184,384]{1,0:T(8,128)S(1)} %copy-done.3), channel_id=1, source_target_pairs={{0,8},{4,12},{8,0},{12,4},{1,9},{5,13},{9,1},{13,5},{2,10},{6,14},... | collective-permute-start | bytes 847880 | tf_op jit(solution)/shard_map/ppermute | solution.py:985
  65.2 0.0 collective-permute-start.9
  65.2 1.5 %collective-permute-start.11 = (f32[4,13,2,384]{3,2,1,0:T(2,128)}, f32[4,13,2,384]{3,2,1,0:T(2,128)S(1)}, u32[]{:S(2)}, u32[]{:S(2)}) collective-permute-start(f32[4,13,2,384]{3,2,1,0:T(2,128)} %get-tuple-element.74), channel_id=1, source_target_pairs={{0,8},{4,12},{8,0},{12,4},{1,9},{5,13},{9,1},{13,5},{2,10},{6,14},... | collective-permute-start | bytes 479240 | tf_op jit(solution)/shard_map/ppermute | solution.py:985
  66.7 0.0 collective-permute-done.6.refs_4_.refs_8_
  66.7 0.8 copy-done.2
  67.5 46.4 %tracers_inner.1 = (f32[10,4,360,360]{3,2,1,0:T(8,128)}, f32[4,360,360]{2,1,0:T(8,128)}, f32[4,3,328,128]{3,2,1,0:T(8,128)}, f32[4,3,328,128]{3,2,1,0:T(8,128)},...) custom-call(s32[10]{0:T(128)} %fusion.s, f32[10,4,360,360]{3,2,1,0:T(8,128)} %refs_0_.5, f32[4,360,360]{2,1,0:T(8,128)} %refs_9_.3, ...), custom_call_target="tpu_custom_call" | custom-call | bytes 165000000 | tf_op jit(solution)/shard_map/tracers_inner/pallas_call | solution.py:884
  114.0 0.0 collective-permute-done.7.refs_1_
  114.0 0.0 copy-start.6
  114.0 0.0 collective-permute-done.8.refs_2_
  114.0 0.0 copy-start.7
  114.0 0.0 collective-permute-done.9.refs_3_
  114.0 0.0 copy-start.8
  114.0 1.3 collective-permute-start.12
  115.4 1.3 collective-permute-start.10
  116.7 0.0 copy-done.15
  116.7 0.0 collective-permute-done.11.refs_14_.refs_8_
  116.7 0.0 copy-start.4
  116.7 0.9 collective-permute-done.10.refs_4_
  117.6 0.7 broadcast_in_dim.16.refs_5_
  118.3 0.0 copy-done.6
  118.3 0.0 copy-done.7
  118.3 0.0 copy-done.8
  118.3 0.0 copy-done.4
  118.3 0.0 copy-done.14
  118.3 9.7 %filtered_band.1 = (f32[4,3,96,128]{3,2,1,0:T(8,128)}, f32[4,3,96,128]{3,2,1,0:T(8,128)}, f32[4,3,96,128]{3,2,1,0:T(8,128)}, f32[4,3,96,128]{3,2,1,0:T(8,128)}, ...) custom-call(s32[10]{0:T(128)} %fusion.s, f32[184,384]{1,0:T(8,128)} %spectra.1.refs_0_, ...), custom_call_target="tpu_custom_call" | custom-call | bytes 39600000 | tf_op jit(solution)/shard_map/filtered_band/pallas_call | solution.py:672
  128.0 2.3 %collective-permute-start.13 = (f32[3,96,128]{2,1,0:T(8,128)}, f32[3,96,128]{2,1,0:T(8,128)S(1)}, u32[]{:S(2)}, u32[]{:S(2)}) collective-permute-start(f32[3,96,128]{2,1,0:T(8,128)} %get-tuple-element.89), channel_id=1, source_target_pairs={{0,1},{2,3},{4,5},{6,7},{8,9},{10,11},{12,13},{14,15},{16,17},{18,... | collective-permute-start | bytes 442376 | tf_op jit(solution)/shard_map/ppermute | solution.py:988
  130.3 13.3 %tracers_polar.1 = (f32[10,4,360,360]{3,2,1,0:T(8,128)}, f32[4,360,360]{2,1,0:T(8,128)}) custom-call(s32[10]{0:T(128)} %fusion.s, f32[10,4,360,360]{3,2,1,0:T(8,128)} %refs_0_.5, f32[4,3,96,128]{3,2,1,0:T(8,128)} %get-tuple-element.75.refs_1_, f32[4,3,96,128]{3,2,1,0:T(8,128)} %get-tuple-element.76.refs_2_, ...), custom_call_target="tpu_custom_call", output_to_operand_aliasing={{0}: (10, {}), {1}: (11, {})} | custom-call | bytes 42900000 | tf_op jit(solution)/shard_map/tracers_polar/pallas_call | solution.py:884
  143.6 0.0 collective-permute-done.13.refs_7_
  143.6 0.0 copy-start.13
  143.6 0.0 collective-permute-done.12.refs_3_
  143.6 0.0 copy-start.9
  143.7 0.6 copy-done.13
  144.3 0.2 copy-done.9
  144.5 7.8 %last_winds.1 = (f32[4,360,360]{2,1,0:T(8,128)}, f32[4,360,360]{2,1,0:T(8,128)}) custom-call(s32[10]{0:T(128)} %fusion.s, f32[4,3,328,128]{3,2,1,0:T(8,128)} %get-tuple-element.84.refs_0_, f32[4,3,328,128]{3,2,1,0:T(8,128)} %get-tuple-element.85.refs_1_, f32[4,3,328,128]{3,2,1,0:T(8,128)} %get-tuple-element.86.refs_2_, f32[3,328,128]{2,1,0:T(8,128)} %copy-done.9, ...), custom_call_target="tpu_custom_call" | custom-call | bytes 26400000 | tf_op jit(solution)/shard_map/last_winds/pallas_call | solution.py:933
  (11 shorter events, 0.1 us)
Async XLA Ops:
  4.9 23.1 %collective-permute-start = (f32[184,360]{1,0:T(8,128)}, f32[184,360]{1,0:T(8,128)S(1)}, u32[]{:S(2)}, u32[]{:S(2)}) collective-permute-start(f32[184,360]{1,0:T(8,128)} %get-tuple-element.59), channel_id=1, source_target_pairs={{0,4},{4,8},{8,12},{12,0},{1,5},{5,9},{9,13},{13,1},{2,6},{6,10},{... | collective-permute-start | bytes 794888 | tf_op jit(solution)/shard_map/ppermute | solution.py:985
  7.9 21.3 %collective-permute-start.1 = (f32[184,360]{1,0:T(8,128)}, f32[184,360]{1,0:T(8,128)S(1)}, u32[]{:S(2)}, u32[]{:S(2)}) collective-permute-start(f32[184,360]{1,0:T(8,128)} %get-tuple-element.60), channel_id=1, source_target_pairs={{0,8},{4,12},{8,0},{12,4},{1,9},{5,13},{9,1},{13,5},{2,10},{6,14},... | collective-permute-start | bytes 794888 | tf_op jit(solution)/shard_map/ppermute | solution.py:985
  10.5 18.7 %collective-permute-start.2 = (f32[184,360]{1,0:T(8,128)}, f32[184,360]{1,0:T(8,128)S(1)}, u32[]{:S(2)}, u32[]{:S(2)}) collective-permute-start(f32[184,360]{1,0:T(8,128)} %get-tuple-element.61), channel_id=1, source_target_pairs={{0,12},{4,0},{8,4},{12,8},{1,13},{5,1},{9,5},{13,9},{2,14},{6,2},{... | collective-permute-start | bytes 794888 | tf_op jit(solution)/shard_map/ppermute | solution.py:985
  23.3 11.8 %collective-permute-start.3 = (f32[360,128]{1,0:T(8,128)}, f32[360,128]{1,0:T(8,128)S(1)}, u32[]{:S(2)}, u32[]{:S(2)}) collective-permute-start(f32[360,128]{1,0:T(8,128)} %get-tuple-element.64), channel_id=1, source_target_pairs={{0,12},{4,0},{8,4},{12,8},{1,13},{5,1},{9,5},{13,9},{2,14},{6,2},{... | collective-permute-start | bytes 552968 | tf_op jit(solution)/shard_map/ppermute | solution.py:985
  23.8 13.3 %collective-permute-start.4 = (f32[360,128]{1,0:T(8,128)}, f32[360,128]{1,0:T(8,128)S(1)}, u32[]{:S(2)}, u32[]{:S(2)}) collective-permute-start(f32[360,128]{1,0:T(8,128)} %get-tuple-element.65), channel_id=1, source_target_pairs={{0,4},{4,8},{8,12},{12,0},{1,5},{5,9},{9,13},{13,1},{2,6},{6,10},{... | collective-permute-start | bytes 552968 | tf_op jit(solution)/shard_map/ppermute | solution.py:985
  28.0 1.2 copy-start.10
  29.2 0.7 copy-start.11
  29.9 0.7 copy-start.12
  35.1 18.0 %copy-start.3 = (f32[184,384]{1,0:T(8,128)S(1)}, f32[184,384]{1,0:T(8,128)}, u32[]{:S(2)}) copy-start(f32[184,384]{1,0:T(8,128)} %spectra.1.refs_0_) | copy-start | bytes 847876
  35.2 2.0 %copy-start = (f32[360,128]{1,0:T(8,128)}, f32[360,128]{1,0:T(8,128)S(1)}, u32[]{:S(2)}) copy-start(f32[360,128]{1,0:T(8,128)S(1)} %collective-permute-done.3.east.refs_5_.refs_12_.refs_6_) | copy-start | bytes 552964
  37.1 0.7 copy-start.1
  42.4 5.5 %collective-permute-start.5 = (f32[4,13,2,384]{3,2,1,0:T(2,128)}, f32[4,13,2,384]{3,2,1,0:T(2,128)S(1)}, u32[]{:S(2)}, u32[]{:S(2)}) collective-permute-start(f32[4,13,2,384]{3,2,1,0:T(2,128)} %get-tuple-element.66), channel_id=1, source_target_pairs={{0,2},{2,0},{1,3},{3,1},{4,6},{6,4},{5,7},{7,5},{8,10},{10,8},{9,1... | collective-permute-start | bytes 479240 | tf_op jit(solution)/shard_map/ppermute | solution.py:1006
  47.9 0.7 copy-start.5
  51.9 14.8 %collective-permute-start.6 = (f32[3,392,128]{2,1,0:T(8,128)}, f32[3,392,128]{2,1,0:T(8,128)S(1)}, u32[]{:S(2)}, u32[]{:S(2)}) collective-permute-start(f32[3,392,128]{2,1,0:T(8,128)} %column_rims.1), channel_id=1, source_target_pairs={{0,1},{2,3},{4,5},{6,7},{8,9},{10,11},{12,13},{14,15},{16,17},{18,... | collective-permute-start | bytes 1806344 | tf_op jit(solution)/shard_map/ppermute | solution.py:988
  53.2 60.8 %collective-permute-start.7 = (f32[184,384]{1,0:T(8,128)S(1)}, f32[184,384]{1,0:T(8,128)S(1)}, u32[]{:S(2)}, u32[]{:S(2)}) collective-permute-start(f32[184,384]{1,0:T(8,128)S(1)} %copy-done.3), channel_id=1, source_target_pairs={{0,4},{4,8},{8,12},{12,0},{1,5},{5,9},{9,13},{13,1},{2,6},{6,10},{... | collective-permute-start | bytes 847880 | tf_op jit(solution)/shard_map/ppermute | solution.py:985
  62.5 51.5 %collective-permute-start.8 = (f32[184,384]{1,0:T(8,128)S(1)}, f32[184,384]{1,0:T(8,128)S(1)}, u32[]{:S(2)}, u32[]{:S(2)}) collective-permute-start(f32[184,384]{1,0:T(8,128)S(1)} %copy-done.3), channel_id=1, source_target_pairs={{0,8},{4,12},{8,0},{12,4},{1,9},{5,13},{9,1},{13,5},{2,10},{6,14},... | collective-permute-start | bytes 847880 | tf_op jit(solution)/shard_map/ppermute | solution.py:985
  65.2 48.8 %collective-permute-start.9 = (f32[184,384]{1,0:T(8,128)S(1)}, f32[184,384]{1,0:T(8,128)S(1)}, u32[]{:S(2)}, u32[]{:S(2)}) collective-permute-start(f32[184,384]{1,0:T(8,128)S(1)} %copy-done.3), channel_id=1, source_target_pairs={{0,12},{4,0},{8,4},{12,8},{1,13},{5,1},{9,5},{13,9},{2,14},{6,2},{... | collective-permute-start | bytes 847880 | tf_op jit(solution)/shard_map/ppermute | solution.py:985
  65.2 51.5 %copy-start.15 = (s32[2,60]{1,0:T(2,128)S(1)}, s32[2,60]{1,0:T(2,128)}, u32[]{:S(2)}) copy-start(s32[2,60]{1,0:T(2,128)} %param.14) | copy-start | bytes 1444
  65.2 51.6 %collective-permute-start.11 = (f32[4,13,2,384]{3,2,1,0:T(2,128)}, f32[4,13,2,384]{3,2,1,0:T(2,128)S(1)}, u32[]{:S(2)}, u32[]{:S(2)}) collective-permute-start(f32[4,13,2,384]{3,2,1,0:T(2,128)} %get-tuple-element.74), channel_id=1, source_target_pairs={{0,8},{4,12},{8,0},{12,4},{1,9},{5,13},{9,1},{13,5},{2,10},{6,14},... | collective-permute-start | bytes 479240 | tf_op jit(solution)/shard_map/ppermute | solution.py:985
  66.7 0.8 copy-start.2
  114.0 4.3 %copy-start.6 = (f32[184,384]{1,0:T(8,128)}, f32[184,384]{1,0:T(8,128)S(1)}, u32[]{:S(2)}) copy-start(f32[184,384]{1,0:T(8,128)S(1)} %collective-permute-done.7.refs_1_) | copy-start | bytes 847876
  114.0 4.3 %copy-start.7 = (f32[184,384]{1,0:T(8,128)}, f32[184,384]{1,0:T(8,128)S(1)}, u32[]{:S(2)}) copy-start(f32[184,384]{1,0:T(8,128)S(1)} %collective-permute-done.8.refs_2_) | copy-start | bytes 847876
  114.0 4.3 %copy-start.8 = (f32[184,384]{1,0:T(8,128)}, f32[184,384]{1,0:T(8,128)S(1)}, u32[]{:S(2)}) copy-start(f32[184,384]{1,0:T(8,128)S(1)} %collective-permute-done.9.refs_3_) | copy-start | bytes 847876
  114.0 29.6 %collective-permute-start.12 = (f32[3,328,128]{2,1,0:T(8,128)}, f32[3,328,128]{2,1,0:T(8,128)S(1)}, u32[]{:S(2)}, u32[]{:S(2)}) collective-permute-start(f32[3,328,128]{2,1,0:T(8,128)} %get-tuple-element.87), channel_id=1, source_target_pairs={{0,1},{2,3},{4,5},{6,7},{8,9},{10,11},{12,13},{14,15},{16,17},{18,... | collective-permute-start | bytes 1511432 | tf_op jit(solution)/shard_map/ppermute | solution.py:988
  115.4 2.2 %collective-permute-start.10 = (f32[64,384]{1,0:T(8,128)S(1)}, f32[64,384]{1,0:T(8,128)S(1)}, u32[]{:S(2)}, u32[]{:S(2)}) collective-permute-start(f32[64,384]{1,0:T(8,128)S(1)} %slice_add_fusion), channel_id=1, source_target_pairs={{0,1},{2,3},{4,5},{6,7},{8,9},{10,11},{12,13},{14,15},{16,17},{18,... | collective-permute-start | bytes 294920 | tf_op jit(solution)/shard_map/ppermute | solution.py:988
  116.7 1.6 %copy-start.4 = (f32[4,13,2,384]{3,2,1,0:T(2,128)}, f32[4,13,2,384]{3,2,1,0:T(2,128)S(1)}, u32[]{:S(2)}) copy-start(f32[4,13,2,384]{3,2,1,0:T(2,128)S(1)} %collective-permute-done.11.refs_14_.refs_8_) | copy-start | bytes 479236
  117.6 0.7 copy-start.14
  128.0 15.6 %collective-permute-start.13 = (f32[3,96,128]{2,1,0:T(8,128)}, f32[3,96,128]{2,1,0:T(8,128)S(1)}, u32[]{:S(2)}, u32[]{:S(2)}) collective-permute-start(f32[3,96,128]{2,1,0:T(8,128)} %get-tuple-element.89), channel_id=1, source_target_pairs={{0,1},{2,3},{4,5},{6,7},{8,9},{10,11},{12,13},{14,15},{16,17},{18,... | collective-permute-start | bytes 442376 | tf_op jit(solution)/shard_map/ppermute | solution.py:988
  143.6 0.7 copy-start.13
  143.6 0.9 copy-start.9

commit v6 on v5

--- a/solution.py
+++ b/solution.py
@@ -550,9 +550,9 @@
 
 def filter_kernel(n, s, *refs):
     pieces = refs[:n]
-    above, limits, basis, slope, column, h, u, v, east, west, pole = refs[n : n + 11]
-    h0_out, u0_out, v0_out, u1_out, v1_out, h1_out, total = refs[n + 11 : n + 18]
-    held, lhs, rhs, cum, press = refs[n + 18 :]
+    limits, basis, slope, column, h, u, v, east, west, pole = refs[n : n + 10]
+    h0_out, u0_out, v0_out, u1_out, v1_out, h1_out, total = refs[n + 10 : n + 17]
+    held, lhs, rhs, cum, press = refs[n + 17 :]
     levels, count, slab = u0_out.shape[:3]
     cols = h.shape[2]
     last = cols - LANE * (count - 1)
@@ -605,6 +605,7 @@
 
         @pl.when(s[0] == int(north))
         def _():
+            after = 3 * POLAR + 4
             first = PAD if north else PAD + BAND - POLAR
             rim = PAD - 2 if north else PAD + BAND
 
@@ -645,7 +646,8 @@
                     v1_out[l, c, rim : rim + 2, :] = back[3 * POLAR + 4 : 3 * POLAR + 6, part]
                 return cum + thick
 
-            lax.fori_loop(0, levels, level_step, above[0 : POLAR + 1, :])
+            upper = sum(pieces[d][after : after + POLAR + 1, :] for d in range(n))
+            lax.fori_loop(0, levels, level_step, upper)
 
     def step(k):
         l, i = k // (slab // 8 - 2), lax.rem(k, slab // 8 - 2) + 1
@@ -658,7 +660,7 @@
     sweep(0, levels * (slab // 8 - 2), step, UNROLL["step"])
 
 
-def filtered_band(scalars, pieces, above, limits, basis, slope, column, h, u, v, east, west, pole):
+def filtered_band(scalars, pieces, limits, basis, slope, column, h, u, v, east, west, pole):
     n = len(pieces)
     rows, waves = pieces[0].shape
     width = basis.shape[2]
@@ -674,7 +676,7 @@
         grid_spec=pltpu.PrefetchScalarGridSpec(
             num_scalar_prefetch=1,
             grid=(1,),
-            in_specs=[HELD] * (n + 2)
+            in_specs=[HELD] * (n + 1)
             + [
                 pl.BlockSpec((1, waves, width), lambda i, s: (s[1], 0, 0)),
                 pl.BlockSpec((1, waves, width), lambda i, s: (s[1], 0, 0)),
@@ -694,7 +696,7 @@
         cost_estimate=cost(12),
         compiler_params=params(),
         name="filtered_band",
-    )(scalars, *pieces, above, limits, basis, slope, column, h, u, v, east, west, pole)
+    )(scalars, *pieces, limits, basis, slope, column, h, u, v, east, west, pole)
 
 
 def slab_kernel(fields, group, rows, place, inner, s, *refs):
@@ -996,24 +998,28 @@
     scalars, packed, deep = lax.optimization_barrier((scalars, packed, thickness))
     east, west = along(packed[0], n - 1), along(packed[1], 1)
     column = column_sum(deep)
-    scalars, column = lax.optimization_barrier((scalars, column))
+    scalars, column, pieces = lax.optimization_barrier((scalars, column, pieces))
+
+    pole, facing = edge_rows(scalars, tracers, *fields, east, west)
+    scalars, pole, facing = lax.optimization_barrier((scalars, pole, facing))
+    facing = lax.ppermute(facing, "lat", [(0, 1), (1, 0)])
+    pole = along(pole, n // 2)
 
     own = spectra(scalars, pieces, forward)
     scalars, own = lax.optimization_barrier((scalars, own))
+    upper = to_lower(own[2 * POLAR :])
+    column = column_rims(scalars, column, cols, east, west, facing)
+    scalars, column, upper = lax.optimization_barrier((scalars, column, upper))
+    column = to_lower(column)
+    own = jnp.concatenate([own, upper], 0)
     pieces = [own] + [along(own, d) for d in range(1, n)]
-
-    pole, facing = edge_rows(scalars, tracers, *fields, east, west)
-    facing = lax.ppermute(facing, "lat", [(0, 1), (1, 0)])
-    pole = along(pole, n // 2)
-    column = to_lower(column_rims(scalars, column, cols, east, west, facing))
     tr, h2, h1, u1, v1, total = tracer_slab(
-        scalars, MIDDLE_AT, inner, 5, tracers, (*fields, column), east, west, facing, None, 50, "tracers_inner"
-    )
-    scalars, total, pieces = lax.optimization_barrier((scalars, total, pieces))
+        scalars, MIDDLE_AT, inner, 10, tracers, (*fields, column), east, west, facing, None, 50, "tracers_inner"
+    )
+    scalars, total, pieces, pole = lax.optimization_barrier((scalars, total, pieces, pole))
     total = to_lower(total)
-    above_band = to_lower(sum(p[2 * POLAR :] for p in pieces))
     h0, u0, v0, u1b, v1b, h1b, band_total = filtered_band(
-        scalars, pieces, above_band, limits, inverse, slope, column, thickness, zonal, meridional, east, west, pole
+        scalars, pieces, limits, inverse, slope, column, thickness, zonal, meridional, east, west, pole
     )
     band_total = to_lower(band_total)
     tr, h2 = tracer_slab(
@@ -1041,7 +1047,7 @@
         and last + 2 * (count + 2) <= LANE
         and cols > LANE
         and 2 * (count + 3) * levels <= last + 2
-        and count % 5 == 0
+        and count % 10 == 0
     )
 
 

time: 153 us -> 149 us (0.974)
  starting transfers between devices: 30.3 us -> 26.5 us
  Pallas kernels: 107 us -> 105 us
    ppermute x9, waiting for transfers between devices: 3.21 us -> 9.14 us  [along(): return lax.ppermute(value, 'lon', [(i, (i + d) % n) for i in range(n)])]
    ppermute x1, waiting for transfers between devices: 3.99 us -> 0.01 us  [shards_tiled(): facing = lax.ppermute(facing, 'lat', [(0, 1), (1, 0)])]
    ppermute x9, starting transfers between devices: 22.5 us -> 19.6 us  [along(): return lax.ppermute(value, 'lon', [(i, (i + d) % n) for i in range(n)])]
    pallas_call x2, Pallas kernels: 59.7 us -> 57.8 us  [tracer_slab(): pl.pallas_call(functools.partial(slab_kernel, rim.shape[1], group, rows,...]
    unnamed x32 -> x33, local copies, waits for them, and re-layouts: 4.5 us -> 4.05 us
  transfers between devices with their start and end apart: 14 -> 14, of which waited for: 4 -> 3; matrix products, arithmetic and copies ran while one was open for 0% -> 2% of each run, Pallas kernels for 58% -> 60%
where the time goes in v6:
time: 149 us; the launch traced here: 148 us
  Pallas kernels  105 us (70%)
  starting transfers between devices  26.5 us (18%)
  waiting for transfers between devices  9.15 us (6%)
  local copies, waits for them, and re-layouts  5.67 us (4%)
    pallas_call x2, Pallas kernels, tracer_slab(): pl.pallas_call(functools.partial(slab_kernel, rim.shape[1], group, rows,...  57.8 us
    ppermute x9, starting transfers between devices, along(): return lax.ppermute(value, 'lon', [(i, (i + d) % n) for i in range(n)])  19.6 us
    pallas_call x1, Pallas kernels, pack_columns(): pl.pallas_call(functools.partial(pack_kernel, count + 3, cols - LANE * hi...  11.5 us
    pallas_call x1, Pallas kernels, filtered_band(): pl.pallas_call(functools.partial(filter_kernel, n), grid_spec=pltpu.Prefe...  9.85 us
    ppermute x9, waiting for transfers between devices, along(): return lax.ppermute(value, 'lon', [(i, (i + d) % n) for i in range(n)])  9.14 us
    pallas_call x1, Pallas kernels, last_winds(): pl.pallas_call(winds_kernel, grid_spec=pltpu.PrefetchScalarGridSpec(num_s...  7.79 us
    ppermute x4, starting transfers between devices, to_lower(): return lax.ppermute(value, 'lev', [(0, 1)])  5.39 us
    pallas_call x1, Pallas kernels, edge_rows(): pl.pallas_call(functools.partial(rows_kernel, fields), grid_spec=pltpu.Pr...  4.56 us
  transfers between devices with their start and end apart: 14, of which 3 were waited for; matrix products, arithmetic and copies ran while one was open for 2% of the time, Pallas kernels for 60%

profile of v6, /device:TPU:0, one launch (start us, length us, event | category | flops | bytes accessed | tf_op | source)
XLA Modules:
  0.0 148.4 jit_solution(4830280376647517050)
XLA Ops:
  0.6 1.2 fusion.s
  1.8 3.1 %band_rows.1 = (f32[184,360]{1,0:T(8,128)}, f32[184,360]{1,0:T(8,128)}, f32[184,360]{1,0:T(8,128)}, f32[184,360]{1,0:T(8,128)}) custom-call(s32[10]{0:T(128)} %fusion.s, f32[4,360,360]{2,1,0:T(8,128)} %refs_9_.3, f32[4,360,360]{2,1,0:T(8,128)} %refs_10_.3, f32[4,360,360]{2,1,0:T(8,128)} %refs_8_.3, f32[4,360,360]{2,1,0:T(8,128)} %refs_9_.3, ...), custom_call_target="tpu_custom_call" | custom-call | bytes 9900000 | tf_op jit(solution)/shard_map/band_rows/pallas_call | solution.py:301
  4.9 3.0 %collective-permute-start = (f32[184,360]{1,0:T(8,128)}, f32[184,360]{1,0:T(8,128)S(1)}, u32[]{:S(2)}, u32[]{:S(2)}) collective-permute-start(f32[184,360]{1,0:T(8,128)} %get-tuple-element.69), channel_id=1, source_target_pairs={{0,4},{4,8},{8,12},{12,0},{1,5},{5,9},{9,13},{13,1},{2,6},{6,10},{... | collective-permute-start | bytes 794888 | tf_op jit(solution)/shard_map/ppermute | solution.py:987
  8.0 2.6 %collective-permute-start.1 = (f32[184,360]{1,0:T(8,128)}, f32[184,360]{1,0:T(8,128)S(1)}, u32[]{:S(2)}, u32[]{:S(2)}) collective-permute-start(f32[184,360]{1,0:T(8,128)} %get-tuple-element.70), channel_id=1, source_target_pairs={{0,8},{4,12},{8,0},{12,4},{1,9},{5,13},{9,1},{13,5},{2,10},{6,14},... | collective-permute-start | bytes 794888 | tf_op jit(solution)/shard_map/ppermute | solution.py:987
  10.5 1.3 collective-permute-start.2
  11.9 11.5 %pack_columns.1 = (f32[360,128]{1,0:T(8,128)}, f32[360,128]{1,0:T(8,128)}) custom-call(s32[10]{0:T(128)} %fusion.s, f32[10,4,360,360]{3,2,1,0:T(8,128)} %refs_0_.5, f32[10,4,360,360]{3,2,1,0:T(8,128)} %refs_0_.5, f32[4,360,360]{2,1,0:T(8,128)} %refs_8_.3, f32[4,360,360]{2,1,0:T(8,128)} %refs_8_.3, f32[4,360,360]{2,1,0:T(8,128)} %refs_9_.3, ...), custom_call_target="tpu_custom_call" | custom-call | bytes 33000000 | tf_op jit(solution)/shard_map/pack_columns/pallas_call | solution.py:383
  23.3 0.5 collective-permute-start.3
  23.8 1.6 %collective-permute-start.4 = (f32[360,128]{1,0:T(8,128)}, f32[360,128]{1,0:T(8,128)S(1)}, u32[]{:S(2)}, u32[]{:S(2)}) collective-permute-start(f32[360,128]{1,0:T(8,128)} %get-tuple-element.74), channel_id=1, source_target_pairs={{0,4},{4,8},{8,12},{12,0},{1,5},{5,9},{9,13},{13,1},{2,6},{6,10},{... | collective-permute-start | bytes 552968 | tf_op jit(solution)/shard_map/ppermute | solution.py:987
  25.4 2.6 %column_sum.1.own = f32[3,392,128]{2,1,0:T(8,128)} custom-call(f32[4,360,360]{2,1,0:T(8,128)} %refs_8_.3), custom_call_target="tpu_custom_call" | custom-call | bytes 9900000 | tf_op jit(solution)/shard_map/column_sum/pallas_call | solution.py:503
  28.0 0.0 collective-permute-done.refs_1_
  28.0 1.2 collective-permute-done.1.refs_2_
  29.2 0.0 collective-permute-done.2.refs_3_
  29.2 4.6 %collective-permute-done.3.east.refs_5_.refs_11_.refs_6_ = f32[360,128]{1,0:T(8,128)S(1)} collective-permute-done((f32[360,128]{1,0:T(8,128)}, f32[360,128]{1,0:T(8,128)S(1)}, u32[]{:S(2)}, u32[]{:S(2)}) %collective-permute-start.3) | collective-permute-done | bytes 184352 | tf_op jit(solution)/shard_map/ppermute | solution.py:987
  33.8 3.3 %collective-permute-done.4.west.refs_6_.refs_12_.refs_7_ = f32[360,128]{1,0:T(8,128)S(1)} collective-permute-done((f32[360,128]{1,0:T(8,128)}, f32[360,128]{1,0:T(8,128)S(1)}, u32[]{:S(2)}, u32[]{:S(2)}) %collective-permute-start.4) | collective-permute-done | bytes 184352 | tf_op jit(solution)/shard_map/ppermute | solution.py:987
  37.1 0.0 copy-done
  37.1 0.7 copy-done.1
  37.8 4.6 %edge_rows.1 = (f32[4,13,2,384]{3,2,1,0:T(2,128)}, f32[4,13,2,384]{3,2,1,0:T(2,128)}) custom-call(s32[10]{0:T(128)} %fusion.s, f32[10,4,360,360]{3,2,1,0:T(8,128)} %refs_0_.5, f32[10,4,360,360]{3,2,1,0:T(8,128)} %refs_0_.5, f32[4,360,360]{2,1,0:T(8,128)} %refs_8_.3, f32[4,360,360]{2,1,0:T(8,128)} %refs_8_.3, f32[4,360,360]{2,1,0:T(8,128)} %refs_9_.3, ...), custom_call_target="tpu_custom_call" | custom-call | bytes 13200000 | tf_op jit(solution)/shard_map/edge_rows/pallas_call | solution.py:442
  42.4 0.0 copy-done.10
  42.4 0.0 copy-done.11
  42.4 0.0 copy-done.12
  42.4 1.6 %collective-permute-start.5 = (f32[4,13,2,384]{3,2,1,0:T(2,128)}, f32[4,13,2,384]{3,2,1,0:T(2,128)S(1)}, u32[]{:S(2)}, u32[]{:S(2)}) collective-permute-start(f32[4,13,2,384]{3,2,1,0:T(2,128)} %get-tuple-element.84), channel_id=1, source_target_pairs={{0,2},{2,0},{1,3},{3,1},{4,6},{6,4},{5,7},{7,5},{8,10},{10,8},{9,1... | collective-permute-start | bytes 479240 | tf_op jit(solution)/shard_map/ppermute | solution.py:1005
  44.0 4.5 %spectra.1 = f32[184,384]{1,0:T(8,128)} custom-call(s32[10]{0:T(128)} %fusion.s, f32[184,360]{1,0:T(8,128)} %get-tuple-element.78.refs_0_, f32[184,360]{1,0:T(8,128)} %copy-done.10, f32[184,360]{1,0:T(8,128)} %copy-done.11, f32[184,360]{1,0:T(8,128)} %copy-done.12, f32[4,360,384]{2,1,0:T(8,128)} %constant.25.clone.refs_4_.refs_5_.refs_6_.refs_7_, ...), custom_call_target="tpu_custom_call" | custom-call | bytes 19800000 | tf_op jit(solution)/shard_map/spectra/pallas_call | solution.py:332
  48.5 0.9 slice.9
  49.4 1.3 collective-permute-start.6
  50.7 0.0 collective-permute-done.5.facing.refs_7_
  50.7 0.0 copy-start.5
  50.7 0.7 copy-done.5
  51.4 3.3 %column_rims.1 = f32[3,392,128]{2,1,0:T(8,128)} custom-call(s32[10]{0:T(128)} %fusion.s, f32[3,392,128]{2,1,0:T(8,128)} %column_sum.1.own, f32[360,128]{1,0:T(8,128)} %copy-done, f32[360,128]{1,0:T(8,128)} %copy-done.1, f32[4,13,2,384]{3,2,1,0:T(2,128)} %copy-done.5), custom_call_target="tpu_custom_call" | custom-call | bytes 6600000 | tf_op jit(solution)/shard_map/column_rims/pallas_call | solution.py:536
  54.7 0.0 collective-permute-done.6
  54.7 1.3 collective-permute-start.7
  56.0 1.0 constant_dynamic-update-slice_fusion.1
  57.0 0.0 copy-start.3
  57.0 0.0 copy-start.14
  57.0 7.3 %collective-permute-start.10 = (f32[248,384]{1,0:T(8,128)S(1)}, f32[248,384]{1,0:T(8,128)S(1)}, u32[]{:S(2)}, u32[]{:S(2)}) collective-permute-start(f32[248,384]{1,0:T(8,128)S(1)} %constant_dynamic-update-slice_fusion.refs_0_), channel_id=1, source_target_pairs={{0,12},{4,0},{8,4},{12,8},{1,13},{5,1},{9,5},{13,9},{2,14},{6,2},{... | collective-permute-start | bytes 1142792 | tf_op jit(solution)/shard_map/ppermute | solution.py:987
  64.3 0.3 collective-permute-start.8
  64.7 1.4 collective-permute-start.9
  66.1 0.0 copy-done.15
  66.1 1.5 %collective-permute-start.11 = (f32[4,13,2,384]{3,2,1,0:T(2,128)S(1)}, f32[4,13,2,384]{3,2,1,0:T(2,128)S(1)}, u32[]{:S(2)}, u32[]{:S(2)}) collective-permute-start(f32[4,13,2,384]{3,2,1,0:T(2,128)S(1)} %copy-done.15), channel_id=1, source_target_pairs={{0,8},{4,12},{8,0},{12,4},{1,9},{5,13},{9,1},{13,5},{2,10},{6,14},... | collective-permute-start | bytes 479240 | tf_op jit(solution)/shard_map/ppermute | solution.py:987
  67.6 0.0 collective-permute-done.7.refs_4_.refs_7_
  67.6 0.8 copy-done.2
  68.4 44.5 %tracers_inner.1 = (f32[10,4,360,360]{3,2,1,0:T(8,128)}, f32[4,360,360]{2,1,0:T(8,128)}, f32[4,3,328,128]{3,2,1,0:T(8,128)}, f32[4,3,328,128]{3,2,1,0:T(8,128)},...) custom-call(s32[10]{0:T(128)} %fusion.s, f32[10,4,360,360]{3,2,1,0:T(8,128)} %refs_0_.5, f32[4,360,360]{2,1,0:T(8,128)} %refs_8_.3, ...), custom_call_target="tpu_custom_call" | custom-call | bytes 165000000 | tf_op jit(solution)/shard_map/tracers_inner/pallas_call | solution.py:886
  112.9 0.0 copy-done.3
  112.9 0.0 collective-permute-done.11.refs_13_.refs_8_
  112.9 0.0 copy-start.4
  112.9 0.0 collective-permute-done.10.refs_3_
  112.9 0.0 copy-start.7
  112.9 0.0 collective-permute-done.8.refs_1_
  112.9 0.0 copy-start.8
  113.0 0.0 collective-permute-done.9.refs_2_
  113.0 0.0 copy-start.9
  113.0 1.3 collective-permute-start.12
  114.3 0.0 copy-done.14
  114.3 0.7 broadcast_in_dim.16.refs_4_
  115.0 0.0 copy-done.4
  115.0 0.0 copy-done.7
  115.0 0.0 copy-done.9
  115.0 9.8 %filtered_band.1 = (f32[4,3,96,128]{3,2,1,0:T(8,128)}, f32[4,3,96,128]{3,2,1,0:T(8,128)}, f32[4,3,96,128]{3,2,1,0:T(8,128)}, f32[4,3,96,128]{3,2,1,0:T(8,128)}, ...) custom-call(s32[10]{0:T(128)} %fusion.s, f32[248,384]{1,0:T(8,128)} %copy-done.3, ...), custom_call_target="tpu_custom_call" | custom-call | bytes 39600000 | tf_op jit(solution)/shard_map/filtered_band/pallas_call | solution.py:674
  124.9 1.5 collective-permute-start.13
  126.3 13.3 %tracers_polar.1 = (f32[10,4,360,360]{3,2,1,0:T(8,128)}, f32[4,360,360]{2,1,0:T(8,128)}) custom-call(s32[10]{0:T(128)} %fusion.s, f32[10,4,360,360]{3,2,1,0:T(8,128)} %refs_0_.5, f32[4,3,96,128]{3,2,1,0:T(8,128)} %get-tuple-element.97.refs_1_, f32[4,3,96,128]{3,2,1,0:T(8,128)} %get-tuple-element.98.refs_2_, ...), custom_call_target="tpu_custom_call", output_to_operand_aliasing={{0}: (10, {}), {1}: (11, {})} | custom-call | bytes 42900000 | tf_op jit(solution)/shard_map/tracers_polar/pallas_call | solution.py:886
  139.7 0.0 collective-permute-done.13.refs_7_
  139.7 0.0 collective-permute-done.12.refs_3_
  139.7 0.6 copy-done.13
  140.3 0.2 copy-done.6
  140.6 7.8 %last_winds.1 = (f32[4,360,360]{2,1,0:T(8,128)}, f32[4,360,360]{2,1,0:T(8,128)}) custom-call(s32[10]{0:T(128)} %fusion.s, f32[4,3,328,128]{3,2,1,0:T(8,128)} %get-tuple-element.106.refs_0_, f32[4,3,328,128]{3,2,1,0:T(8,128)} %get-tuple-element.107.refs_1_, f32[4,3,328,128]{3,2,1,0:T(8,128)} %get-tuple-element.108.refs_2_, f32[3,328,128]{2,1,0:T(8,128)} %copy-done.6, ...), custom_call_target="tpu_custom_call" | custom-call | bytes 26400000 | tf_op jit(solution)/shard_map/last_winds/pallas_call | solution.py:935
  (13 shorter events, 0.0 us)
Async XLA Ops:
  4.9 23.1 %collective-permute-start = (f32[184,360]{1,0:T(8,128)}, f32[184,360]{1,0:T(8,128)S(1)}, u32[]{:S(2)}, u32[]{:S(2)}) collective-permute-start(f32[184,360]{1,0:T(8,128)} %get-tuple-element.69), channel_id=1, source_target_pairs={{0,4},{4,8},{8,12},{12,0},{1,5},{5,9},{9,13},{13,1},{2,6},{6,10},{... | collective-permute-start | bytes 794888 | tf_op jit(solution)/shard_map/ppermute | solution.py:987
  8.0 21.3 %collective-permute-start.1 = (f32[184,360]{1,0:T(8,128)}, f32[184,360]{1,0:T(8,128)S(1)}, u32[]{:S(2)}, u32[]{:S(2)}) collective-permute-start(f32[184,360]{1,0:T(8,128)} %get-tuple-element.70), channel_id=1, source_target_pairs={{0,8},{4,12},{8,0},{12,4},{1,9},{5,13},{9,1},{13,5},{2,10},{6,14},... | collective-permute-start | bytes 794888 | tf_op jit(solution)/shard_map/ppermute | solution.py:987
  10.5 18.7 %collective-permute-start.2 = (f32[184,360]{1,0:T(8,128)}, f32[184,360]{1,0:T(8,128)S(1)}, u32[]{:S(2)}, u32[]{:S(2)}) collective-permute-start(f32[184,360]{1,0:T(8,128)} %get-tuple-element.71), channel_id=1, source_target_pairs={{0,12},{4,0},{8,4},{12,8},{1,13},{5,1},{9,5},{13,9},{2,14},{6,2},{... | collective-permute-start | bytes 794888 | tf_op jit(solution)/shard_map/ppermute | solution.py:987
  23.3 10.5 %collective-permute-start.3 = (f32[360,128]{1,0:T(8,128)}, f32[360,128]{1,0:T(8,128)S(1)}, u32[]{:S(2)}, u32[]{:S(2)}) collective-permute-start(f32[360,128]{1,0:T(8,128)} %get-tuple-element.73), channel_id=1, source_target_pairs={{0,12},{4,0},{8,4},{12,8},{1,13},{5,1},{9,5},{13,9},{2,14},{6,2},{... | collective-permute-start | bytes 552968 | tf_op jit(solution)/shard_map/ppermute | solution.py:987
  23.8 13.3 %collective-permute-start.4 = (f32[360,128]{1,0:T(8,128)}, f32[360,128]{1,0:T(8,128)S(1)}, u32[]{:S(2)}, u32[]{:S(2)}) collective-permute-start(f32[360,128]{1,0:T(8,128)} %get-tuple-element.74), channel_id=1, source_target_pairs={{0,4},{4,8},{8,12},{12,0},{1,5},{5,9},{9,13},{13,1},{2,6},{6,10},{... | collective-permute-start | bytes 552968 | tf_op jit(solution)/shard_map/ppermute | solution.py:987
  28.0 14.4 %copy-start.10 = (f32[184,360]{1,0:T(8,128)}, f32[184,360]{1,0:T(8,128)S(1)}, u32[]{:S(2)}) copy-start(f32[184,360]{1,0:T(8,128)S(1)} %collective-permute-done.refs_1_) | copy-start | bytes 794884
  29.2 13.1 %copy-start.11 = (f32[184,360]{1,0:T(8,128)}, f32[184,360]{1,0:T(8,128)S(1)}, u32[]{:S(2)}) copy-start(f32[184,360]{1,0:T(8,128)S(1)} %collective-permute-done.1.refs_2_) | copy-start | bytes 794884
  29.2 13.2 %copy-start.12 = (f32[184,360]{1,0:T(8,128)}, f32[184,360]{1,0:T(8,128)S(1)}, u32[]{:S(2)}) copy-start(f32[184,360]{1,0:T(8,128)S(1)} %collective-permute-done.2.refs_3_) | copy-start | bytes 794884
  33.8 3.3 %copy-start = (f32[360,128]{1,0:T(8,128)}, f32[360,128]{1,0:T(8,128)S(1)}, u32[]{:S(2)}) copy-start(f32[360,128]{1,0:T(8,128)S(1)} %collective-permute-done.3.east.refs_5_.refs_11_.refs_6_) | copy-start | bytes 552964
  37.1 0.7 copy-start.1
  42.4 8.3 %collective-permute-start.5 = (f32[4,13,2,384]{3,2,1,0:T(2,128)}, f32[4,13,2,384]{3,2,1,0:T(2,128)S(1)}, u32[]{:S(2)}, u32[]{:S(2)}) collective-permute-start(f32[4,13,2,384]{3,2,1,0:T(2,128)} %get-tuple-element.84), channel_id=1, source_target_pairs={{0,2},{2,0},{1,3},{3,1},{4,6},{6,4},{5,7},{7,5},{8,10},{10,8},{9,1... | collective-permute-start | bytes 479240 | tf_op jit(solution)/shard_map/ppermute | solution.py:1005
  48.5 17.6 %copy-start.15 = (f32[4,13,2,384]{3,2,1,0:T(2,128)S(1)}, f32[4,13,2,384]{3,2,1,0:T(2,128)}, u32[]{:S(2)}) copy-start(f32[4,13,2,384]{3,2,1,0:T(2,128)} %get-tuple-element.90) | copy-start | bytes 479236
  49.4 5.3 %collective-permute-start.6 = (f32[64,384]{1,0:T(8,128)S(1)}, f32[64,384]{1,0:T(8,128)S(1)}, u32[]{:S(2)}, u32[]{:S(2)}) collective-permute-start(f32[64,384]{1,0:T(8,128)S(1)} %slice.9), channel_id=1, source_target_pairs={{0,1},{2,3},{4,5},{6,7},{8,9},{10,11},{12,13},{14,15},{16,17},{18,... | collective-permute-start | bytes 294920 | tf_op jit(solution)/shard_map/ppermute | solution.py:990
  50.7 0.7 copy-start.5
  54.7 12.9 %collective-permute-start.7 = (f32[3,392,128]{2,1,0:T(8,128)}, f32[3,392,128]{2,1,0:T(8,128)S(1)}, u32[]{:S(2)}, u32[]{:S(2)}) collective-permute-start(f32[3,392,128]{2,1,0:T(8,128)} %column_rims.1), channel_id=1, source_target_pairs={{0,1},{2,3},{4,5},{6,7},{8,9},{10,11},{12,13},{14,15},{16,17},{18,... | collective-permute-start | bytes 1806344 | tf_op jit(solution)/shard_map/ppermute | solution.py:990
  57.0 55.9 %copy-start.3 = (f32[248,384]{1,0:T(8,128)}, f32[248,384]{1,0:T(8,128)S(1)}, u32[]{:S(2)}) copy-start(f32[248,384]{1,0:T(8,128)S(1)} %constant_dynamic-update-slice_fusion.refs_0_) | copy-start | bytes 1142788
  57.0 57.3 %copy-start.14 = (s32[2,60]{1,0:T(2,128)S(1)}, s32[2,60]{1,0:T(2,128)}, u32[]{:S(2)}) copy-start(s32[2,60]{1,0:T(2,128)} %param.14) | copy-start | bytes 1444
  57.0 55.9 %collective-permute-start.10 = (f32[248,384]{1,0:T(8,128)S(1)}, f32[248,384]{1,0:T(8,128)S(1)}, u32[]{:S(2)}, u32[]{:S(2)}) collective-permute-start(f32[248,384]{1,0:T(8,128)S(1)} %constant_dynamic-update-slice_fusion.refs_0_), channel_id=1, source_target_pairs={{0,12},{4,0},{8,4},{12,8},{1,13},{5,1},{9,5},{13,9},{2,14},{6,2},{... | collective-permute-start | bytes 1142792 | tf_op jit(solution)/shard_map/ppermute | solution.py:987
  64.3 48.6 %collective-permute-start.8 = (f32[248,384]{1,0:T(8,128)S(1)}, f32[248,384]{1,0:T(8,128)S(1)}, u32[]{:S(2)}, u32[]{:S(2)}) collective-permute-start(f32[248,384]{1,0:T(8,128)S(1)} %constant_dynamic-update-slice_fusion.refs_0_), channel_id=1, source_target_pairs={{0,4},{4,8},{8,12},{12,0},{1,5},{5,9},{9,13},{13,1},{2,6},{6,10},{... | collective-permute-start | bytes 1142792 | tf_op jit(solution)/shard_map/ppermute | solution.py:987
  64.7 48.3 %collective-permute-start.9 = (f32[248,384]{1,0:T(8,128)S(1)}, f32[248,384]{1,0:T(8,128)S(1)}, u32[]{:S(2)}, u32[]{:S(2)}) collective-permute-start(f32[248,384]{1,0:T(8,128)S(1)} %constant_dynamic-update-slice_fusion.refs_0_), channel_id=1, source_target_pairs={{0,8},{4,12},{8,0},{12,4},{1,9},{5,13},{9,1},{13,5},{2,10},{6,14},... | collective-permute-start | bytes 1142792 | tf_op jit(solution)/shard_map/ppermute | solution.py:987
  66.1 46.8 %collective-permute-start.11 = (f32[4,13,2,384]{3,2,1,0:T(2,128)S(1)}, f32[4,13,2,384]{3,2,1,0:T(2,128)S(1)}, u32[]{:S(2)}, u32[]{:S(2)}) collective-permute-start(f32[4,13,2,384]{3,2,1,0:T(2,128)S(1)} %copy-done.15), channel_id=1, source_target_pairs={{0,8},{4,12},{8,0},{12,4},{1,9},{5,13},{9,1},{13,5},{2,10},{6,14},... | collective-permute-start | bytes 479240 | tf_op jit(solution)/shard_map/ppermute | solution.py:987
  67.6 0.8 copy-start.2
  112.9 2.1 %copy-start.4 = (f32[4,13,2,384]{3,2,1,0:T(2,128)}, f32[4,13,2,384]{3,2,1,0:T(2,128)S(1)}, u32[]{:S(2)}) copy-start(f32[4,13,2,384]{3,2,1,0:T(2,128)S(1)} %collective-permute-done.11.refs_13_.refs_8_) | copy-start | bytes 479236
  112.9 2.1 %copy-start.7 = (f32[248,384]{1,0:T(8,128)}, f32[248,384]{1,0:T(8,128)S(1)}, u32[]{:S(2)}) copy-start(f32[248,384]{1,0:T(8,128)S(1)} %collective-permute-done.10.refs_3_) | copy-start | bytes 1142788
  112.9 2.1 %copy-start.8 = (f32[248,384]{1,0:T(8,128)}, f32[248,384]{1,0:T(8,128)S(1)}, u32[]{:S(2)}) copy-start(f32[248,384]{1,0:T(8,128)S(1)} %collective-permute-done.8.refs_1_) | copy-start | bytes 1142788
  113.0 2.1 %copy-start.9 = (f32[248,384]{1,0:T(8,128)}, f32[248,384]{1,0:T(8,128)S(1)}, u32[]{:S(2)}) copy-start(f32[248,384]{1,0:T(8,128)S(1)} %collective-permute-done.9.refs_2_) | copy-start | bytes 1142788
  113.0 26.7 %collective-permute-start.12 = (f32[3,328,128]{2,1,0:T(8,128)}, f32[3,328,128]{2,1,0:T(8,128)S(1)}, u32[]{:S(2)}, u32[]{:S(2)}) collective-permute-start(f32[3,328,128]{2,1,0:T(8,128)} %get-tuple-element.109), channel_id=1, source_target_pairs={{0,1},{2,3},{4,5},{6,7},{8,9},{10,11},{12,13},{14,15},{16,17},{18,... | collective-permute-start | bytes 1511432 | tf_op jit(solution)/shard_map/ppermute | solution.py:990
  124.9 14.8 %collective-permute-start.13 = (f32[3,96,128]{2,1,0:T(8,128)}, f32[3,96,128]{2,1,0:T(8,128)S(1)}, u32[]{:S(2)}, u32[]{:S(2)}) collective-permute-start(f32[3,96,128]{2,1,0:T(8,128)} %get-tuple-element.111), channel_id=1, source_target_pairs={{0,1},{2,3},{4,5},{6,7},{8,9},{10,11},{12,13},{14,15},{16,17},{18,... | collective-permute-start | bytes 442376 | tf_op jit(solution)/shard_map/ppermute | solution.py:990
  139.7 0.7 copy-start.13
  139.7 0.9 copy-start.6

commit v7 on v6

--- a/solution.py
+++ b/solution.py
@@ -319,6 +319,7 @@
         part = dot3(refs[d][...], refs[n + d][0])
         total = part if total is None else total + part
     refs[2 * n][...] = total
+    refs[2 * n + 1][...] = total[2 * POLAR :]
 
 
 def spectra(scalars, pieces, basis):
@@ -335,9 +336,9 @@
             num_scalar_prefetch=1,
             grid=(1,),
             in_specs=[HELD] * n + [spec(d) for d in range(n)],
-            out_specs=pl.BlockSpec((rows, waves), lambda i, s: (0, 0)),
+            out_specs=[pl.BlockSpec((k, waves), lambda i, s: (0, 0)) for k in (rows, rows - 2 * POLAR)],
         ),
-        out_shape=jax.ShapeDtypeStruct((rows, waves), jnp.float32),
+        out_shape=[jax.ShapeDtypeStruct((k, waves), jnp.float32) for k in (rows, rows - 2 * POLAR)],
         cost_estimate=cost(6),
         compiler_params=params(),
         name="spectra",
@@ -998,16 +999,16 @@
     scalars, packed, deep = lax.optimization_barrier((scalars, packed, thickness))
     east, west = along(packed[0], n - 1), along(packed[1], 1)
     column = column_sum(deep)
-    scalars, column, pieces = lax.optimization_barrier((scalars, column, pieces))
+    scalars, column, pieces, limits = lax.optimization_barrier((scalars, column, pieces, limits))
 
     pole, facing = edge_rows(scalars, tracers, *fields, east, west)
     scalars, pole, facing = lax.optimization_barrier((scalars, pole, facing))
     facing = lax.ppermute(facing, "lat", [(0, 1), (1, 0)])
     pole = along(pole, n // 2)
 
-    own = spectra(scalars, pieces, forward)
-    scalars, own = lax.optimization_barrier((scalars, own))
-    upper = to_lower(own[2 * POLAR :])
+    own, upper = spectra(scalars, pieces, forward)
+    scalars, own, upper = lax.optimization_barrier((scalars, own, upper))
+    upper = to_lower(upper)
     column = column_rims(scalars, column, cols, east, west, facing)
     scalars, column, upper = lax.optimization_barrier((scalars, column, upper))
     column = to_lower(column)

time: 149 us -> 148 us (level)
  transfers between devices with their start and end apart: 14 -> 14, of which waited for: 3 -> 3; matrix products, arithmetic and copies ran while one was open for 2% -> 1% of each run, Pallas kernels for 60% -> 61%
where the time goes in v7:
time: 148 us; the launch traced here: 147 us
  Pallas kernels  105 us (71%)
  starting transfers between devices  26.7 us (18%)
  waiting for transfers between devices  8.3 us (6%)
  local copies, waits for them, and re-layouts  4.85 us (3%)
    pallas_call x2, Pallas kernels, tracer_slab(): pl.pallas_call(functools.partial(slab_kernel, rim.shape[1], group, rows,...  57.8 us
    ppermute x9, starting transfers between devices, along(): return lax.ppermute(value, 'lon', [(i, (i + d) % n) for i in range(n)])  19.6 us
    pallas_call x1, Pallas kernels, pack_columns(): pl.pallas_call(functools.partial(pack_kernel, count + 3, cols - LANE * hi...  11.5 us
    pallas_call x1, Pallas kernels, filtered_band(): pl.pallas_call(functools.partial(filter_kernel, n), grid_spec=pltpu.Prefe...  9.85 us
    ppermute x9, waiting for transfers between devices, along(): return lax.ppermute(value, 'lon', [(i, (i + d) % n) for i in range(n)])  8.29 us
    pallas_call x1, Pallas kernels, last_winds(): pl.pallas_call(winds_kernel, grid_spec=pltpu.PrefetchScalarGridSpec(num_s...  7.8 us
    ppermute x4, starting transfers between devices, to_lower(): return lax.ppermute(value, 'lev', [(0, 1)])  5.52 us
    pallas_call x1, Pallas kernels, edge_rows(): pl.pallas_call(functools.partial(rows_kernel, fields), grid_spec=pltpu.Pr...  4.56 us
  transfers between devices with their start and end apart: 14, of which 3 were waited for; matrix products, arithmetic and copies ran while one was open for 1% of the time, Pallas kernels for 61%

profile of v7, /device:TPU:0, one launch (start us, length us, event | category | flops | bytes accessed | tf_op | source)
XLA Modules:
  0.0 146.9 jit_solution(2161369052493782590)
XLA Ops:
  0.6 1.2 fusion.s
  1.8 3.1 %band_rows.1 = (f32[184,360]{1,0:T(8,128)}, f32[184,360]{1,0:T(8,128)}, f32[184,360]{1,0:T(8,128)}, f32[184,360]{1,0:T(8,128)}) custom-call(s32[10]{0:T(128)} %fusion.s, f32[4,360,360]{2,1,0:T(8,128)} %refs_9_.3, f32[4,360,360]{2,1,0:T(8,128)} %refs_10_.3, f32[4,360,360]{2,1,0:T(8,128)} %refs_8_.3, f32[4,360,360]{2,1,0:T(8,128)} %refs_9_.3, ...), custom_call_target="tpu_custom_call" | custom-call | bytes 9900000 | tf_op jit(solution)/shard_map/band_rows/pallas_call | solution.py:301
  4.9 3.0 %collective-permute-start = (f32[184,360]{1,0:T(8,128)}, f32[184,360]{1,0:T(8,128)S(1)}, u32[]{:S(2)}, u32[]{:S(2)}) collective-permute-start(f32[184,360]{1,0:T(8,128)} %get-tuple-element.73), channel_id=1, source_target_pairs={{0,4},{4,8},{8,12},{12,0},{1,5},{5,9},{9,13},{13,1},{2,6},{6,10},{... | collective-permute-start | bytes 794888 | tf_op jit(solution)/shard_map/ppermute | solution.py:988
  7.9 2.6 %collective-permute-start.1 = (f32[184,360]{1,0:T(8,128)}, f32[184,360]{1,0:T(8,128)S(1)}, u32[]{:S(2)}, u32[]{:S(2)}) collective-permute-start(f32[184,360]{1,0:T(8,128)} %get-tuple-element.74), channel_id=1, source_target_pairs={{0,8},{4,12},{8,0},{12,4},{1,9},{5,13},{9,1},{13,5},{2,10},{6,14},... | collective-permute-start | bytes 794888 | tf_op jit(solution)/shard_map/ppermute | solution.py:988
  10.5 1.3 collective-permute-start.2
  11.9 11.5 %pack_columns.1 = (f32[360,128]{1,0:T(8,128)}, f32[360,128]{1,0:T(8,128)}) custom-call(s32[10]{0:T(128)} %fusion.s, f32[10,4,360,360]{3,2,1,0:T(8,128)} %refs_0_.5, f32[10,4,360,360]{3,2,1,0:T(8,128)} %refs_0_.5, f32[4,360,360]{2,1,0:T(8,128)} %refs_8_.3, f32[4,360,360]{2,1,0:T(8,128)} %refs_8_.3, f32[4,360,360]{2,1,0:T(8,128)} %refs_9_.3, ...), custom_call_target="tpu_custom_call" | custom-call | bytes 33000000 | tf_op jit(solution)/shard_map/pack_columns/pallas_call | solution.py:384
  23.3 0.5 collective-permute-start.3
  23.8 1.6 %collective-permute-start.4 = (f32[360,128]{1,0:T(8,128)}, f32[360,128]{1,0:T(8,128)S(1)}, u32[]{:S(2)}, u32[]{:S(2)}) collective-permute-start(f32[360,128]{1,0:T(8,128)} %get-tuple-element.78), channel_id=1, source_target_pairs={{0,4},{4,8},{8,12},{12,0},{1,5},{5,9},{9,13},{13,1},{2,6},{6,10},{... | collective-permute-start | bytes 552968 | tf_op jit(solution)/shard_map/ppermute | solution.py:988
  25.4 2.6 %column_sum.1.own = f32[3,392,128]{2,1,0:T(8,128)} custom-call(f32[4,360,360]{2,1,0:T(8,128)} %refs_8_.3), custom_call_target="tpu_custom_call" | custom-call | bytes 9900000 | tf_op jit(solution)/shard_map/column_sum/pallas_call | solution.py:504
  28.0 0.0 copy-done.14
  28.0 0.0 collective-permute-done.refs_1_
  28.0 0.0 copy-start.10
  28.0 1.2 collective-permute-done.1.refs_2_
  29.2 0.0 collective-permute-done.2.refs_3_
  29.2 0.8 broadcast_in_dim.16.refs_4_
  30.0 3.8 %collective-permute-done.3.east.refs_5_.refs_11_.refs_6_ = f32[360,128]{1,0:T(8,128)S(1)} collective-permute-done((f32[360,128]{1,0:T(8,128)}, f32[360,128]{1,0:T(8,128)S(1)}, u32[]{:S(2)}, u32[]{:S(2)}) %collective-permute-start.3) | collective-permute-done | bytes 184352 | tf_op jit(solution)/shard_map/ppermute | solution.py:988
  33.8 3.3 %collective-permute-done.4.west.refs_6_.refs_12_.refs_7_ = f32[360,128]{1,0:T(8,128)S(1)} collective-permute-done((f32[360,128]{1,0:T(8,128)}, f32[360,128]{1,0:T(8,128)S(1)}, u32[]{:S(2)}, u32[]{:S(2)}) %collective-permute-start.4) | collective-permute-done | bytes 184352 | tf_op jit(solution)/shard_map/ppermute | solution.py:988
  37.1 0.0 copy-done
  37.1 0.7 copy-done.1
  37.8 4.6 %edge_rows.1 = (f32[4,13,2,384]{3,2,1,0:T(2,128)}, f32[4,13,2,384]{3,2,1,0:T(2,128)}) custom-call(s32[10]{0:T(128)} %fusion.s, f32[10,4,360,360]{3,2,1,0:T(8,128)} %refs_0_.5, f32[10,4,360,360]{3,2,1,0:T(8,128)} %refs_0_.5, f32[4,360,360]{2,1,0:T(8,128)} %refs_8_.3, f32[4,360,360]{2,1,0:T(8,128)} %refs_8_.3, f32[4,360,360]{2,1,0:T(8,128)} %refs_9_.3, ...), custom_call_target="tpu_custom_call" | custom-call | bytes 13200000 | tf_op jit(solution)/shard_map/edge_rows/pallas_call | solution.py:443
  42.3 0.0 copy-done.10
  42.3 0.0 copy-done.11
  42.4 0.0 copy-done.12
  42.4 1.6 %collective-permute-start.5 = (f32[4,13,2,384]{3,2,1,0:T(2,128)}, f32[4,13,2,384]{3,2,1,0:T(2,128)S(1)}, u32[]{:S(2)}, u32[]{:S(2)}) collective-permute-start(f32[4,13,2,384]{3,2,1,0:T(2,128)} %get-tuple-element.90), channel_id=1, source_target_pairs={{0,2},{2,0},{1,3},{3,1},{4,6},{6,4},{5,7},{7,5},{8,10},{10,8},{9,1... | collective-permute-start | bytes 479240 | tf_op jit(solution)/shard_map/ppermute | solution.py:1006
  43.9 4.5 %spectra.1 = (f32[184,384]{1,0:T(8,128)}, f32[64,384]{1,0:T(8,128)}) custom-call(s32[10]{0:T(128)} %fusion.s, f32[184,360]{1,0:T(8,128)} %get-tuple-element.82.refs_0_, f32[184,360]{1,0:T(8,128)} %copy-done.10, f32[184,360]{1,0:T(8,128)} %copy-done.11, f32[184,360]{1,0:T(8,128)} %copy-done.12, f32[4,360,384]{2,1,0:T(8,128)} %constant.25.clone.refs_4_.refs_5_.refs_6_.refs_7_, ...), custom_call_target="tpu_custom_call" | custom-call | bytes 19800000 | tf_op jit(solution)/shard_map/spectra/pallas_call | solution.py:333
  48.5 1.4 collective-permute-start.6
  49.9 0.0 collective-permute-done.5.facing.refs_7_
  49.9 0.0 copy-start.5
  49.9 0.6 copy-done.5
  50.5 3.3 %column_rims.1 = f32[3,392,128]{2,1,0:T(8,128)} custom-call(s32[10]{0:T(128)} %fusion.s, f32[3,392,128]{2,1,0:T(8,128)} %column_sum.1.own, f32[360,128]{1,0:T(8,128)} %copy-done, f32[360,128]{1,0:T(8,128)} %copy-done.1, f32[4,13,2,384]{3,2,1,0:T(2,128)} %copy-done.5), custom_call_target="tpu_custom_call" | custom-call | bytes 6600000 | tf_op jit(solution)/shard_map/column_rims/pallas_call | solution.py:537
  53.9 0.0 collective-permute-done.6
  53.9 1.3 collective-permute-start.7
  55.2 1.0 constant_dynamic-update-slice_fusion.1
  56.2 0.0 copy-start.3
  56.2 7.3 %collective-permute-start.10 = (f32[248,384]{1,0:T(8,128)S(1)}, f32[248,384]{1,0:T(8,128)S(1)}, u32[]{:S(2)}, u32[]{:S(2)}) collective-permute-start(f32[248,384]{1,0:T(8,128)S(1)} %constant_dynamic-update-slice_fusion.refs_0_), channel_id=1, source_target_pairs={{0,12},{4,0},{8,4},{12,8},{1,13},{5,1},{9,5},{13,9},{2,14},{6,2},{... | collective-permute-start | bytes 1142792 | tf_op jit(solution)/shard_map/ppermute | solution.py:988
  63.5 0.3 collective-permute-start.8
  63.8 1.4 collective-permute-start.9
  65.2 0.0 copy-done.15
  65.2 1.5 %collective-permute-start.11 = (f32[4,13,2,384]{3,2,1,0:T(2,128)S(1)}, f32[4,13,2,384]{3,2,1,0:T(2,128)S(1)}, u32[]{:S(2)}, u32[]{:S(2)}) collective-permute-start(f32[4,13,2,384]{3,2,1,0:T(2,128)S(1)} %copy-done.15), channel_id=1, source_target_pairs={{0,8},{4,12},{8,0},{12,4},{1,9},{5,13},{9,1},{13,5},{2,10},{6,14},... | collective-permute-start | bytes 479240 | tf_op jit(solution)/shard_map/ppermute | solution.py:988
  66.8 0.0 collective-permute-done.7.refs_4_.refs_7_
  66.8 0.8 copy-done.2
  67.6 44.5 %tracers_inner.1 = (f32[10,4,360,360]{3,2,1,0:T(8,128)}, f32[4,360,360]{2,1,0:T(8,128)}, f32[4,3,328,128]{3,2,1,0:T(8,128)}, f32[4,3,328,128]{3,2,1,0:T(8,128)},...) custom-call(s32[10]{0:T(128)} %fusion.s, f32[10,4,360,360]{3,2,1,0:T(8,128)} %refs_0_.5, f32[4,360,360]{2,1,0:T(8,128)} %refs_8_.3, ...), custom_call_target="tpu_custom_call" | custom-call | bytes 165000000 | tf_op jit(solution)/shard_map/tracers_inner/pallas_call | solution.py:887
  112.1 0.0 copy-done.3
  112.1 0.0 collective-permute-done.11.refs_13_.refs_8_
  112.1 0.0 copy-start.4
  112.1 0.0 collective-permute-done.10.refs_3_
  112.1 0.0 copy-start.7
  112.1 0.0 collective-permute-done.8.refs_1_
  112.1 0.0 copy-start.8
  112.1 0.0 collective-permute-done.9.refs_2_
  112.2 0.0 copy-start.9
  112.2 1.3 collective-permute-start.12
  113.5 0.0 copy-done.4
  113.5 0.0 copy-done.7
  113.5 0.0 copy-done.8
  113.5 0.0 copy-done.9
  113.5 9.8 %filtered_band.1 = (f32[4,3,96,128]{3,2,1,0:T(8,128)}, f32[4,3,96,128]{3,2,1,0:T(8,128)}, f32[4,3,96,128]{3,2,1,0:T(8,128)}, f32[4,3,96,128]{3,2,1,0:T(8,128)}, ...) custom-call(s32[10]{0:T(128)} %fusion.s, f32[248,384]{1,0:T(8,128)} %copy-done.3, ...), custom_call_target="tpu_custom_call" | custom-call | bytes 39600000 | tf_op jit(solution)/shard_map/filtered_band/pallas_call | solution.py:675
  123.4 1.5 collective-permute-start.13
  124.9 13.3 %tracers_polar.1 = (f32[10,4,360,360]{3,2,1,0:T(8,128)}, f32[4,360,360]{2,1,0:T(8,128)}) custom-call(s32[10]{0:T(128)} %fusion.s, f32[10,4,360,360]{3,2,1,0:T(8,128)} %refs_0_.5, f32[4,3,96,128]{3,2,1,0:T(8,128)} %get-tuple-element.105.refs_1_, f32[4,3,96,128]{3,2,1,0:T(8,128)} %get-tuple-element.106.refs_2_, ...), custom_call_target="tpu_custom_call", output_to_operand_aliasing={{0}: (10, {}), {1}: (11, {})} | custom-call | bytes 42900000 | tf_op jit(solution)/shard_map/tracers_polar/pallas_call | solution.py:887
  138.2 0.0 collective-permute-done.13.refs_7_
  138.2 0.0 collective-permute-done.12.refs_3_
  138.2 0.6 copy-done.13
  138.8 0.3 copy-done.6
  139.1 7.8 %last_winds.1 = (f32[4,360,360]{2,1,0:T(8,128)}, f32[4,360,360]{2,1,0:T(8,128)}) custom-call(s32[10]{0:T(128)} %fusion.s, f32[4,3,328,128]{3,2,1,0:T(8,128)} %get-tuple-element.114.refs_0_, f32[4,3,328,128]{3,2,1,0:T(8,128)} %get-tuple-element.115.refs_1_, f32[4,3,328,128]{3,2,1,0:T(8,128)} %get-tuple-element.116.refs_2_, f32[3,328,128]{2,1,0:T(8,128)} %copy-done.6, ...), custom_call_target="tpu_custom_call" | custom-call | bytes 26400000 | tf_op jit(solution)/shard_map/last_winds/pallas_call | solution.py:936
  (12 shorter events, 0.0 us)
Async XLA Ops:
  4.9 23.1 %collective-permute-start = (f32[184,360]{1,0:T(8,128)}, f32[184,360]{1,0:T(8,128)S(1)}, u32[]{:S(2)}, u32[]{:S(2)}) collective-permute-start(f32[184,360]{1,0:T(8,128)} %get-tuple-element.73), channel_id=1, source_target_pairs={{0,4},{4,8},{8,12},{12,0},{1,5},{5,9},{9,13},{13,1},{2,6},{6,10},{... | collective-permute-start | bytes 794888 | tf_op jit(solution)/shard_map/ppermute | solution.py:988
  7.9 21.3 %collective-permute-start.1 = (f32[184,360]{1,0:T(8,128)}, f32[184,360]{1,0:T(8,128)S(1)}, u32[]{:S(2)}, u32[]{:S(2)}) collective-permute-start(f32[184,360]{1,0:T(8,128)} %get-tuple-element.74), channel_id=1, source_target_pairs={{0,8},{4,12},{8,0},{12,4},{1,9},{5,13},{9,1},{13,5},{2,10},{6,14},... | collective-permute-start | bytes 794888 | tf_op jit(solution)/shard_map/ppermute | solution.py:988
  10.5 18.7 %collective-permute-start.2 = (f32[184,360]{1,0:T(8,128)}, f32[184,360]{1,0:T(8,128)S(1)}, u32[]{:S(2)}, u32[]{:S(2)}) collective-permute-start(f32[184,360]{1,0:T(8,128)} %get-tuple-element.75), channel_id=1, source_target_pairs={{0,12},{4,0},{8,4},{12,8},{1,13},{5,1},{9,5},{13,9},{2,14},{6,2},{... | collective-permute-start | bytes 794888 | tf_op jit(solution)/shard_map/ppermute | solution.py:988
  23.3 4.7 %copy-start.14 = (s32[2,60]{1,0:T(2,128)S(1)}, s32[2,60]{1,0:T(2,128)}, u32[]{:S(2)}) copy-start(s32[2,60]{1,0:T(2,128)} %param.14) | copy-start | bytes 1444
  23.3 10.5 %collective-permute-start.3 = (f32[360,128]{1,0:T(8,128)}, f32[360,128]{1,0:T(8,128)S(1)}, u32[]{:S(2)}, u32[]{:S(2)}) collective-permute-start(f32[360,128]{1,0:T(8,128)} %get-tuple-element.77), channel_id=1, source_target_pairs={{0,12},{4,0},{8,4},{12,8},{1,13},{5,1},{9,5},{13,9},{2,14},{6,2},{... | collective-permute-start | bytes 552968 | tf_op jit(solution)/shard_map/ppermute | solution.py:988
  23.8 13.3 %collective-permute-start.4 = (f32[360,128]{1,0:T(8,128)}, f32[360,128]{1,0:T(8,128)S(1)}, u32[]{:S(2)}, u32[]{:S(2)}) collective-permute-start(f32[360,128]{1,0:T(8,128)} %get-tuple-element.78), channel_id=1, source_target_pairs={{0,4},{4,8},{8,12},{12,0},{1,5},{5,9},{9,13},{13,1},{2,6},{6,10},{... | collective-permute-start | bytes 552968 | tf_op jit(solution)/shard_map/ppermute | solution.py:988
  28.0 14.3 %copy-start.10 = (f32[184,360]{1,0:T(8,128)}, f32[184,360]{1,0:T(8,128)S(1)}, u32[]{:S(2)}) copy-start(f32[184,360]{1,0:T(8,128)S(1)} %collective-permute-done.refs_1_) | copy-start | bytes 794884
  29.2 13.2 %copy-start.11 = (f32[184,360]{1,0:T(8,128)}, f32[184,360]{1,0:T(8,128)S(1)}, u32[]{:S(2)}) copy-start(f32[184,360]{1,0:T(8,128)S(1)} %collective-permute-done.1.refs_2_) | copy-start | bytes 794884
  29.2 13.2 %copy-start.12 = (f32[184,360]{1,0:T(8,128)}, f32[184,360]{1,0:T(8,128)S(1)}, u32[]{:S(2)}) copy-start(f32[184,360]{1,0:T(8,128)S(1)} %collective-permute-done.2.refs_3_) | copy-start | bytes 794884
  33.8 3.3 %copy-start = (f32[360,128]{1,0:T(8,128)}, f32[360,128]{1,0:T(8,128)S(1)}, u32[]{:S(2)}) copy-start(f32[360,128]{1,0:T(8,128)S(1)} %collective-permute-done.3.east.refs_5_.refs_11_.refs_6_) | copy-start | bytes 552964
  37.1 0.7 copy-start.1
  42.4 7.5 %collective-permute-start.5 = (f32[4,13,2,384]{3,2,1,0:T(2,128)}, f32[4,13,2,384]{3,2,1,0:T(2,128)S(1)}, u32[]{:S(2)}, u32[]{:S(2)}) collective-permute-start(f32[4,13,2,384]{3,2,1,0:T(2,128)} %get-tuple-element.90), channel_id=1, source_target_pairs={{0,2},{2,0},{1,3},{3,1},{4,6},{6,4},{5,7},{7,5},{8,10},{10,8},{9,1... | collective-permute-start | bytes 479240 | tf_op jit(solution)/shard_map/ppermute | solution.py:1006
  48.5 16.8 %copy-start.15 = (f32[4,13,2,384]{3,2,1,0:T(2,128)S(1)}, f32[4,13,2,384]{3,2,1,0:T(2,128)}, u32[]{:S(2)}) copy-start(f32[4,13,2,384]{3,2,1,0:T(2,128)} %get-tuple-element.97) | copy-start | bytes 479236
  48.5 5.4 %collective-permute-start.6 = (f32[64,384]{1,0:T(8,128)}, f32[64,384]{1,0:T(8,128)S(1)}, u32[]{:S(2)}, u32[]{:S(2)}) collective-permute-start(f32[64,384]{1,0:T(8,128)} %get-tuple-element.91), channel_id=1, source_target_pairs={{0,1},{2,3},{4,5},{6,7},{8,9},{10,11},{12,13},{14,15},{16,17},{18,... | collective-permute-start | bytes 294920 | tf_op jit(solution)/shard_map/ppermute | solution.py:991
  49.9 0.7 copy-start.5
  53.9 12.9 %collective-permute-start.7 = (f32[3,392,128]{2,1,0:T(8,128)}, f32[3,392,128]{2,1,0:T(8,128)S(1)}, u32[]{:S(2)}, u32[]{:S(2)}) collective-permute-start(f32[3,392,128]{2,1,0:T(8,128)} %column_rims.1), channel_id=1, source_target_pairs={{0,1},{2,3},{4,5},{6,7},{8,9},{10,11},{12,13},{14,15},{16,17},{18,... | collective-permute-start | bytes 1806344 | tf_op jit(solution)/shard_map/ppermute | solution.py:991
  56.2 55.9 %copy-start.3 = (f32[248,384]{1,0:T(8,128)}, f32[248,384]{1,0:T(8,128)S(1)}, u32[]{:S(2)}) copy-start(f32[248,384]{1,0:T(8,128)S(1)} %constant_dynamic-update-slice_fusion.refs_0_) | copy-start | bytes 1142788
  56.2 55.9 %collective-permute-start.10 = (f32[248,384]{1,0:T(8,128)S(1)}, f32[248,384]{1,0:T(8,128)S(1)}, u32[]{:S(2)}, u32[]{:S(2)}) collective-permute-start(f32[248,384]{1,0:T(8,128)S(1)} %constant_dynamic-update-slice_fusion.refs_0_), channel_id=1, source_target_pairs={{0,12},{4,0},{8,4},{12,8},{1,13},{5,1},{9,5},{13,9},{2,14},{6,2},{... | collective-permute-start | bytes 1142792 | tf_op jit(solution)/shard_map/ppermute | solution.py:988
  63.5 48.6 %collective-permute-start.8 = (f32[248,384]{1,0:T(8,128)S(1)}, f32[248,384]{1,0:T(8,128)S(1)}, u32[]{:S(2)}, u32[]{:S(2)}) collective-permute-start(f32[248,384]{1,0:T(8,128)S(1)} %constant_dynamic-update-slice_fusion.refs_0_), channel_id=1, source_target_pairs={{0,4},{4,8},{8,12},{12,0},{1,5},{5,9},{9,13},{13,1},{2,6},{6,10},{... | collective-permute-start | bytes 1142792 | tf_op jit(solution)/shard_map/ppermute | solution.py:988
  63.8 48.3 %collective-permute-start.9 = (f32[248,384]{1,0:T(8,128)S(1)}, f32[248,384]{1,0:T(8,128)S(1)}, u32[]{:S(2)}, u32[]{:S(2)}) collective-permute-start(f32[248,384]{1,0:T(8,128)S(1)} %constant_dynamic-update-slice_fusion.refs_0_), channel_id=1, source_target_pairs={{0,8},{4,12},{8,0},{12,4},{1,9},{5,13},{9,1},{13,5},{2,10},{6,14},... | collective-permute-start | bytes 1142792 | tf_op jit(solution)/shard_map/ppermute | solution.py:988
  65.2 46.8 %collective-permute-start.11 = (f32[4,13,2,384]{3,2,1,0:T(2,128)S(1)}, f32[4,13,2,384]{3,2,1,0:T(2,128)S(1)}, u32[]{:S(2)}, u32[]{:S(2)}) collective-permute-start(f32[4,13,2,384]{3,2,1,0:T(2,128)S(1)} %copy-done.15), channel_id=1, source_target_pairs={{0,8},{4,12},{8,0},{12,4},{1,9},{5,13},{9,1},{13,5},{2,10},{6,14},... | collective-permute-start | bytes 479240 | tf_op jit(solution)/shard_map/ppermute | solution.py:988
  66.8 0.8 copy-start.2
  112.1 1.4 copy-start.4
  112.1 1.4 copy-start.7
  112.1 1.4 copy-start.8
  112.2 1.4 copy-start.9
  112.2 26.0 %collective-permute-start.12 = (f32[3,328,128]{2,1,0:T(8,128)}, f32[3,328,128]{2,1,0:T(8,128)S(1)}, u32[]{:S(2)}, u32[]{:S(2)}) collective-permute-start(f32[3,328,128]{2,1,0:T(8,128)} %get-tuple-element.117), channel_id=1, source_target_pairs={{0,1},{2,3},{4,5},{6,7},{8,9},{10,11},{12,13},{14,15},{16,17},{18,... | collective-permute-start | bytes 1511432 | tf_op jit(solution)/shard_map/ppermute | solution.py:991
  123.4 14.8 %collective-permute-start.13 = (f32[3,96,128]{2,1,0:T(8,128)}, f32[3,96,128]{2,1,0:T(8,128)S(1)}, u32[]{:S(2)}, u32[]{:S(2)}) collective-permute-start(f32[3,96,128]{2,1,0:T(8,128)} %get-tuple-element.119), channel_id=1, source_target_pairs={{0,1},{2,3},{4,5},{6,7},{8,9},{10,11},{12,13},{14,15},{16,17},{18,... | collective-permute-start | bytes 442376 | tf_op jit(solution)/shard_map/ppermute | solution.py:991
  138.2 0.6 copy-start.13
  138.2 0.9 copy-start.6
